TPU v7x, 1024 devices: a whole 4x8x16 slice. The times are simulated.
1024 devices in a mesh: expert: 16 (over z), etp: 4 (over x), dp: 16 (over y, core).
Axes of the slice: x: 4, y: 8, z: 16, core: 2. Of those that a mesh axis runs over, the one named last changes fastest.
Arguments:
- tokens: bfloat16 [1024, 6144], P('expert', 'dp'), may hold values from -6 to 6
- routes: int32 [1024, 4], P('expert'), may hold values from 0 to 15, all different within a row; in each aligned block of 64 rows (0 to 63, 64 to 127, ...) at most 21 rows name the same one
- combine_weights: float32 [1024, 4], P('expert'), may hold values from 0.2 to 1
- gate_weight: bfloat16 [16, 6144, 2688], P('expert', 'dp', 'etp'), may hold values from -0.078125 to 0.078125
- up_weight: bfloat16 [16, 6144, 2688], P('expert', 'dp', 'etp'), may hold values from -0.078125 to 0.078125
- down_weight: bfloat16 [16, 2688, 6144], P('expert', 'etp', 'dp'), may hold values from -0.125 to 0.125
- out_cotangent: bfloat16 [1024, 6144], P('expert', 'dp'), may hold values from -6 to 6
Outputs:
- layer_output: bfloat16 [1024, 6144], P('expert', ('dp', 'etp'))
- tokens_grad: bfloat16 [1024, 6144], P('expert', ('dp', 'etp'))
- gate_grad: bfloat16 [16, 6144, 2688], P('expert', 'dp', 'etp')
- up_grad: bfloat16 [16, 6144, 2688], P('expert', 'dp', 'etp')
- down_grad: bfloat16 [16, 2688, 6144], P('expert', 'etp', 'dp')
Inputs may be any that keep to these rules, and one draw needn't show every extreme that they name: `routes`: A token names 4 different experts. Among the tokens of one block of 64, no expert is named by more than 21 tokens, and in every draw some block names some expert exactly 21 times; every expert is named somewhere.
All inputs are finite; a program needn't handle non-finite values.
Results may differ from a plain program's by a relative error of at most 0.038.
Values may be sent and summed in bfloat16 or wider, within the bound.
No kernel may reach another device: no remote copies, remote signals or barrier semaphores. Data moves between devices by JAX's collectives and lax.ppermute only.
A program may use at most 32 MiB of HBM per device.

v0:
```python
import jax
import jax.numpy as jnp
from jax import lax
from jax.sharding import PartitionSpec as P


def dp_rows(term_fn, share_rows):
    return lax.psum_scatter(
        term_fn(jnp.int32(0), share_rows * lax.axis_size("dp")).astype(jnp.bfloat16),
        "dp",
        scatter_dimension=0,
        tiled=True,
    ).astype(jnp.float32)


def dp_gather(share_block):
    return lax.all_gather(share_block, "dp", axis=0, tiled=True)


def contract_rows(left_side, right_side):
    return lax.dot_general(
        left_side, right_side, (((0,), (0,)), ((), ())), preferred_element_type=jnp.float32
    )


def contract_cols(left_side, right_side):
    return lax.dot_general(
        left_side, right_side, (((1,), (1,)), ((), ())), preferred_element_type=jnp.float32
    )


def gate_grads(d_hidden, gate_sum, up_sum):
    sigmoid_gate = jax.nn.sigmoid(gate_sum)
    d_gate = (d_hidden * up_sum * sigmoid_gate * (1.0 + gate_sum * (1.0 - sigmoid_gate))).astype(
        jnp.bfloat16
    )
    d_up = (d_hidden * gate_sum * sigmoid_gate).astype(jnp.bfloat16)
    return jnp.concatenate([d_gate, d_up], axis=1)


def local(tokens, routes, combine_weights, gate_weight, up_weight, down_weight, out_cotangent):
    block_len, top_count = routes.shape
    expert_count = lax.axis_size("expert")
    dp_count = lax.axis_size("dp")
    capacity = min(block_len, block_len * top_count * 4 // (3 * expert_count))
    hidden_width = gate_weight.shape[2]
    flat_ids = routes.reshape(-1)
    hit_table = (flat_ids[:, None] == jnp.arange(expert_count, dtype=jnp.int32)[None, :]).astype(
        jnp.int32
    )
    rank_in_block = jnp.sum((jnp.cumsum(hit_table, axis=0) - hit_table) * hit_table, axis=1)
    slot_index = flat_ids * capacity + rank_in_block
    placement = slot_index[:, None] == jnp.arange(expert_count * capacity, dtype=jnp.int32)[None, :]
    place_bf = placement.astype(jnp.bfloat16)
    repeated = jnp.repeat(tokens, top_count, axis=0)
    scaled = (
        combine_weights.reshape(-1)[:, None]
        * jnp.repeat(out_cotangent, top_count, axis=0).astype(jnp.float32)
    ).astype(jnp.bfloat16)
    x_send = contract_rows(place_bf, repeated).astype(jnp.bfloat16)
    g_send = contract_rows(place_bf, scaled).astype(jnp.bfloat16)
    x_slots, g_slots = (
        lax.all_to_all(x_send, "expert", split_axis=0, concat_axis=0, tiled=True),
        lax.all_to_all(g_send, "expert", split_axis=0, concat_axis=0, tiled=True),
    )
    weight_gate = gate_weight[0]
    weight_up = up_weight[0]
    weight_down = down_weight[0]
    slot_total = x_slots.shape[0]
    share_rows = slot_total // dp_count

    def gate_up_term(first_row, row_count):
        return jnp.concatenate(
            [
                jnp.dot(x_slots, weight_gate, preferred_element_type=jnp.float32),
                jnp.dot(x_slots, weight_up, preferred_element_type=jnp.float32),
            ],
            axis=1,
        )

    summed = dp_rows(gate_up_term, share_rows)
    gate_sum = summed[:, :hidden_width]
    up_sum = summed[:, hidden_width:]
    hidden_all = dp_gather((jax.nn.silu(gate_sum) * up_sum).astype(jnp.bfloat16))

    def back_term(first_row, row_count):
        return contract_cols(g_slots, weight_down)

    d_hidden = dp_rows(back_term, share_rows)
    d_both = dp_gather(gate_grads(d_hidden, gate_sum, up_sum))
    d_gate = d_both[:, :hidden_width]
    d_up = d_both[:, hidden_width:]
    y_part = jnp.dot(hidden_all, weight_down, preferred_element_type=jnp.float32)
    down_grad = contract_rows(hidden_all, g_slots).astype(jnp.bfloat16)
    gate_grad = contract_rows(x_slots, d_gate).astype(jnp.bfloat16)
    up_grad = contract_rows(x_slots, d_up).astype(jnp.bfloat16)
    dx_part = contract_cols(d_gate, weight_gate) + contract_cols(d_up, weight_up)
    y_cols, dx_cols = (
        lax.psum_scatter(
            y_part.astype(jnp.bfloat16), "etp", scatter_dimension=1, tiled=True
        ).astype(jnp.float32),
        lax.psum_scatter(
            dx_part.astype(jnp.bfloat16), "etp", scatter_dimension=1, tiled=True
        ).astype(jnp.float32),
    )
    y_back, dx_back = (
        lax.all_to_all(
            y_cols.astype(jnp.bfloat16), "expert", split_axis=0, concat_axis=0, tiled=True
        ),
        lax.all_to_all(
            dx_cols.astype(jnp.bfloat16), "expert", split_axis=0, concat_axis=0, tiled=True
        ),
    )
    gate_weighted = placement.astype(jnp.float32) * combine_weights.reshape(-1)[:, None]
    output_rows = jnp.dot(
        gate_weighted, y_back.astype(jnp.float32), precision=lax.Precision.HIGHEST
    )
    layer_output = jnp.sum(output_rows.reshape(block_len, top_count, -1), axis=1).astype(
        jnp.bfloat16
    )
    grad_rows = jnp.dot(place_bf, dx_back, preferred_element_type=jnp.float32)
    tokens_grad = jnp.sum(grad_rows.reshape(block_len, top_count, -1), axis=1).astype(jnp.bfloat16)
    return (layer_output, tokens_grad, gate_grad[None], up_grad[None], down_grad[None])


def solution(mesh):
    placed = (
        P("expert", "dp"),
        P("expert", None),
        P("expert", None),
        P("expert", "dp", "etp"),
        P("expert", "dp", "etp"),
        P("expert", "etp", "dp"),
        P("expert", "dp"),
    )
    return jax.shard_map(
        local,
        mesh=mesh,
        in_specs=placed,
        out_specs=(
            P("expert", ("dp", "etp")),
            P("expert", ("dp", "etp")),
            P("expert", "dp", "etp"),
            P("expert", "dp", "etp"),
            P("expert", "etp", "dp"),
        ),
        check_vma=False,
    )
```

profile of v0, /device:TPU:40, one launch (start us, length us, event | category | flops | bytes accessed | tf_op | source)
XLA Modules:
  0.0 307.0 jit_solution(12294439857048208328)
XLA Ops:
  7.2 0.8 copy.34
  8.0 0.1 eq.71
  8.1 0.1 eq.75
  8.2 0.6 reduce-window.6
  8.8 0.2 slice_reduce_fusion
  9.1 0.9 broadcast_in_dim.18
  9.9 0.1 reshape.101
  10.0 0.1 fusion.37
  10.1 0.4 convolution_convert_fusion.8
  10.5 0.8 all_to_all.32
  11.3 18.9 %all-to-all-start = ((bf16[16,21,384]{2,1,0:T(8,128)(2,1)}), bf16[16,21,384]{2,1,0:T(8,128)(2,1)S(1)}, u32[]{:S(2)}, u32[]{:S(2)}) async-start(bf16[16,21,384]{2,1,0:T(8,128)(2,1)} %all_to_all.32), calls=%async_computation | async-start | bytes 589824 | tf_op jit(solution)/shard_map/all_to_all | solution.py:63
  30.2 0.1 broadcast_in_dim.19
  30.2 0.1 convert_element_type.78
  30.4 0.1 copy.40
  30.5 0.1 mul.73
  30.6 0.4 convolution_convert_fusion.7
  31.0 0.8 all_to_all.38
  31.8 17.7 %all-to-all-done = bf16[16,21,384]{2,1,0:T(8,128)(2,1)S(1)} async-done(((bf16[16,21,384]{2,1,0:T(8,128)(2,1)}), bf16[16,21,384]{2,1,0:T(8,128)(2,1)S(1)}, u32[]{:S(2)}, u32[]{:S(2)}) %all-to-all-start) | async-done | bytes 258080 | tf_op jit(solution)/shard_map/all_to_all | solution.py:63
  49.4 6.3 %all-to-all-start.2 = ((bf16[16,21,384]{2,1,0:T(8,128)(2,1)}), bf16[16,21,384]{2,1,0:T(8,128)(2,1)S(1)}, u32[]{:S(2)}, u32[]{:S(2)}) async-start(bf16[16,21,384]{2,1,0:T(8,128)(2,1)} %all_to_all.38), calls=%async_computation.3 | async-start | bytes 589824 | tf_op jit(solution)/shard_map/all_to_all | solution.py:64
  55.7 0.0 all-reduce.5.cloned.1.call-start
  55.8 0.1 all_to_all.34
  55.9 0.5 convolution_convert_fusion.4
  56.3 0.5 convolution_convert_fusion.5
  56.8 1.3 pad_maximum_fusion
  58.1 0.0 all-reduce.5.cloned.1.call-update
  58.1 0.0 reduce-scatter.5.cloned.1.call-start
  58.1 16.8 %all-to-all-done.2 = bf16[16,21,384]{2,1,0:T(8,128)(2,1)S(1)} async-done(((bf16[16,21,384]{2,1,0:T(8,128)(2,1)}), bf16[16,21,384]{2,1,0:T(8,128)(2,1)S(1)}, u32[]{:S(2)}, u32[]{:S(2)}) %all-to-all-start.2) | async-done | bytes 258080 | tf_op jit(solution)/shard_map/all_to_all | solution.py:64
  74.9 0.1 all_to_all.40
  75.0 0.5 convolution_convert_fusion.3
  75.5 25.7 %fusion = bf16[24,672]{1,0:T(8,128)(2,1)S(1)} fusion(bf16[336,672]{1,0:T(8,128)(2,1)S(1)} %convolution_convert_fusion.3), kind=kCustom, calls=%all-reduce-scatter | all-reduce-scatter fusion | flops 258049 | bytes 487936
  101.2 1.9 collective-permute-start
  103.1 1.9 collective-permute-start.1
  105.1 0.1 reduce_sum.30
  105.2 0.1 copy.37
  105.3 1.4 fusion.40
  107.9 3.1 %collective-permute-done.1 = bf16[21,672]{1,0:T(8,128)(2,1)S(1)} collective-permute-done((bf16[21,672]{1,0:T(8,128)(2,1)S(1)}, bf16[21,672]{1,0:T(8,128)(2,1)S(1)}, u32[]{:S(2)}, u32[]{:S(2)}) %collective-permute-start.1) | collective-permute-done | bytes 28256
  111.0 0.3 concatenate.9
  111.4 71.4 %all-reduce.5.cloned.1.call-done = bf16[336,1344]{1,0:T(8,128)(2,1)} async-done(((bf16[336,1344]{1,0:T(8,128)(2,1)}), bf16[336,1344]{1,0:T(8,128)(2,1)}) %all-reduce.5.cloned.1.call-update) | async-done | bytes 903184
  182.8 0.9 dynamic-slice_convert_fusion
  183.7 0.1 fusion.31
  183.8 19.1 %all-gather = bf16[16,21,672]{2,1,0:T(8,128)(2,1)S(1)} all-gather(bf16[1,21,672]{2,1,0:T(8,128)(2,1)S(1)} %get-tuple-element.7), channel_id=1, replica_groups=mesh['expert'=16,'etp'=4,'dp'=16] {'dp'}, dimensions={0}, use_global_device_ids=true | all-gather | bytes 479808 | tf_op jit(solution)/shard_map/all_gather | solution.py:17
  202.9 0.2 reshape.103
  203.2 1.3 convolution_convert_fusion.6
  204.5 0.0 reduce-scatter.5.cloned.1.call-update
  204.5 0.0 reduce-scatter.7.cloned.1.call-start
  204.6 0.1 maximum_bitcast_fusion
  204.6 17.5 %all-gather.1 = bf16[16,21,1344]{2,1,0:T(8,128)(2,1)S(1)} all-gather(bf16[1,21,1344]{2,1,0:T(8,128)(2,1)S(1)} %maximum_bitcast_fusion), channel_id=1, replica_groups=mesh['expert'=16,'etp'=4,'dp'=16] {'dp'}, dimensions={0}, use_global_device_ids=true | all-gather | bytes 959616 | tf_op jit(solution)/shard_map/all_gather | solution.py:17
  222.1 0.5 reshape.105
  222.6 1.6 fusion.9
  224.3 1.3 fusion.4
  225.7 11.0 %reduce-scatter.5.cloned.1.call-done = bf16[336,96]{0,1:T(8,128)(2,1)} async-done(((bf16[336,384]{0,1:T(8,128)(2,1)}), bf16[336,96]{0,1:T(8,128)(2,1)}) %reduce-scatter.5.cloned.1.call-update) | async-done | bytes 64528 | tf_op jit(solution)/shard_map/reduce_scatter | solution.py:99
  236.7 1.0 copy.38
  237.7 0.7 all_to_all.35
  238.4 13.0 %all-to-all-start.1 = ((bf16[16,21,96]{2,1,0:T(8,128)(2,1)}), bf16[16,21,96]{2,1,0:T(8,128)(2,1)S(1)}, u32[]{:S(2)}, u32[]{:S(2)}) async-start(bf16[16,21,96]{2,1,0:T(8,128)(2,1)} %all_to_all.35), calls=%async_computation.2 | async-start | bytes 196608 | tf_op jit(solution)/shard_map/all_to_all | solution.py:107
  251.4 1.3 fusion.1
  252.7 1.3 fusion.3
  254.0 17.8 %reduce-scatter.7.cloned.1.call-done = bf16[336,96]{0,1:T(8,128)(2,1)} async-done(((bf16[336,384]{0,1:T(8,128)(2,1)}), bf16[336,96]{0,1:T(8,128)(2,1)}) %reduce-scatter.7.cloned.1.call-update) | async-done | bytes 64528 | tf_op jit(solution)/shard_map/reduce_scatter | solution.py:102
  271.8 1.0 copy.41
  272.8 0.7 all_to_all.41
  273.5 13.0 %all-to-all-start.3 = ((bf16[16,21,96]{2,1,0:T(8,128)(2,1)}), bf16[16,21,96]{2,1,0:T(8,128)(2,1)S(1)}, u32[]{:S(2)}, u32[]{:S(2)}) async-start(bf16[16,21,96]{2,1,0:T(8,128)(2,1)} %all_to_all.41), calls=%async_computation.5 | async-start | bytes 196608 | tf_op jit(solution)/shard_map/all_to_all | solution.py:110
  286.5 1.6 fusion.2
  288.1 1.0 convolution_reduce_fusion
  289.1 10.5 %all-to-all-done.3 = bf16[16,21,96]{2,1,0:T(8,128)(2,1)S(1)} async-done(((bf16[16,21,96]{2,1,0:T(8,128)(2,1)}), bf16[16,21,96]{2,1,0:T(8,128)(2,1)S(1)}, u32[]{:S(2)}, u32[]{:S(2)}) %all-to-all-start.3) | async-done | bytes 64544 | tf_op jit(solution)/shard_map/all_to_all | solution.py:110
  299.6 0.9 convolution_reduce_fusion.1
  (29 shorter events, 0.2 us)
Async XLA Ops:
  7.2 67.9 %copy-start = (bf16[1,672,384]{2,1,0:T(8,128)(2,1)S(1)}, bf16[1,672,384]{2,1,0:T(8,128)(2,1)}, u32[]{:S(2)}) copy-start(bf16[1,672,384]{2,1,0:T(8,128)(2,1)} %param.12) | copy-start | bytes 1548292
  9.1 21.1 %copy-start.6 = (bf16[64,384]{1,0:T(8,128)(2,1)S(1)}, bf16[64,384]{1,0:T(8,128)(2,1)}, u32[]{:S(2)}) copy-start(bf16[64,384]{1,0:T(8,128)(2,1)} %param.13) | copy-start | bytes 147460
  10.5 19.9 %copy-start.8 = (f32[64,4]{0,1:T(4,128)S(1)}, f32[64,4]{0,1:T(4,128)}, u32[]{:S(2)}) copy-start(f32[64,4]{0,1:T(4,128)} %param.9) | copy-start | bytes 3076
  11.3 38.2 %all-to-all-start = ((bf16[16,21,384]{2,1,0:T(8,128)(2,1)}), bf16[16,21,384]{2,1,0:T(8,128)(2,1)S(1)}, u32[]{:S(2)}, u32[]{:S(2)}) async-start(bf16[16,21,384]{2,1,0:T(8,128)(2,1)} %all_to_all.32), calls=%async_computation | async-start | bytes 589824 | tf_op jit(solution)/shard_map/all_to_all | solution.py:63
  30.6 25.3 %copy-start.2 = (bf16[1,384,672]{1,2,0:T(8,128)(2,1)S(1)}, bf16[1,384,672]{1,2,0:T(8,128)(2,1)}, u32[]{:S(2)}) copy-start(bf16[1,384,672]{1,2,0:T(8,128)(2,1)} %param.11) | copy-start | bytes 1548292
  31.8 24.6 %copy-start.1 = (bf16[1,384,672]{1,2,0:T(8,128)(2,1)S(1)}, bf16[1,384,672]{1,2,0:T(8,128)(2,1)}, u32[]{:S(2)}) copy-start(bf16[1,384,672]{1,2,0:T(8,128)(2,1)} %param.10) | copy-start | bytes 1548292
  49.4 25.5 %all-to-all-start.2 = ((bf16[16,21,384]{2,1,0:T(8,128)(2,1)}), bf16[16,21,384]{2,1,0:T(8,128)(2,1)S(1)}, u32[]{:S(2)}, u32[]{:S(2)}) async-start(bf16[16,21,384]{2,1,0:T(8,128)(2,1)} %all_to_all.38), calls=%async_computation.3 | async-start | bytes 589824 | tf_op jit(solution)/shard_map/all_to_all | solution.py:64
  55.7 127.1 %all-reduce.5.cloned.1.call-start = ((), (), s32[]{:S(2)}) async-start(), calls=%async_computation.8 | async-start | bytes 1892352
  58.1 178.6 %reduce-scatter.5.cloned.1.call-start = ((), (), s32[]{:S(2)}) async-start(), calls=%async_computation.6 | async-start | bytes 368640 | tf_op jit(solution)/shard_map/reduce_scatter | solution.py:99
  101.2 9.8 %collective-permute-start = (bf16[24,672]{1,0:T(8,128)(2,1)S(1)}, bf16[24,672]{1,0:T(8,128)(2,1)S(1)}, u32[]{:S(2)}, u32[]{:S(2)}) collective-permute-start(bf16[24,672]{1,0:T(8,128)(2,1)S(1)} %fusion), channel_id=1, source_target_pairs={{0,1},{1,2},{2,3},{3,4},{4,5},{5,6},{6,7},{7,8},{8,9},{9,10},{10,1... | collective-permute-start | bytes 96776
  103.1 7.9 %collective-permute-start.1 = (bf16[21,672]{1,0:T(8,128)(2,1)S(1)}, bf16[21,672]{1,0:T(8,128)(2,1)S(1)}, u32[]{:S(2)}, u32[]{:S(2)}) collective-permute-start(bf16[21,672]{1,0:T(8,128)(2,1)S(1)} %slice.29), channel_id=1, source_target_pairs={{0,2},{1,3},{2,4},{3,5},{4,6},{5,7},{6,8},{7,9},{8,10},{9,11},{10,... | collective-permute-start | bytes 84680
  203.2 1.4 copy-start.4
  204.5 67.3 %reduce-scatter.7.cloned.1.call-start = ((), (), s32[]{:S(2)}) async-start(), calls=%async_computation.7 | async-start | bytes 368640 | tf_op jit(solution)/shard_map/reduce_scatter | solution.py:102
  222.6 1.7 copy-start.3
  224.3 1.4 copy-start.7
  225.6 27.1 %copy-start.5 = (bf16[336,672]{1,0:T(8,128)(2,1)S(1)}, bf16[336,672]{1,0:T(8,128)(2,1)}, u32[]{:S(2)}) copy-start(bf16[336,672]{1,0:T(8,128)(2,1)} %copy-done.4) | copy-start | bytes 1354756
  238.4 35.2 %all-to-all-start.1 = ((bf16[16,21,96]{2,1,0:T(8,128)(2,1)}), bf16[16,21,96]{2,1,0:T(8,128)(2,1)S(1)}, u32[]{:S(2)}, u32[]{:S(2)}) async-start(bf16[16,21,96]{2,1,0:T(8,128)(2,1)} %all_to_all.35), calls=%async_computation.2 | async-start | bytes 196608 | tf_op jit(solution)/shard_map/all_to_all | solution.py:107
  273.5 26.1 %all-to-all-start.3 = ((bf16[16,21,96]{2,1,0:T(8,128)(2,1)}), bf16[16,21,96]{2,1,0:T(8,128)(2,1)S(1)}, u32[]{:S(2)}, u32[]{:S(2)}) async-start(bf16[16,21,96]{2,1,0:T(8,128)(2,1)} %all_to_all.41), calls=%async_computation.5 | async-start | bytes 196608 | tf_op jit(solution)/shard_map/all_to_all | solution.py:110
Sparse Core Ops, SparseCore 0:
  58.9 123.8 all-reduce.4
  204.6 32.0 reduce-scatter.4
  240.5 31.3 reduce-scatter.6
where the time goes:
time: 308 us; the launch traced here: 307 us
  waiting for transfers between devices  148 us (48%)
  blocking collectives  62.3 us (20%)
  starting transfers between devices  55.1 us (18%)
  between operations  15.4 us (5%)
  matrix products  12.4 us (4%)
  local copies, waits for them, and re-layouts  10.4 us (3%)
  other arithmetic  3.08 us (1%)
    unnamed x6, waiting for transfers between devices  74.6 us
    all_gather x2, blocking collectives, dp_gather(): return lax.all_gather(share_block, 'dp', axis=0, tiled=True)  36.6 us
    unnamed x1, blocking collectives  25.7 us
    all_to_all x1, starting transfers between devices, local(): lax.all_to_all(x_send, 'expert', split_axis=0, concat_axis=0, tiled=True)  18.9 us
    reduce_scatter x1, waiting for transfers between devices, local(): lax.psum_scatter(dx_part.astype(jnp.bfloat16), 'etp', scatter_dimension=1...  17.8 us
    all_to_all x1, waiting for transfers between devices, local(): lax.all_to_all(x_send, 'expert', split_axis=0, concat_axis=0, tiled=True)  17.7 us
    all_to_all x1, waiting for transfers between devices, local(): lax.all_to_all(g_send, 'expert', split_axis=0, concat_axis=0, tiled=True)  16.8 us
    all_to_all x1, starting transfers between devices, local(): lax.all_to_all(y_cols.astype(jnp.bfloat16), 'expert', split_axis=0, conca...  13 us
  transfers between devices with their start and end apart: 9, of which 7 were waited for; matrix products, arithmetic and copies ran while one was open for 14% of the time, Pallas kernels for 0%

commit v1 on v0

v1 whole, which is shorter than its diff:
```python
import jax
import jax.numpy as jnp
from jax import lax
from jax.sharding import PartitionSpec as P

PAD_CAP = 24
LANES = 128
f32 = jnp.float32
bf16 = jnp.bfloat16


def mm(left, right, dims):
    return lax.dot_general(left, right, (dims, ((), ())), preferred_element_type=f32)


def swap(x, axis, groups=None):
    return lax.all_to_all(
        x, axis, split_axis=0, concat_axis=0, tiled=True, axis_index_groups=groups
    )


def widen(x, width):
    return jnp.pad(x, ((0, 0), (0, width - x.shape[1])))


def local(tokens, routes, combine_weights, gate_weight, up_weight, down_weight, out_cotangent):
    block_len, top_count = routes.shape
    n_exp = lax.axis_size("expert")
    n_etp = lax.axis_size("etp")
    n_dp = lax.axis_size("dp")
    n_y = n_dp // 2
    width = tokens.shape[1]
    piece = width // n_etp
    hid = gate_weight.shape[2]
    slots = n_exp * PAD_CAP
    same_core = [[2 * y + c for y in range(n_y)] for c in range(2)]
    same_chip = [[2 * y, 2 * y + 1] for y in range(n_y)]
    col = lax.axis_index("etp") * piece

    slot = lax.broadcasted_iota(jnp.int32, (block_len, slots), 1)
    owner = slot // PAD_CAP
    rank = slot % PAD_CAP
    hit = owner == routes[:, 0:1]
    weight = jnp.where(hit, combine_weights[:, 0:1], 0.0)
    for k in range(1, top_count):
        hit_k = owner == routes[:, k : k + 1]
        weight = jnp.where(hit_k, combine_weights[:, k : k + 1], weight)
        hit = hit | hit_k
    earlier = (
        lax.broadcasted_iota(jnp.int32, (block_len, block_len), 1)
        < lax.broadcasted_iota(jnp.int32, (block_len, block_len), 0)
    ).astype(bf16)
    before = mm(earlier, hit.astype(bf16), ((1,), (0,)))
    place = hit & (before == rank.astype(f32))
    weight = jnp.where(place, weight, 0.0)
    place_bf = place.astype(bf16)

    tok = lax.dynamic_slice_in_dim(tokens, col, piece, 1)
    cot = lax.dynamic_slice_in_dim(out_cotangent, col, piece, 1)
    both = mm(place_bf, jnp.concatenate([widen(tok, LANES), widen(cot, LANES)], 1), ((0,), (0,)))
    slot_weight = jnp.sum(weight, axis=0)[:, None]
    scale = jnp.where(
        lax.broadcasted_iota(jnp.int32, (slots, 2 * LANES), 1) < LANES, 1.0, slot_weight
    )
    send = (both * scale).astype(bf16).reshape(n_exp, PAD_CAP, 2 * LANES)
    got = swap(send, "expert").reshape(1, slots, 2 * LANES)
    pieces = swap(jnp.broadcast_to(got, (n_etp, slots, 2 * LANES)), "etp")
    x = jnp.concatenate([pieces[i, :, :piece] for i in range(n_etp)], axis=1)
    g = jnp.concatenate([pieces[i, :, LANES : LANES + piece] for i in range(n_etp)], axis=1)

    w_gate, w_up, w_down = gate_weight[0], up_weight[0], down_weight[0]
    part = jnp.concatenate(
        [
            mm(x, w_gate, ((1,), (0,))).astype(bf16),
            mm(x, w_up, ((1,), (0,))).astype(bf16),
            mm(g, w_down, ((1,), (1,))).astype(bf16),
        ],
        axis=1,
    ).reshape(2, slots // 2, 3 * hid)
    chip = swap(part, "dp", same_chip).astype(f32)
    chip = (chip[0] + chip[1]).astype(bf16).reshape(n_y, PAD_CAP, 3 * hid)
    total = jnp.sum(swap(chip, "dp", same_core).astype(f32), axis=0)
    gate, up, d_hidden = total[:, :hid], total[:, hid : 2 * hid], total[:, 2 * hid :]
    sig = jax.nn.sigmoid(gate)
    act = jnp.concatenate(
        [
            (gate * sig * up).astype(bf16),
            (d_hidden * up * sig * (1.0 + gate * (1.0 - sig))).astype(bf16),
            (d_hidden * gate * sig).astype(bf16),
        ],
        axis=1,
    )
    half = lax.all_gather(act, "dp", axis=0, tiled=True, axis_index_groups=same_core)
    full = swap(
        jnp.broadcast_to(half[None], (2, slots // 2, 3 * hid)), "dp", same_chip
    ).reshape(slots, 3 * hid)
    hidden, d_gate, d_up = full[:, :hid], full[:, hid : 2 * hid], full[:, 2 * hid :]

    y = mm(hidden, w_down, ((1,), (0,))).astype(bf16)
    dx = (mm(d_gate, w_gate, ((1,), (1,))) + mm(d_up, w_up, ((1,), (1,)))).astype(bf16)
    out = jnp.stack(
        [
            jnp.concatenate(
                [
                    widen(y[:, i * piece : (i + 1) * piece], LANES),
                    widen(dx[:, i * piece : (i + 1) * piece], LANES),
                ],
                axis=1,
            )
            for i in range(n_etp)
        ]
    )
    out = jnp.sum(swap(out, "etp").astype(f32), axis=0).astype(bf16)
    back = swap(out.reshape(n_exp, PAD_CAP, 2 * LANES), "expert").reshape(slots, 2 * LANES)
    down_grad = mm(hidden, g, ((0,), (0,))).astype(bf16)
    gate_grad = mm(x, d_gate, ((0,), (0,))).astype(bf16)
    up_grad = mm(x, d_up, ((0,), (0,))).astype(bf16)
    layer_output = jnp.dot(
        weight, back[:, :piece].astype(f32), precision=lax.Precision.HIGHEST
    ).astype(bf16)
    tokens_grad = mm(place_bf, back[:, LANES : LANES + piece], ((1,), (0,))).astype(bf16)
    return layer_output, tokens_grad, gate_grad[None], up_grad[None], down_grad[None]


def solution(mesh):
    placed = (
        P("expert", "dp"),
        P("expert", None),
        P("expert", None),
        P("expert", "dp", "etp"),
        P("expert", "dp", "etp"),
        P("expert", "etp", "dp"),
        P("expert", "dp"),
    )
    return jax.shard_map(
        local,
        mesh=mesh,
        in_specs=placed,
        out_specs=(
            P("expert", ("dp", "etp")),
            P("expert", ("dp", "etp")),
            P("expert", "dp", "etp"),
            P("expert", "dp", "etp"),
            P("expert", "etp", "dp"),
        ),
        check_vma=False,
    )
```

time: 308 us -> 170 us (0.55)
  the two profiles are of different devices: /device:TPU:40 before, /device:TPU:64 now
where the time goes in v1:
time: 170 us; the launch traced here: 169 us
  blocking collectives  132 us (78%)
  matrix products  11.7 us (7%)
  waiting for transfers between devices  10.1 us (6%)
  starting transfers between devices  6.08 us (4%)
  local copies, waits for them, and re-layouts  5.96 us (4%)
  other arithmetic  2.59 us (2%)
    all_to_all x6, blocking collectives, swap(): lax.all_to_all(x, axis, split_axis=0, concat_axis=0, tiled=True, axis_ind...  106 us
    all_gather x1, blocking collectives, local(): lax.all_gather(act, 'dp', axis=0, tiled=True, axis_index_groups=same_core)  25.9 us
    dot_general x12, matrix products, mm(): lax.dot_general(left, right, (dims, ((), ())), preferred_element_type=f32)  10.8 us
    all_to_all x1, waiting for transfers between devices, swap(): lax.all_to_all(x, axis, split_axis=0, concat_axis=0, tiled=True, axis_ind...  10.1 us
    all_to_all x1, starting transfers between devices, swap(): lax.all_to_all(x, axis, split_axis=0, concat_axis=0, tiled=True, axis_ind...  6.08 us
  transfers between devices with their start and end apart: 1, of which 1 were waited for; matrix products, arithmetic and copies ran while one was open for 3% of the time, Pallas kernels for 0%

profile of v1, /device:TPU:64, one launch (start us, length us, event | category | flops | bytes accessed | tf_op | source)
XLA Modules:
  0.0 169.1 jit_solution(9786084792107937745)
XLA Ops:
  0.6 0.0 copy-start
  0.7 0.0 copy-start.24
  0.7 0.8 slice_bitcast_fusion.15
  1.6 0.8 slice_bitcast_fusion.11
  2.4 0.0 copy-start.20
  2.4 0.0 copy-start.22
  2.4 0.9 constant_dynamic-slice_fusion
  3.3 0.3 fusion.46
  3.6 0.3 fusion.5
  3.8 0.0 copy-done.24
  3.9 34.0 %all_to_all.35 = bf16[16,24,256]{2,1,0:T(8,128)(2,1)S(1)} all-to-all(bf16[16,24,256]{2,1,0:T(8,128)(2,1)S(1)} %bitcast.81), channel_id=1, replica_groups=mesh['expert'=16,'etp'=4,'dp'=16] {'expert'}, dimensions={0} | all-to-all | bytes 393216 | tf_op jit(solution)/shard_map/all_to_all | solution.py:17
  38.0 0.1 broadcast_in_dim.87
  38.0 0.0 copy-start.2
  38.0 16.0 %all_to_all.36 = bf16[4,384,256]{2,1,0:T(8,128)(2,1)S(1)} all-to-all(bf16[4,384,256]{2,1,0:T(8,128)(2,1)S(1)} %broadcast_in_dim.87), channel_id=1, replica_groups=mesh['expert'=16,'etp'=4,'dp'=16] {'etp'}, dimensions={0} | all-to-all | bytes 1572864 | tf_op jit(solution)/shard_map/all_to_all | solution.py:17
  54.0 0.1 slice_bitcast_fusion.7
  54.2 0.0 copy-start.5
  54.2 0.0 copy-start.7
  54.2 0.0 copy-start.9
  54.2 0.0 copy-done.2
  54.2 0.6 convolution_convert_fusion.4
  54.8 0.2 copy-done.1
  55.1 0.6 convolution_convert_fusion.5
  55.7 0.0 copy-done.3
  55.7 0.0 copy-done.5
  55.7 0.0 copy-done.7
  55.7 0.0 copy-done.9
  55.7 0.0 copy-done
  55.7 0.6 convolution_convert_fusion.3
  56.3 1.3 pad_maximum_fusion
  57.7 1.7 %copy.14 = bf16[384,2016]{1,0:T(8,128)(2,1)S(1)} copy(bf16[384,2016]{0,1:T(8,128)(2,1)} %pad_maximum_fusion) | data formatting | bytes 3096576 | tf_op jit(solution)/shard_map/concatenate | solution.py:72
  59.4 5.0 %all_to_all.37 = bf16[2,192,2016]{2,1,0:T(8,128)(2,1)S(1)} all-to-all(bf16[2,192,2016]{2,1,0:T(8,128)(2,1)S(1)} %bitcast.70), channel_id=1, replica_groups={{0,1},{2,3},{4,5},{6,7},{8,9},{10,11},{12,13},{14,15},{16,17},{18,19},{..., dimensions={0} | all-to-all | bytes 3096576 | tf_op jit(solution)/shard_map/all_to_all | solution.py:17
  64.4 0.4 convert_element_type.81
  64.7 0.2 fusion
  64.9 30.3 %all_to_all.38 = bf16[8,24,2016]{2,1,0:T(8,128)(2,1)S(1)} all-to-all(bf16[8,24,2016]{2,1,0:T(8,128)(2,1)S(1)} %bitcast.77), channel_id=1, replica_groups={{0,2,4,6,8,10,12,14},{1,3,5,7,9,11,13,15},{16,18,20,22,24,26,28,30},{17..., dimensions={0} | all-to-all | bytes 1548288 | tf_op jit(solution)/shard_map/all_to_all | solution.py:17
  95.2 0.1 convert_reduce_fusion
  95.4 0.1 multiply_convert_fusion
  95.5 0.1 concatenate.31
  95.6 25.9 %all_gather.3 = bf16[192,2016]{1,0:T(8,128)(2,1)S(1)} all-gather(bf16[24,2016]{1,0:T(8,128)(2,1)S(1)} %concatenate.31), channel_id=1, replica_groups={{0,2,4,6,8,10,12,14},{1,3,5,7,9,11,13,15},{16,18,20,22,24,26,28,30},{17..., dimensions={0}, use_global_device_ids=true | all-gather | bytes 870912 | tf_op jit(solution)/shard_map/all_gather | solution.py:93
  121.5 0.2 broadcast_in_dim.88
  121.7 5.0 %all_to_all.39 = bf16[2,192,2016]{2,1,0:T(8,128)(2,1)S(1)} all-to-all(bf16[2,192,2016]{2,1,0:T(8,128)(2,1)S(1)} %broadcast_in_dim.88), channel_id=1, replica_groups={{0,1},{2,3},{4,5},{6,7},{8,9},{10,11},{12,13},{14,15},{16,17},{18,19},{..., dimensions={0} | all-to-all | bytes 3096576 | tf_op jit(solution)/shard_map/all_to_all | solution.py:17
  126.7 0.5 convolution_convert_fusion.6
  127.2 0.7 fusion.10
  127.9 0.0 copy-start.11
  128.0 0.7 fusion.4
  128.7 0.1 slice_select_fusion.1
  128.9 0.1 pad_maximum_fusion.1
  129.0 15.3 %all_to_all.40 = bf16[4,384,256]{1,2,0:T(8,128)(2,1)S(1)} all-to-all(bf16[4,384,256]{1,2,0:T(8,128)(2,1)S(1)} %pad_maximum_fusion.1), channel_id=1, replica_groups=mesh['expert'=16,'etp'=4,'dp'=16] {'etp'}, dimensions={0} | all-to-all | bytes 1572864 | tf_op jit(solution)/shard_map/all_to_all | solution.py:17
  144.3 0.2 reduce_sum.32
  144.5 0.0 copy-start.6
  144.5 0.0 copy-start.8
  144.5 0.0 copy-start.10
  144.5 0.8 copy.15
  145.3 6.1 %all-to-all-start.6 = ((bf16[16,24,256]{2,1,0:T(8,128)(2,1)}), bf16[16,24,256]{2,1,0:T(8,128)(2,1)S(1)}, u32[]{:S(2)}, u32[]{:S(2)}) async-start(bf16[16,24,256]{2,1,0:T(8,128)(2,1)} %bitcast.28), calls=%async_computation.6 | async-start | bytes 393216 | tf_op jit(solution)/shard_map/all_to_all | solution.py:17
  151.4 2.8 %fusion.1 = bf16[1,384,672]{1,2,0:T(8,128)(2,1)} fusion(bf16[384,2016]{1,0:T(8,128)(2,1)S(1)} %bitcast.74, bf16[384,96]{1,0:T(8,128)(2,1)} %copy-done.5, bf16[384,96]{1,0:T(8,128)(2,1)} %copy-done.7, bf16[384,96]{1,0:T(8,128)(2,1)} %copy-done.9, bf16[384,96]{1,0:T(8,128)(2,1)} %copy-done.3), kind=kOutput, calls=%fused_computation.11 | convolution fusion | flops 199618560 | bytes 1400832 | tf_op jit(solution)/shard_map/dot_general | solution.py:13
  154.1 0.0 copy-done.4
  154.1 0.0 copy-done.8
  154.2 1.7 %fusion.2 = bf16[1,384,672]{1,2,0:T(8,128)(2,1)} fusion(bf16[384,2016]{1,0:T(8,128)(2,1)S(1)} %bitcast.75, bf16[384,96]{1,0:T(8,128)(2,1)S(1)} %copy-done.6, bf16[384,96]{1,0:T(8,128)(2,1)S(1)} %copy-done.8, bf16[384,96]{1,0:T(8,128)(2,1)S(1)} %copy-done.10, bf16[384,96]{1,0:T(8,128)(2,1)S(1)} %copy-done.4), kind=kOutput, calls=%fused_computation.12 | convolution fusion | flops 199618560 | bytes 1499136 | tf_op jit(solution)/shard_map/dot_general | solution.py:13
  155.9 0.0 copy-start.21
  155.9 0.0 copy-start.23
  155.9 1.4 fusion.3
  157.3 10.1 %all-to-all-done.6 = bf16[16,24,256]{2,1,0:T(8,128)(2,1)S(1)} async-done(((bf16[16,24,256]{2,1,0:T(8,128)(2,1)}), bf16[16,24,256]{2,1,0:T(8,128)(2,1)S(1)}, u32[]{:S(2)}, u32[]{:S(2)}) %all-to-all-start.6) | async-done | bytes 196640 | tf_op jit(solution)/shard_map/all_to_all | solution.py:17
  167.4 0.0 copy-done.15
  167.4 0.9 convolution_convert_fusion.8
  168.3 0.8 convolution_convert_fusion.7
  (37 shorter events, 0.2 us)
Async XLA Ops:
  0.6 55.1 %copy-start = (bf16[1,672,384]{2,1,0:T(8,128)(2,1)S(1)}, bf16[1,672,384]{2,1,0:T(8,128)(2,1)}, u32[]{:S(2)}) copy-start(bf16[1,672,384]{2,1,0:T(8,128)(2,1)} %param.12) | copy-start | bytes 1548292
  0.7 3.2 %copy-start.24 = (pred[384]{0:T(512)(128)(4,1)}, pred[384]{0:T(512)(128)(4,1)S(1)}, u32[]{:S(2)}) copy-start(pred[384]{0:T(512)(128)(4,1)S(1)} %get-tuple-element.38) | copy-start | bytes 1156
  1.6 2.3 %copy-start.12 = (s32[64]{0:T(128)}, s32[64]{0:T(128)S(1)}, u32[]{:S(2)}) copy-start(s32[64]{0:T(128)S(1)} %get-tuple-element.28) | copy-start | bytes 772
  1.6 2.3 %copy-start.14 = (s32[64]{0:T(128)}, s32[64]{0:T(128)S(1)}, u32[]{:S(2)}) copy-start(s32[64]{0:T(128)S(1)} %get-tuple-element.29) | copy-start | bytes 772
  2.4 1.5 copy-start.16
  2.4 1.5 copy-start.18
  2.4 1.5 copy-start.20
  2.4 1.5 copy-start.22
  38.0 16.2 %copy-start.2 = (bf16[1,384,672]{1,2,0:T(8,128)(2,1)S(1)}, bf16[1,384,672]{1,2,0:T(8,128)(2,1)}, u32[]{:S(2)}) copy-start(bf16[1,384,672]{1,2,0:T(8,128)(2,1)} %param.11) | copy-start | bytes 1548292
  54.0 1.0 copy-start.1
  54.2 1.5 copy-start.3
  54.2 1.5 copy-start.5
  54.2 1.5 copy-start.7
  54.2 1.5 copy-start.9
  127.9 0.7 copy-start.11
  144.4 9.7 %copy-start.4 = (bf16[384,96]{1,0:T(8,128)(2,1)S(1)}, bf16[384,96]{1,0:T(8,128)(2,1)}, u32[]{:S(2)}) copy-start(bf16[384,96]{1,0:T(8,128)(2,1)} %copy-done.3) | copy-start | bytes 221188
  144.5 9.7 %copy-start.6 = (bf16[384,96]{1,0:T(8,128)(2,1)S(1)}, bf16[384,96]{1,0:T(8,128)(2,1)}, u32[]{:S(2)}) copy-start(bf16[384,96]{1,0:T(8,128)(2,1)} %copy-done.5) | copy-start | bytes 221188
  144.5 9.7 %copy-start.8 = (bf16[384,96]{1,0:T(8,128)(2,1)S(1)}, bf16[384,96]{1,0:T(8,128)(2,1)}, u32[]{:S(2)}) copy-start(bf16[384,96]{1,0:T(8,128)(2,1)} %copy-done.7) | copy-start | bytes 221188
  144.5 9.7 %copy-start.10 = (bf16[384,96]{1,0:T(8,128)(2,1)S(1)}, bf16[384,96]{1,0:T(8,128)(2,1)}, u32[]{:S(2)}) copy-start(bf16[384,96]{1,0:T(8,128)(2,1)} %copy-done.9) | copy-start | bytes 221188
  145.3 22.1 %all-to-all-start.6 = ((bf16[16,24,256]{2,1,0:T(8,128)(2,1)}), bf16[16,24,256]{2,1,0:T(8,128)(2,1)S(1)}, u32[]{:S(2)}, u32[]{:S(2)}) async-start(bf16[16,24,256]{2,1,0:T(8,128)(2,1)} %bitcast.28), calls=%async_computation.6 | async-start | bytes 393216 | tf_op jit(solution)/shard_map/all_to_all | solution.py:17
  155.9 11.5 %copy-start.13 = (s32[64]{0:T(128)S(1)}, s32[64]{0:T(128)}, u32[]{:S(2)}) copy-start(s32[64]{0:T(128)} %copy-done.12) | copy-start | bytes 772
  155.9 11.5 %copy-start.15 = (s32[64]{0:T(128)S(1)}, s32[64]{0:T(128)}, u32[]{:S(2)}) copy-start(s32[64]{0:T(128)} %copy-done.14) | copy-start | bytes 772
  155.9 11.5 %copy-start.17 = (f32[64]{0:T(128)S(1)}, f32[64]{0:T(128)}, u32[]{:S(2)}) copy-start(f32[64]{0:T(128)} %copy-done.16) | copy-start | bytes 772
  155.9 11.5 %copy-start.19 = (f32[64]{0:T(128)S(1)}, f32[64]{0:T(128)}, u32[]{:S(2)}) copy-start(f32[64]{0:T(128)} %copy-done.18) | copy-start | bytes 772
  155.9 11.5 %copy-start.21 = (f32[64]{0:T(128)S(1)}, f32[64]{0:T(128)}, u32[]{:S(2)}) copy-start(f32[64]{0:T(128)} %copy-done.20) | copy-start | bytes 772
  155.9 11.5 %copy-start.23 = (f32[64]{0:T(128)S(1)}, f32[64]{0:T(128)}, u32[]{:S(2)}) copy-start(f32[64]{0:T(128)} %copy-done.22) | copy-start | bytes 772
  155.9 11.5 %copy-start.25 = (pred[384]{0:T(512)(128)(4,1)S(1)}, pred[384]{0:T(512)(128)(4,1)}, u32[]{:S(2)}) copy-start(pred[384]{0:T(512)(128)(4,1)} %copy-done.24) | copy-start | bytes 1156

commit v2 on v1

v2 whole, which is shorter than its diff:
```python
import functools

import jax
import jax.numpy as jnp
from jax import lax
from jax.experimental import pallas as pl
from jax.experimental.pallas import tpu as pltpu
from jax.sharding import PartitionSpec as P

PAD_CAP = 24
LANES = 128
f32 = jnp.float32
bf16 = jnp.bfloat16


def mm(left, right, dims):
    return lax.dot_general(left, right, (dims, ((), ())), preferred_element_type=f32)


def swap(x, axis, groups=None):
    return lax.all_to_all(
        x, axis, split_axis=0, concat_axis=0, tiled=True, axis_index_groups=groups
    )


def call(kernel, out_shapes, flops, n_scalar, *args, far=False, scratch=(), room=12):
    smem = pl.BlockSpec(memory_space=pltpu.SMEM)
    vmem = pl.BlockSpec(memory_space=pltpu.VMEM)
    held = pl.BlockSpec(memory_space=pltpu.HBM) if far else vmem
    moved = sum(a.size * a.dtype.itemsize for a in args) + sum(
        o.size * o.dtype.itemsize for o in out_shapes
    )
    return pl.pallas_call(
        kernel,
        out_shape=out_shapes,
        in_specs=[smem] * n_scalar + [held] * (len(args) - n_scalar),
        out_specs=[vmem] * len(out_shapes),
        scratch_shapes=list(scratch),
        compiler_params=pltpu.CompilerParams(vmem_limit_bytes=room * 1024 * 1024),
        cost_estimate=pl.CostEstimate(flops=flops, bytes_accessed=moved, transcendentals=0),
    )(*args)


def dispatch_kernel(
    piece, col_ref, tok_hbm, cot_hbm, route_hbm, cw_hbm, send_ref, place_ref, weight_ref,
    tok_ref, cot_ref, route_ref, cw_ref, sems,
):
    pairs = ((route_hbm, route_ref), (cw_hbm, cw_ref), (tok_hbm, tok_ref), (cot_hbm, cot_ref))
    copies = [pltpu.make_async_copy(a, b, sems.at[i]) for i, (a, b) in enumerate(pairs)]
    for copy in copies:
        copy.start()
    copies[0].wait()
    copies[1].wait()
    width = tok_ref.shape[1]
    top_count, block_len = route_ref.shape
    slots = send_ref.shape[0]
    slot = lax.broadcasted_iota(jnp.int32, (slots, block_len), 0)
    owner = lax.shift_right_logical(slot * 2731, 16)
    rank = slot - owner * PAD_CAP
    hit = jnp.zeros((slots, block_len), f32)
    weight = jnp.zeros((slots, block_len), f32)
    for k in range(top_count):
        hit_k = owner == route_ref[k : k + 1, :]
        hit = jnp.where(hit_k, 1.0, hit)
        weight = jnp.where(hit_k, cw_ref[k : k + 1, :], weight)
    earlier = (
        lax.broadcasted_iota(jnp.int32, (block_len, block_len), 0)
        < lax.broadcasted_iota(jnp.int32, (block_len, block_len), 1)
    )
    earlier = jnp.where(earlier, 1.0, 0.0).astype(bf16)
    before = mm(hit.astype(bf16), earlier, ((1,), (0,)))
    place = jnp.where(before == rank.astype(f32), hit, 0.0)
    weight = weight * place
    place_bf = place.astype(bf16)
    place_ref[...] = place_bf
    weight_ref[...] = weight
    lane = lax.broadcasted_iota(jnp.int32, (width, LANES), 1)
    row = lax.broadcasted_iota(jnp.int32, (width, LANES), 0)
    pick = jnp.where((row == lane + col_ref[0]) & (lane < piece), 1.0, 0.0).astype(bf16)
    copies[2].wait()
    copies[3].wait()
    tok = mm(tok_ref[...], pick, ((1,), (0,))).astype(bf16)
    cot = mm(cot_ref[...], pick, ((1,), (0,))).astype(bf16)
    send_ref[:, :LANES] = mm(place_bf, tok, ((1,), (0,))).astype(bf16)
    slot_weight = jnp.sum(weight, axis=1, keepdims=True)
    send_ref[:, LANES:] = (mm(place_bf, cot, ((1,), (0,))) * slot_weight).astype(bf16)


def front_kernel(
    piece, half_ref, piece_ref, gate_ref, up_ref, down_ref, part_ref, x_ref, g_ref
):
    rows = part_ref.shape[0]
    hid = gate_ref.shape[0]
    at = pl.ds(pl.multiple_of(half_ref[0] * rows, 16), rows)
    n_etp = piece_ref.shape[0]
    x = jnp.concatenate([piece_ref[i, at, 0:piece] for i in range(n_etp)], axis=1)
    g = jnp.concatenate(
        [piece_ref[i, at, LANES : LANES + piece] for i in range(n_etp)], axis=1
    )
    x_ref[...] = x
    g_ref[...] = g
    ends = (0, hid, 2 * hid, 3 * hid)
    for lo in range(0, 3 * hid, 256):
        hi = min(lo + 256, 3 * hid)
        total = None
        for left, first in ((x, 0), (g, 2)):
            rights, filled = [], False
            for j, ref in enumerate((gate_ref, up_ref, down_ref)):
                a, b = max(lo, ends[j]), min(hi, ends[j + 1])
                if a >= b:
                    continue
                if (j == 2) == (first == 2):
                    rights.append(ref[a - ends[j] : b - ends[j], :])
                    filled = True
                else:
                    rights.append(jnp.zeros((b - a, ref.shape[1]), bf16))
            if not filled:
                continue
            right = rights[0] if len(rights) == 1 else jnp.concatenate(rights, axis=0)
            term = mm(left, right, ((1,), (1,)))
            total = term if total is None else total + term
        part_ref[:, lo:hi] = total.astype(bf16)


def combine_kernel(piece, weight_ref, place_ref, back_ref, out_ref, grad_ref):
    back = back_ref[...]
    rest = weight_ref[...]
    total = None
    for _ in range(3):
        high = rest.astype(bf16)
        rest = rest - high.astype(f32)
        term = mm(high, back, ((0,), (0,)))
        total = term if total is None else total + term
    out_ref[...] = total[:, :piece].astype(bf16)
    grad_ref[...] = mm(place_ref[...], back, ((0,), (0,)))[:, piece : 2 * piece].astype(bf16)


def local(tokens, routes, combine_weights, gate_weight, up_weight, down_weight, out_cotangent):
    block_len, top_count = routes.shape
    n_exp = lax.axis_size("expert")
    n_etp = lax.axis_size("etp")
    n_dp = lax.axis_size("dp")
    n_y = n_dp // 2
    width = tokens.shape[1]
    piece = width // n_etp
    hid = gate_weight.shape[2]
    slots = n_exp * PAD_CAP
    same_core = [[2 * y + c for y in range(n_y)] for c in range(2)]
    same_chip = [[2 * y, 2 * y + 1] for y in range(n_y)]
    core = lax.bitwise_and(lax.axis_index("dp"), 1)
    col = lax.axis_index("etp") * piece

    send, place, weight = call(
        functools.partial(dispatch_kernel, piece),
        [
            jax.ShapeDtypeStruct((slots, 2 * LANES), bf16),
            jax.ShapeDtypeStruct((slots, block_len), bf16),
            jax.ShapeDtypeStruct((slots, block_len), f32),
        ],
        50_000_000,
        1,
        col[None],
        tokens,
        out_cotangent,
        routes.T,
        combine_weights.T,
        far=True,
        room=60,
        scratch=[
            pltpu.VMEM(tokens.shape, bf16),
            pltpu.VMEM(out_cotangent.shape, bf16),
            pltpu.VMEM((top_count, block_len), jnp.int32),
            pltpu.VMEM((top_count, block_len), f32),
            pltpu.SemaphoreType.DMA((4,)),
        ],
    )
    got = swap(send.reshape(n_exp, PAD_CAP, 2 * LANES), "expert").reshape(1, slots, 2 * LANES)
    pieces = swap(jnp.broadcast_to(got, (n_etp, slots, 2 * LANES)), "etp")

    w_gate, w_up, w_down = gate_weight[0].T, up_weight[0].T, down_weight[0]

    def front(which):
        return call(
            functools.partial(front_kernel, piece),
            [
                jax.ShapeDtypeStruct((slots // 2, 3 * hid), bf16),
                jax.ShapeDtypeStruct((slots // 2, width), bf16),
                jax.ShapeDtypeStruct((slots // 2, width), bf16),
            ],
            3 * slots * width * hid,
            1,
            which[None],
            pieces,
            w_gate,
            w_up,
            w_down,
        )

    theirs, x_theirs, g_theirs = front(1 - core)
    theirs = lax.ppermute(theirs, "dp", [(i, i ^ 1) for i in range(n_dp)])
    mine, x_mine, g_mine = front(core)
    chip = (mine.astype(f32) + theirs.astype(f32)).astype(bf16).reshape(n_y, PAD_CAP, 3 * hid)
    total = jnp.sum(swap(chip, "dp", same_core).astype(f32), axis=0)
    gate, up, d_hidden = total[:, :hid], total[:, hid : 2 * hid], total[:, 2 * hid :]
    sig = jax.nn.sigmoid(gate)
    act = jnp.concatenate(
        [
            (gate * sig * up).astype(bf16),
            (d_hidden * up * sig * (1.0 + gate * (1.0 - sig))).astype(bf16),
            (d_hidden * gate * sig).astype(bf16),
        ],
        axis=1,
    )
    half = lax.all_gather(act, "dp", axis=0, tiled=True, axis_index_groups=same_core)
    full = swap(
        jnp.broadcast_to(half[None], (2, slots // 2, 3 * hid)), "dp", same_chip
    ).reshape(slots, 3 * hid)
    hidden, d_gate, d_up = full[:, :hid], full[:, hid : 2 * hid], full[:, 2 * hid :]

    y = mm(hidden, w_down, ((1,), (0,))).astype(bf16)
    dx = (mm(d_gate, w_gate, ((1,), (0,))) + mm(d_up, w_up, ((1,), (0,)))).astype(bf16)
    out = jnp.concatenate(
        [y.T.reshape(n_etp, piece, slots), dx.T.reshape(n_etp, piece, slots)], axis=1
    )
    out = jnp.sum(swap(out, "etp").astype(f32), axis=0).astype(bf16).T
    back = swap(out.reshape(n_exp, PAD_CAP, 2 * piece), "expert").reshape(slots, 2 * piece)

    def in_order(own, other):
        first = core == 0
        return jnp.concatenate(
            [jnp.where(first, own, other), jnp.where(first, other, own)], axis=0
        )

    x = in_order(x_mine, x_theirs)
    g = in_order(g_mine, g_theirs)
    down_grad = mm(hidden, g, ((0,), (0,))).astype(bf16)
    gate_grad = mm(x, d_gate, ((0,), (0,))).astype(bf16)
    up_grad = mm(x, d_up, ((0,), (0,))).astype(bf16)
    layer_output, tokens_grad = call(
        functools.partial(combine_kernel, piece),
        [
            jax.ShapeDtypeStruct((block_len, piece), bf16),
            jax.ShapeDtypeStruct((block_len, piece), bf16),
        ],
        40_000_000,
        0,
        weight,
        place,
        back,
    )
    return layer_output, tokens_grad, gate_grad[None], up_grad[None], down_grad[None]


def solution(mesh):
    placed = (
        P("expert", "dp"),
        P("expert", None),
        P("expert", None),
        P("expert", "dp", "etp"),
        P("expert", "dp", "etp"),
        P("expert", "etp", "dp"),
        P("expert", "dp"),
    )
    return jax.shard_map(
        local,
        mesh=mesh,
        in_specs=placed,
        out_specs=(
            P("expert", ("dp", "etp")),
            P("expert", ("dp", "etp")),
            P("expert", "dp", "etp"),
            P("expert", "dp", "etp"),
            P("expert", "etp", "dp"),
        ),
        check_vma=False,
    )
```

time: 170 us -> 163 us (0.959)
  blocking collectives: 132 us -> 95.5 us
  waiting for transfers between devices: 10.1 us -> 35.3 us
  starting transfers between devices: 6.08 us -> 15.7 us
  matrix products: 11.7 us -> 6.43 us
  Pallas kernels: 0 us -> 4.68 us
  local copies, waits for them, and re-layouts: 5.96 us -> 2.1 us
    all_to_all x6 -> x3, blocking collectives: 106 us -> 69.6 us  [swap(): lax.all_to_all(x, axis, split_axis=0, concat_axis=0, tiled=True, axis_ind...]
    all_to_all x1 -> x3, waiting for transfers between devices: 10.1 us -> 33.8 us  [swap(): lax.all_to_all(x, axis, split_axis=0, concat_axis=0, tiled=True, axis_ind...]
    all_to_all x1 -> x3, starting transfers between devices: 6.08 us -> 13.8 us  [swap(): lax.all_to_all(x, axis, split_axis=0, concat_axis=0, tiled=True, axis_ind...]
    pallas_call x0 -> x4, Pallas kernels: none -> 4.68 us  [call(): pl.pallas_call(kernel, out_shape=out_shapes, in_specs=[smem] * n_scalar +...]
    dot_general x12 -> x6, matrix products: 10.8 us -> 6.43 us  [mm(): lax.dot_general(left, right, (dims, ((), ())), preferred_element_type=f32)]
    ppermute x0 -> x1, starting transfers between devices: none -> 1.92 us  [local(): theirs = lax.ppermute(theirs, 'dp', [(i, i ^ 1) for i in range(n_dp)])]
    concatenate x1 -> x0, local copies, waits for them, and re-layouts: 1.71 us -> none  [local(): jnp.concatenate([mm(x, w_gate, ((1,), (0,))).astype(bf16), mm(x, w_up, ((...]
  transfers between devices with their start and end apart: 1 -> 4, of which waited for: 1 -> 4; matrix products, arithmetic and copies ran while one was open for 3% -> 3% of each run, Pallas kernels for 0% -> 0%
where the time goes in v2:
time: 163 us; the launch traced here: 162 us
  blocking collectives  95.5 us (59%)
  waiting for transfers between devices  35.3 us (22%)
  starting transfers between devices  15.7 us (10%)
  matrix products  6.43 us (4%)
  Pallas kernels  4.68 us (3%)
  local copies, waits for them, and re-layouts  2.1 us (1%)
    all_to_all x3, blocking collectives, swap(): lax.all_to_all(x, axis, split_axis=0, concat_axis=0, tiled=True, axis_ind...  69.6 us
    all_to_all x3, waiting for transfers between devices, swap(): lax.all_to_all(x, axis, split_axis=0, concat_axis=0, tiled=True, axis_ind...  33.8 us
    all_gather x1, blocking collectives, local(): lax.all_gather(act, 'dp', axis=0, tiled=True, axis_index_groups=same_core)  25.9 us
    all_to_all x3, starting transfers between devices, swap(): lax.all_to_all(x, axis, split_axis=0, concat_axis=0, tiled=True, axis_ind...  13.8 us
    dot_general x6, matrix products, mm(): lax.dot_general(left, right, (dims, ((), ())), preferred_element_type=f32)  6.43 us
    pallas_call x4, Pallas kernels, call(): pl.pallas_call(kernel, out_shape=out_shapes, in_specs=[smem] * n_scalar +...  4.68 us
  transfers between devices with their start and end apart: 4, of which 4 were waited for; matrix products, arithmetic and copies ran while one was open for 3% of the time, Pallas kernels for 0%

profile of v2, /device:TPU:64, one launch (start us, length us, event | category | flops | bytes accessed | tf_op | source)
XLA Modules:
  0.0 162.1 jit_solution(14393497299658878631)
XLA Ops:
  0.6 0.0 copy-start
  0.6 0.0 copy-start.1
  0.7 0.0 copy-start.2
  0.7 2.2 %shard_map.110 = (bf16[384,256]{1,0:T(8,128)(2,1)}, bf16[384,64]{1,0:T(8,128)(2,1)}, f32[384,64]{1,0:T(8,128)}) custom-call(s32[1]{0:T(128)} %bitcast.col_ref, bf16[64,384]{1,0:T(8,128)(2,1)} %tok_hbm.1, bf16[64,384]{1,0:T(8,128)(2,1)} %cot_hbm.1, s32[4,64]{1,0:T(4,128)} %bitcast.56, f32[4,64]{1,0:T(4,128)} %bitcast.57), custom_call_target="tpu_custom_call" | custom-call | flops 50000000 | bytes 444420 | tf_op jit(solution)/shard_map/pallas_call | solution.py:33
  2.8 34.2 %all_to_all.30 = bf16[16,24,256]{2,1,0:T(8,128)(2,1)S(1)} all-to-all(bf16[16,24,256]{2,1,0:T(8,128)(2,1)} %bitcast.55), channel_id=1, replica_groups=mesh['expert'=16,'etp'=4,'dp'=16] {'expert'}, dimensions={0} | all-to-all | bytes 393216 | tf_op jit(solution)/shard_map/all_to_all | solution.py:21
  37.1 1.0 broadcast_in_dim.34
  38.1 4.3 %all-to-all-start.1 = ((bf16[4,384,256]{2,1,0:T(8,128)(2,1)}), bf16[4,384,256]{2,1,0:T(8,128)(2,1)S(1)}, u32[]{:S(2)}, u32[]{:S(2)}) async-start(bf16[4,384,256]{2,1,0:T(8,128)(2,1)} %broadcast_in_dim.34), calls=%async_computation.1 | async-start | bytes 1572864 | tf_op jit(solution)/shard_map/all_to_all | solution.py:21
  42.3 11.8 %all-to-all-done.1.piece_ref = bf16[4,384,256]{2,1,0:T(8,128)(2,1)S(1)} async-done(((bf16[4,384,256]{2,1,0:T(8,128)(2,1)}), bf16[4,384,256]{2,1,0:T(8,128)(2,1)S(1)}, u32[]{:S(2)}, u32[]{:S(2)}) %all-to-all-start.1) | async-done | bytes 786464 | tf_op jit(solution)/shard_map/all_to_all | solution.py:21
  54.1 0.0 copy-done
  54.1 0.0 copy-done.1
  54.1 0.0 copy-done.2
  54.1 0.8 shard_map.112
  54.9 1.9 %collective-permute-start = (bf16[192,2016]{1,0:T(8,128)(2,1)S(1)}, bf16[192,2016]{1,0:T(8,128)(2,1)S(1)}, u32[]{:S(2)}, u32[]{:S(2)}) collective-permute-start(bf16[192,2016]{1,0:T(8,128)(2,1)S(1)} %get-tuple-element.20), channel_id=1, source_target_pairs={{0,1},{1,0},{2,3},{3,2},{4,5},{5,4},{6,7},{7,6},{8,9},{9,8},{10,11... | collective-permute-start | bytes 2322440 | tf_op jit(solution)/shard_map/ppermute | solution.py:200
  56.9 0.8 shard_map.111
  57.7 1.5 collective-permute-done
  59.1 0.3 add_convert_fusion
  59.4 30.3 %all_to_all.31 = bf16[8,24,2016]{2,1,0:T(8,128)(2,1)S(1)} all-to-all(bf16[8,24,2016]{2,1,0:T(8,128)(2,1)S(1)} %bitcast.50), channel_id=1, replica_groups={{0,2,4,6,8,10,12,14},{1,3,5,7,9,11,13,15},{16,18,20,22,24,26,28,30},{17..., dimensions={0} | all-to-all | bytes 1548288 | tf_op jit(solution)/shard_map/all_to_all | solution.py:21
  89.7 0.1 convert_reduce_fusion
  89.8 0.1 multiply_convert_fusion
  89.9 0.1 concatenate.12
  90.0 25.9 %all_gather.3 = bf16[192,2016]{1,0:T(8,128)(2,1)S(1)} all-gather(bf16[24,2016]{1,0:T(8,128)(2,1)S(1)} %concatenate.12), channel_id=1, replica_groups={{0,2,4,6,8,10,12,14},{1,3,5,7,9,11,13,15},{16,18,20,22,24,26,28,30},{17..., dimensions={0}, use_global_device_ids=true | all-gather | bytes 870912 | tf_op jit(solution)/shard_map/all_gather | solution.py:214
  116.0 0.2 broadcast_in_dim.36
  116.2 5.0 %all_to_all.32 = bf16[2,192,2016]{2,1,0:T(8,128)(2,1)S(1)} all-to-all(bf16[2,192,2016]{2,1,0:T(8,128)(2,1)S(1)} %broadcast_in_dim.36), channel_id=1, replica_groups={{0,1},{2,3},{4,5},{6,7},{8,9},{10,11},{12,13},{14,15},{16,17},{18,19},{..., dimensions={0} | all-to-all | bytes 3096576 | tf_op jit(solution)/shard_map/all_to_all | solution.py:21
  121.2 0.0 copy-start.5
  121.2 0.6 fusion.7
  121.8 0.5 convolution_convert_fusion.3
  122.4 0.0 copy-done.5
  122.4 0.7 fusion.3
  123.0 0.9 pad_maximum_fusion
  123.9 3.5 %all-to-all-start.4 = ((bf16[4,192,384]{2,1,0:T(8,128)(2,1)}), bf16[4,192,384]{2,1,0:T(8,128)(2,1)S(1)}, u32[]{:S(2)}, u32[]{:S(2)}) async-start(bf16[4,192,384]{2,1,0:T(8,128)(2,1)} %pad_maximum_fusion), calls=%async_computation.4 | async-start | bytes 1179648 | tf_op jit(solution)/shard_map/all_to_all | solution.py:21
  127.4 0.0 copy-start.6
  127.4 10.7 %all-to-all-done.4 = bf16[4,192,384]{2,1,0:T(8,128)(2,1)S(1)} async-done(((bf16[4,192,384]{2,1,0:T(8,128)(2,1)}), bf16[4,192,384]{2,1,0:T(8,128)(2,1)S(1)}, u32[]{:S(2)}, u32[]{:S(2)}) %all-to-all-start.4) | async-done | bytes 589856 | tf_op jit(solution)/shard_map/all_to_all | solution.py:21
  138.1 0.1 reduce_sum.22
  138.2 0.8 copy.13
  139.1 6.1 %all-to-all-start.5 = ((bf16[16,24,192]{2,1,0:T(8,128)(2,1)}), bf16[16,24,192]{2,1,0:T(8,128)(2,1)S(1)}, u32[]{:S(2)}, u32[]{:S(2)}) async-start(bf16[16,24,192]{2,1,0:T(8,128)(2,1)} %bitcast.21), calls=%async_computation.5 | async-start | bytes 393216 | tf_op jit(solution)/shard_map/all_to_all | solution.py:21
  145.1 0.1 broadcast_select_fusion.1
  145.2 0.0 copy-done.6
  145.2 1.6 %fusion = bf16[1,384,672]{1,2,0:T(8,128)(2,1)} fusion(bf16[384,2016]{1,0:T(8,128)(2,1)S(1)} %bitcast.47, bf16[192,384]{1,0:T(8,128)(2,1)S(1)} %get-tuple-element.34, bf16[192,384]{1,0:T(8,128)(2,1)S(1)} %get-tuple-element.35), kind=kOutput, calls=%fused_computation.6 | convolution fusion | flops 199028736 | bytes 1400832 | tf_op jit(solution)/shard_map/dot_general | solution.py:17
  146.8 0.0 copy-start.3
  146.8 0.0 copy-start.4
  146.8 1.6 %fusion.1 = bf16[1,384,672]{1,2,0:T(8,128)(2,1)} fusion(bf16[384,2016]{1,0:T(8,128)(2,1)S(1)} %bitcast.48, bf16[192,384]{1,0:T(8,128)(2,1)S(1)} %get-tuple-element.34, bf16[192,384]{1,0:T(8,128)(2,1)S(1)} %get-tuple-element.35), kind=kOutput, calls=%fused_computation.7 | convolution fusion | flops 199028736 | bytes 1400832 | tf_op jit(solution)/shard_map/dot_general | solution.py:17
  148.5 1.3 fusion.2
  149.8 11.3 %all-to-all-done.5 = bf16[16,24,192]{2,1,0:T(8,128)(2,1)S(1)} async-done(((bf16[16,24,192]{2,1,0:T(8,128)(2,1)}), bf16[16,24,192]{2,1,0:T(8,128)(2,1)S(1)}, u32[]{:S(2)}, u32[]{:S(2)}) %all-to-all-start.5) | async-done | bytes 147488 | tf_op jit(solution)/shard_map/all_to_all | solution.py:21
  161.1 0.0 copy-done.3
  161.1 0.0 copy-done.4
  161.1 0.9 shard_map.113
Async XLA Ops:
  0.6 53.5 %copy-start = (bf16[1,384,672]{1,2,0:T(8,128)(2,1)S(1)}, bf16[1,384,672]{1,2,0:T(8,128)(2,1)}, u32[]{:S(2)}) copy-start(bf16[1,384,672]{1,2,0:T(8,128)(2,1)} %param.10) | copy-start | bytes 1548292
  0.6 53.5 %copy-start.1 = (bf16[1,384,672]{1,2,0:T(8,128)(2,1)S(1)}, bf16[1,384,672]{1,2,0:T(8,128)(2,1)}, u32[]{:S(2)}) copy-start(bf16[1,384,672]{1,2,0:T(8,128)(2,1)} %param.11) | copy-start | bytes 1548292
  0.7 53.5 %copy-start.2 = (bf16[1,672,384]{2,1,0:T(8,128)(2,1)S(1)}, bf16[1,672,384]{2,1,0:T(8,128)(2,1)}, u32[]{:S(2)}) copy-start(bf16[1,672,384]{2,1,0:T(8,128)(2,1)} %param.12) | copy-start | bytes 1548292
  38.1 16.1 %all-to-all-start.1 = ((bf16[4,384,256]{2,1,0:T(8,128)(2,1)}), bf16[4,384,256]{2,1,0:T(8,128)(2,1)S(1)}, u32[]{:S(2)}, u32[]{:S(2)}) async-start(bf16[4,384,256]{2,1,0:T(8,128)(2,1)} %broadcast_in_dim.34), calls=%async_computation.1 | async-start | bytes 1572864 | tf_op jit(solution)/shard_map/all_to_all | solution.py:21
  54.9 4.2 %collective-permute-start = (bf16[192,2016]{1,0:T(8,128)(2,1)S(1)}, bf16[192,2016]{1,0:T(8,128)(2,1)S(1)}, u32[]{:S(2)}, u32[]{:S(2)}) collective-permute-start(bf16[192,2016]{1,0:T(8,128)(2,1)S(1)} %get-tuple-element.20), channel_id=1, source_target_pairs={{0,1},{1,0},{2,3},{3,2},{4,5},{5,4},{6,7},{7,6},{8,9},{9,8},{10,11... | collective-permute-start | bytes 2322440 | tf_op jit(solution)/shard_map/ppermute | solution.py:200
  121.2 1.2 copy-start.5
  123.9 14.2 %all-to-all-start.4 = ((bf16[4,192,384]{2,1,0:T(8,128)(2,1)}), bf16[4,192,384]{2,1,0:T(8,128)(2,1)S(1)}, u32[]{:S(2)}, u32[]{:S(2)}) async-start(bf16[4,192,384]{2,1,0:T(8,128)(2,1)} %pad_maximum_fusion), calls=%async_computation.4 | async-start | bytes 1179648 | tf_op jit(solution)/shard_map/all_to_all | solution.py:21
  127.4 17.8 %copy-start.6 = (bf16[2,192,2016]{2,1,0:T(8,128)(2,1)S(1)}, bf16[2,192,2016]{2,1,0:T(8,128)(2,1)}, u32[]{:S(2)}) copy-start(bf16[2,192,2016]{2,1,0:T(8,128)(2,1)} %copy-done.5) | copy-start | bytes 4644868
  139.1 22.0 %all-to-all-start.5 = ((bf16[16,24,192]{2,1,0:T(8,128)(2,1)}), bf16[16,24,192]{2,1,0:T(8,128)(2,1)S(1)}, u32[]{:S(2)}, u32[]{:S(2)}) async-start(bf16[16,24,192]{2,1,0:T(8,128)(2,1)} %bitcast.21), calls=%async_computation.5 | async-start | bytes 393216 | tf_op jit(solution)/shard_map/all_to_all | solution.py:21
  146.8 14.3 %copy-start.3 = (f32[384,64]{1,0:T(8,128)S(1)}, f32[384,64]{1,0:T(8,128)}, u32[]{:S(2)}) copy-start(f32[384,64]{1,0:T(8,128)} %get-tuple-element.16.weight_ref) | copy-start | bytes 294916
  146.8 14.3 %copy-start.4 = (bf16[384,64]{1,0:T(8,128)(2,1)S(1)}, bf16[384,64]{1,0:T(8,128)(2,1)}, u32[]{:S(2)}) copy-start(bf16[384,64]{1,0:T(8,128)(2,1)} %get-tuple-element.17.place_ref) | copy-start | bytes 147460

commit v3 on v2

v3 whole, which is shorter than its diff:
```python
import functools

import jax
import jax.numpy as jnp
from jax import lax
from jax.experimental import pallas as pl
from jax.experimental.pallas import tpu as pltpu
from jax.sharding import PartitionSpec as P

LANES = 128
f32 = jnp.float32
bf16 = jnp.bfloat16


def mm(left, right, dims):
    return lax.dot_general(left, right, (dims, ((), ())), preferred_element_type=f32)


def swap(x, axis, groups=None):
    return lax.all_to_all(
        x, axis, split_axis=0, concat_axis=0, tiled=True, axis_index_groups=groups
    )


def iota(shape, axis):
    return lax.broadcasted_iota(jnp.int32, shape, axis)


def call(kernel, outs, flops, n_scalar, *args, far=False, scratch=(), room=16):
    smem = pl.BlockSpec(memory_space=pltpu.SMEM)
    vmem = pl.BlockSpec(memory_space=pltpu.VMEM)
    held = pl.BlockSpec(memory_space=pltpu.HBM) if far else vmem
    outs = [jax.ShapeDtypeStruct(*o) for o in outs]
    moved = sum(a.size * a.dtype.itemsize for a in (*args, *outs))
    return pl.pallas_call(
        kernel,
        out_shape=outs,
        in_specs=[smem] * n_scalar + [held] * (len(args) - n_scalar),
        out_specs=[vmem] * len(outs),
        scratch_shapes=list(scratch),
        compiler_params=pltpu.CompilerParams(vmem_limit_bytes=room * 1024 * 1024),
        cost_estimate=pl.CostEstimate(flops=flops, bytes_accessed=moved, transcendentals=0),
    )(*args)


CAP = 21
PACK = 32
FOLD = PACK - CAP


def dispatch_kernel(
    piece,
    col_ref,
    tok_hbm,
    cot_hbm,
    route_hbm,
    cw_hbm,
    send_ref,
    place_ref,
    place_b_ref,
    place_c_ref,
    weight_ref,
    tok_ref,
    cot_ref,
    route_ref,
    cw_ref,
    sems,
):
    pairs = ((route_hbm, route_ref), (cw_hbm, cw_ref), (tok_hbm, tok_ref), (cot_hbm, cot_ref))
    copies = [pltpu.make_async_copy(a, b, sems.at[i]) for i, (a, b) in enumerate(pairs)]
    for copy in copies:
        copy.start()
    copies[0].wait()
    copies[1].wait()
    width = tok_ref.shape[1]
    top_count, block_len = route_ref.shape
    rows = send_ref.shape[0]
    row = iota((rows, block_len), 0)
    owner = lax.shift_right_logical(row, 5)
    inner = row & (PACK - 1)
    hit = jnp.zeros((rows, block_len), f32)
    weight = jnp.zeros((rows, block_len), f32)
    for k in range(top_count):
        hit_k = owner == route_ref[k : k + 1, :]
        hit = jnp.where(hit_k, 1.0, hit)
        weight = jnp.where(hit_k, cw_ref[k : k + 1, :], weight)
    square = (block_len, block_len)
    earlier = jnp.where(iota(square, 0) < iota(square, 1), 1.0, 0.0).astype(bf16)
    before = mm(hit.astype(bf16), earlier, ((1,), (0,)))
    inner_f = inner.astype(f32)
    folded = jnp.where(inner >= CAP, hit, 0.0)
    place = jnp.where((before == inner_f) & (inner < CAP), hit, 0.0)
    place_b = jnp.where(before == inner_f - CAP, folded, 0.0)
    place_c = jnp.where(before == inner_f - (CAP - FOLD), folded, 0.0)
    place_ref[...] = place.astype(bf16)
    place_b_ref[...] = place_b.astype(bf16)
    place_c_ref[...] = place_c.astype(bf16)
    weight_ref[...] = weight * place
    pick_row = iota((width, LANES), 0) - col_ref[0]
    lane = iota((width, LANES), 1)
    pick_x = jnp.where((pick_row == lane) & (lane < piece), 1.0, 0.0).astype(bf16)
    pick_g = jnp.where((pick_row == lane - piece) & (lane >= piece), 1.0, 0.0).astype(bf16)
    rest = (lane & 63) + (LANES - piece)
    pick_r = jnp.where(pick_row == rest, 1.0, 0.0).astype(bf16)
    copies[2].wait()
    copies[3].wait()
    cot = cot_ref[...]
    first = mm(tok_ref[...], pick_x, ((1,), (0,))) + mm(cot, pick_g, ((1,), (0,)))
    last = mm(cot, pick_r, ((1,), (0,))).astype(bf16)
    lanes = iota((rows, LANES), 1)
    scale = jnp.sum(weight * place, axis=1, keepdims=True)
    scale_b = jnp.sum(weight * place_b, axis=1, keepdims=True)
    scale_c = jnp.sum(weight * place_c, axis=1, keepdims=True)
    a = mm(place.astype(bf16), first.astype(bf16), ((1,), (0,)))
    b = mm(place_b.astype(bf16), last, ((1,), (0,)))
    c = mm(place_c.astype(bf16), last, ((1,), (0,)))
    a = jnp.where(lanes < piece, a, a * scale)
    send_ref[...] = (a + jnp.where(lanes < 64, b * scale_b, c * scale_c)).astype(bf16)


def selectors(slots, rows, flip):
    shape, slot_axis = ((rows, slots), 1) if flip else ((slots, rows), 0)
    slot = iota(shape, slot_axis)
    row = iota(shape, 1 - slot_axis)
    base = lax.shift_right_logical(row, 5) * CAP
    inner = row & (PACK - 1)
    at = slot - base
    sel_a = jnp.where((at == inner) & (inner < CAP), 1.0, 0.0).astype(bf16)
    low = at == inner - CAP
    high = (at == inner - (CAP - FOLD)) & (inner < PACK - 1)
    sel_b = jnp.where((low | high) & (inner >= CAP), 1.0, 0.0).astype(bf16)
    return sel_a, sel_b


def is_low(slots, lanes):
    slot = iota((slots, lanes), 0)
    rank = slot - lax.shift_right_logical(slot * 3121, 16) * CAP
    return rank < FOLD


def partials(half_ref, xg, w_ref, part_ref):
    chunks = part_ref.shape[0]
    for j in range(0, chunks, 2):
        at = half_ref[0] * chunks + j
        w = jnp.concatenate([w_ref[at], w_ref[at + 1]], axis=0)
        got = mm(xg, w, ((1,), (1,))).astype(bf16)
        part_ref[j] = got[:, :LANES]
        part_ref[j + 1] = got[:, LANES:]


def first_kernel(piece, half_ref, pack_ref, w_ref, part_ref, xg_ref):
    n_etp, rows, _ = pack_ref.shape
    slots = part_ref.shape[1]
    sel_a, sel_b = selectors(slots, rows, False)
    packed = jnp.concatenate([pack_ref[i] for i in range(n_etp)], axis=1)
    a = mm(sel_a, packed, ((1,), (0,)))
    b = mm(sel_b, packed, ((1,), (0,)))
    low = is_low(slots, 64)
    parts_x, parts_g = [], []
    for i in range(n_etp):
        at = LANES * i
        parts_x.append(a[:, at : at + piece])
        parts_g.append(a[:, at + piece : at + LANES])
        parts_g.append(jnp.where(low, b[:, at : at + 64], b[:, at + 64 : at + LANES]))
    xg = jnp.concatenate(parts_x + parts_g, axis=1).astype(bf16)
    xg_ref[...] = xg
    partials(half_ref, xg, w_ref, part_ref)


def second_kernel(half_ref, xg_ref, w_ref, part_ref):
    partials(half_ref, xg_ref[...], w_ref, part_ref)


def act_kernel(unit, sum_ref, act_ref):
    total = sum_ref[0].astype(f32)
    for j in range(1, sum_ref.shape[0]):
        total = total + sum_ref[j].astype(f32)
    keep = iota(total.shape, 1) < unit
    gate = jnp.where(keep, total, 0.0)
    up = jnp.where(keep, pltpu.roll(total, LANES - unit, 1), 0.0)
    d_hidden = jnp.where(keep, pltpu.roll(total, LANES - 2 * unit, 1), 0.0)
    sig = jax.nn.sigmoid(gate)
    hidden = gate * sig * up
    d_gate = d_hidden * up * sig * (1.0 + gate * (1.0 - sig))
    d_up = d_hidden * gate * sig
    act_ref[...] = (
        hidden + pltpu.roll(d_gate, unit, 1) + pltpu.roll(d_up, 2 * unit, 1)
    ).astype(bf16)


def back_sum(half_ref, act_ref, w_ref):
    chunks = act_ref.shape[0]
    act = jnp.concatenate([act_ref[j] for j in range(chunks)], axis=1)
    w = w_ref[pl.ds(half_ref[0] * chunks, chunks)]
    return mm(act, w.reshape(chunks * LANES, w.shape[2]), ((1,), (0,)))


def back_kernel(half_ref, act_ref, w_ref, sum_ref):
    sum_ref[...] = back_sum(half_ref, act_ref, w_ref)


def pack_kernel(piece, half_ref, act_ref, w_ref, sum_ref, pack_ref):
    n_etp, rows, _ = pack_ref.shape
    slots, width = sum_ref.shape[0], sum_ref.shape[1] // 2
    total = (sum_ref[...] + back_sum(half_ref, act_ref, w_ref)).astype(bf16).astype(f32)
    sel_a, sel_b = selectors(slots, rows, True)
    low = is_low(slots, 64)
    for i in range(n_etp):
        y = total[:, piece * i : piece * (i + 1)]
        at = width + piece * i
        a = jnp.concatenate([y, total[:, at : at + LANES - piece]], axis=1).astype(bf16)
        tail = total[:, at + LANES - piece : at + piece]
        b = jnp.concatenate(
            [jnp.where(low, tail, 0.0), jnp.where(low, 0.0, tail)], axis=1
        ).astype(bf16)
        pack_ref[i] = (mm(sel_a, a, ((1,), (0,))) + mm(sel_b, b, ((1,), (0,)))).astype(bf16)


def combine_kernel(
    piece, weight_ref, place_ref, place_b_ref, place_c_ref, back_ref, out_ref, grad_ref
):
    back = back_ref[...]
    rest = weight_ref[...]
    total = None
    for _ in range(3):
        high = rest.astype(bf16)
        rest = rest - high.astype(f32)
        term = mm(high, back, ((0,), (0,)))
        total = term if total is None else total + term
    out_ref[...] = total[:, :piece].astype(bf16)
    a = mm(place_ref[...], back, ((0,), (0,)))
    b = mm(place_b_ref[...], back, ((0,), (0,)))
    c = mm(place_c_ref[...], back, ((0,), (0,)))
    grad_ref[...] = jnp.concatenate(
        [a[:, piece:LANES], b[:, :64] + c[:, 64:]], axis=1
    ).astype(bf16)


def local(tokens, routes, combine_weights, gate_weight, up_weight, down_weight, out_cotangent):
    block_len, top_count = routes.shape
    n_exp = lax.axis_size("expert")
    n_etp = lax.axis_size("etp")
    n_dp = lax.axis_size("dp")
    n_y = n_dp // 2
    width = tokens.shape[1]
    piece = width // n_etp
    hid = gate_weight.shape[2]
    unit = hid // n_dp
    slots = n_exp * CAP
    rows = n_exp * PACK
    same_core = [[2 * y + c for y in range(n_y)] for c in range(2)]
    other_core = [(i, i ^ 1) for i in range(n_dp)]
    core = lax.bitwise_and(lax.axis_index("dp"), 1)
    mine, theirs = core[None], (1 - core)[None]
    col = lax.axis_index("etp") * piece

    send, place, place_b, place_c, weight = call(
        functools.partial(dispatch_kernel, piece),
        [
            ((rows, LANES), bf16),
            ((rows, block_len), bf16),
            ((rows, block_len), bf16),
            ((rows, block_len), bf16),
            ((rows, block_len), f32),
        ],
        60_000_000,
        1,
        col[None],
        tokens,
        out_cotangent,
        routes.T,
        combine_weights.T,
        far=True,
        room=60,
        scratch=[
            pltpu.VMEM(tokens.shape, bf16),
            pltpu.VMEM(out_cotangent.shape, bf16),
            pltpu.VMEM((top_count, block_len), jnp.int32),
            pltpu.VMEM((top_count, block_len), f32),
            pltpu.SemaphoreType.DMA((4,)),
        ],
    )
    send, gate_weight, up_weight, down_weight = lax.optimization_barrier(
        (send, gate_weight, up_weight, down_weight)
    )
    w_gate = gate_weight[0].T.reshape(n_dp, unit, width)
    w_up = up_weight[0].T.reshape(n_dp, unit, width)
    w_down = down_weight[0].reshape(n_dp, unit, width)

    def zeros(n):
        return jnp.zeros((n_dp, n, width), bf16)

    spare = LANES - 3 * unit
    w_front = jnp.concatenate(
        [
            jnp.concatenate([w_gate, w_up, zeros(unit + spare)], axis=1),
            jnp.concatenate([zeros(2 * unit), w_down, zeros(spare)], axis=1),
        ],
        axis=2,
    )
    w_back = jnp.concatenate(
        [
            jnp.concatenate([w_down, zeros(2 * unit + spare)], axis=1),
            jnp.concatenate([zeros(unit), w_gate, w_up, zeros(spare)], axis=1),
        ],
        axis=2,
    )

    got = swap(send.reshape(n_exp, PACK, LANES), "expert").reshape(1, rows, LANES)
    packs = swap(jnp.broadcast_to(got, (n_etp, rows, LANES)), "etp")

    half_flops = 2 * slots * 2 * width * n_y * LANES
    part_shape = ((n_y, slots, LANES), bf16)
    part_theirs, xg = call(
        functools.partial(first_kernel, piece),
        [part_shape, ((slots, 2 * width), bf16)],
        2 * half_flops,
        1,
        theirs,
        packs,
        w_front,
    )
    arrived = lax.ppermute(part_theirs, "dp", other_core)
    (part_mine,) = call(second_kernel, [part_shape], half_flops, 1, mine, xg, w_front)
    chip = (part_mine.astype(f32) + arrived.astype(f32)).astype(bf16)
    (act,) = call(
        functools.partial(act_kernel, unit),
        [((slots, LANES), bf16)],
        10_000_000,
        0,
        swap(chip, "dp", same_core),
    )
    act_mine = lax.all_gather(act, "dp", axis=0, axis_index_groups=same_core)
    act_theirs = lax.ppermute(act_mine, "dp", other_core)
    (total,) = call(
        back_kernel, [((slots, 2 * width), f32)], half_flops, 1, mine, act_mine, w_back
    )
    (out,) = call(
        functools.partial(pack_kernel, piece),
        [((n_etp, rows, LANES), bf16)],
        2 * half_flops,
        1,
        theirs,
        act_theirs,
        w_back,
        total,
    )
    out = jnp.sum(swap(out, "etp").astype(f32), axis=0).astype(bf16)
    back = swap(out.reshape(n_exp, PACK, LANES), "expert").reshape(rows, LANES)

    grads = [mm(a, xg, ((1,), (0,))).astype(bf16) for a in (act_mine, act_theirs)]

    def take(start, at):
        own, other = (g[:, start : start + unit, at : at + width] for g in grads)
        first = core == 0
        ordered = jnp.concatenate(
            [jnp.where(first, own, other), jnp.where(first, other, own)], axis=0
        )
        return ordered.reshape(hid, width)

    down_grad = take(0, width)
    gate_grad = take(unit, 0).T
    up_grad = take(2 * unit, 0).T
    layer_output, tokens_grad = call(
        functools.partial(combine_kernel, piece),
        [((block_len, piece), bf16), ((block_len, piece), bf16)],
        50_000_000,
        0,
        weight,
        place,
        place_b,
        place_c,
        back,
    )
    return layer_output, tokens_grad, gate_grad[None], up_grad[None], down_grad[None]


def solution(mesh):
    placed = (
        P("expert", "dp"),
        P("expert", None),
        P("expert", None),
        P("expert", "dp", "etp"),
        P("expert", "dp", "etp"),
        P("expert", "etp", "dp"),
        P("expert", "dp"),
    )
    return jax.shard_map(
        local,
        mesh=mesh,
        in_specs=placed,
        out_specs=(
            P("expert", ("dp", "etp")),
            P("expert", ("dp", "etp")),
            P("expert", "dp", "etp"),
            P("expert", "dp", "etp"),
            P("expert", "etp", "dp"),
        ),
        check_vma=False,
    )
```

time: 163 us -> 158 us (0.969)
  the two profiles are of different devices: /device:TPU:64 before, /device:TPU:2 now
where the time goes in v3:
time: 158 us; the launch traced here: 157 us
  blocking collectives  56 us (35%)
  starting transfers between devices  38.3 us (24%)
  waiting for transfers between devices  23.4 us (15%)
  local copies, waits for them, and re-layouts  13.8 us (9%)
  Pallas kernels  11.7 us (7%)
  other arithmetic  7.8 us (5%)
  matrix products  5.53 us (4%)
    all_to_all x4, starting transfers between devices, swap(): lax.all_to_all(x, axis, split_axis=0, concat_axis=0, tiled=True, axis_ind...  34.5 us
    all_to_all x1, blocking collectives, swap(): lax.all_to_all(x, axis, split_axis=0, concat_axis=0, tiled=True, axis_ind...  28.2 us
    all_gather x1, blocking collectives, local(): act_mine = lax.all_gather(act, 'dp', axis=0, axis_index_groups=same_core)  27.8 us
    all_to_all x4, waiting for transfers between devices, swap(): lax.all_to_all(x, axis, split_axis=0, concat_axis=0, tiled=True, axis_ind...  21.4 us
    pallas_call x7, Pallas kernels, call(): pl.pallas_call(kernel, out_shape=outs, in_specs=[smem] * n_scalar + [held...  11.7 us
    dot_general x2, matrix products, mm(): lax.dot_general(left, right, (dims, ((), ())), preferred_element_type=f32)  5.53 us
    concatenate x1, other arithmetic, local(): jnp.concatenate([jnp.concatenate([w_down, zeros(2 * unit + spare)], axis=...  5 us
  transfers between devices with their start and end apart: 6, of which 6 were waited for; matrix products, arithmetic and copies ran while one was open for 14% of the time, Pallas kernels for 2%

profile of v3, /device:TPU:2, one launch (start us, length us, event | category | flops | bytes accessed | tf_op | source)
XLA Modules:
  0.0 157.4 jit_solution(16721169872670898498)
XLA Ops:
  0.6 2.2 %shard_map.110 = (bf16[512,128]{1,0:T(8,128)(2,1)}, bf16[512,64]{1,0:T(8,128)(2,1)}, bf16[512,64]{1,0:T(8,128)(2,1)}, bf16[512,64]{1,0:T(8,128)(2,1)}, f32[512,64]{1,0:T(8,128)}) custom-call(s32[1]{0:T(128)} %bitcast.col_ref, bf16[64,384]{1,0:T(8,128)(2,1)} %tok_hbm.1, bf16[64,384]{1,0:T(8,128)(2,1)} %cot_hbm.1, s32[4,64]{1,0:T(4,128)} %bitcast.36, ...), custom_call_target="tpu_custom_call" | custom-call | flops 60000000 | bytes 559108 | tf_op jit(solution)/shard_map/pallas_call | solution.py:35
  2.9 18.9 %all-to-all-start = ((bf16[16,32,128]{2,1,0:T(8,128)(2,1)}), bf16[16,32,128]{2,1,0:T(8,128)(2,1)S(1)}, u32[]{:S(2)}, u32[]{:S(2)}) async-start(bf16[16,32,128]{2,1,0:T(8,128)(2,1)} %bitcast.35), calls=%async_computation | async-start | bytes 262144 | tf_op jit(solution)/shard_map/all_to_all | solution.py:20
  21.8 2.0 %reshape_squeeze.3 = bf16[16,42,384]{2,1,0:T(8,128)(2,1)} reshape(bf16[1,672,384]{2,1,0:T(8,128)(2,1)} %param.12) | data formatting | bytes 1032192 | tf_op jit(solution)/shard_map/reshape;squeeze | solution.py:288
  23.8 2.0 %reshape.35 = bf16[16,42,384]{2,1,0:T(8,128)(2,1)} reshape(bf16[672,384]{1,0:T(8,128)(2,1)} %bitcast.31) | data formatting | bytes 1032192 | tf_op jit(solution)/shard_map/reshape | solution.py:287
  25.8 2.0 %reshape.34 = bf16[16,42,384]{2,1,0:T(8,128)(2,1)} reshape(bf16[672,384]{1,0:T(8,128)(2,1)} %bitcast.32) | data formatting | bytes 1032192 | tf_op jit(solution)/shard_map/reshape | solution.py:286
  27.9 0.7 pad.15.clone
  28.6 0.7 pad.14.clone
  29.3 7.2 %all-to-all-done = bf16[16,32,128]{2,1,0:T(8,128)(2,1)S(1)} async-done(((bf16[16,32,128]{2,1,0:T(8,128)(2,1)}), bf16[16,32,128]{2,1,0:T(8,128)(2,1)S(1)}, u32[]{:S(2)}, u32[]{:S(2)}) %all-to-all-start) | async-done | bytes 131104 | tf_op jit(solution)/shard_map/all_to_all | solution.py:20
  36.5 0.9 broadcast_in_dim.36
  37.3 4.8 %all-to-all-start.1 = ((bf16[4,512,128]{2,1,0:T(8,128)(2,1)}), bf16[4,512,128]{2,1,0:T(8,128)(2,1)}, u32[]{:S(2)}, u32[]{:S(2)}) async-start(bf16[4,512,128]{2,1,0:T(8,128)(2,1)} %broadcast_in_dim.36), calls=%async_computation.1 | async-start | bytes 1048576 | tf_op jit(solution)/shard_map/all_to_all | solution.py:20
  42.2 5.0 %fusion.1 = (bf16[16,128,768]{2,1,0:T(8,128)(2,1)S(1)}, bf16[16,128,768]{2,1,0:T(8,128)(2,1)}) fusion(bf16[16,42,384]{2,1,0:T(8,128)(2,1)} %reshape_squeeze.3, bf16[16,42,384]{2,1,0:T(8,128)(2,1)} %reshape.35, bf16[16,42,384]{2,1,0:T(8,128)(2,1)} %reshape.34, bf16[128,768]{1,0:T(8,128)(2,1)S(1)} %pad.8.clone, bf16[128,768]{1,0:T(8,128)(2,1)S(1)} %pad.17.clone, ...), kind=kLoop, calls=%fused_computation.2 | loop fusion | flops 36175872 | bytes 8626176 | tf_op jit(solution)/shard_map/concatenate | solution.py:301
  47.2 1.7 %all-to-all-done.1.pack_ref = bf16[4,512,128]{2,1,0:T(8,128)(2,1)} async-done(((bf16[4,512,128]{2,1,0:T(8,128)(2,1)}), bf16[4,512,128]{2,1,0:T(8,128)(2,1)}, u32[]{:S(2)}, u32[]{:S(2)}) %all-to-all-start.1) | async-done | bytes 524320 | tf_op jit(solution)/shard_map/all_to_all | solution.py:20
  48.9 0.0 copy-start
  48.9 1.9 %copy-done = bf16[16,128,768]{2,1,0:T(8,128)(2,1)S(1)} copy-done((bf16[16,128,768]{2,1,0:T(8,128)(2,1)S(1)}, bf16[16,128,768]{2,1,0:T(8,128)(2,1)}, u32[]{:S(2)}) %copy-start) | copy-done | bytes 3145752
  50.8 0.0 copy-start.1
  50.8 2.6 %shard_map.111 = (bf16[8,336,128]{2,1,0:T(8,128)(2,1)S(1)}, bf16[336,768]{1,0:T(8,128)(2,1)S(1)}) custom-call(s32[1]{0:T(128)} %bitcast.3.half_ref, bf16[4,512,128]{2,1,0:T(8,128)(2,1)} %all-to-all-done.1.pack_ref, bf16[16,128,768]{2,1,0:T(8,128)(2,1)S(1)} %copy-done), custom_call_target="tpu_custom_call" | custom-call | flops 1056964608 | bytes 4874244 | tf_op jit(solution)/shard_map/pallas_call | solution.py:35
  53.4 0.0 copy-start.2
  53.4 1.9 %collective-permute-start = (bf16[8,336,128]{2,1,0:T(8,128)(2,1)S(1)}, bf16[8,336,128]{2,1,0:T(8,128)(2,1)S(1)}, u32[]{:S(2)}, u32[]{:S(2)}) collective-permute-start(bf16[8,336,128]{2,1,0:T(8,128)(2,1)S(1)} %get-tuple-element.28), channel_id=1, source_target_pairs={{0,1},{1,0},{2,3},{3,2},{4,5},{5,4},{6,7},{7,6},{8,9},{9,8},{10,11... | collective-permute-start | bytes 2064392 | tf_op jit(solution)/shard_map/ppermute | solution.py:323
  55.3 0.0 copy-done.1
  55.3 0.7 shard_map.112
  56.1 1.4 collective-permute-done
  57.4 0.2 add_convert_fusion
  57.6 0.0 copy-done.2
  57.6 28.2 %all_to_all.25.sum_ref = bf16[8,336,128]{2,1,0:T(8,128)(2,1)S(1)} all-to-all(bf16[8,336,128]{2,1,0:T(8,128)(2,1)S(1)} %add_convert_fusion), channel_id=1, replica_groups={{0,2,4,6,8,10,12,14},{1,3,5,7,9,11,13,15},{16,18,20,22,24,26,28,30},{17..., dimensions={0} | all-to-all | bytes 1376256 | tf_op jit(solution)/shard_map/all_to_all | solution.py:20
  85.8 0.3 shard_map.113
  86.2 27.8 %all-gather = bf16[2688,128]{1,0:T(8,128)(2,1)} all-gather(bf16[336,128]{1,0:T(8,128)(2,1)S(1)} %shard_map.113), channel_id=2, replica_groups={{0,2,4,6,8,10,12,14},{1,3,5,7,9,11,13,15},{16,18,20,22,24,26,28,30},{17..., dimensions={0}, use_global_device_ids=true | all-gather | bytes 774144 | tf_op jit(solution)/shard_map/all_gather | solution.py:333
  113.9 1.9 %collective-permute-start.1 = (bf16[8,336,128]{2,1,0:T(8,128)(2,1)}, bf16[8,336,128]{2,1,0:T(8,128)(2,1)}, u32[]{:S(2)}, u32[]{:S(2)}) collective-permute-start(bf16[8,336,128]{2,1,0:T(8,128)(2,1)} %bitcast.11.act_ref), channel_id=1, source_target_pairs={{0,1},{1,0},{2,3},{3,2},{4,5},{5,4},{6,7},{7,6},{8,9},{9,8},{10,11... | collective-permute-start | bytes 2064392 | tf_op jit(solution)/shard_map/ppermute | solution.py:334
  115.9 1.8 %shard_map.114.sum_ref = f32[336,768]{1,0:T(8,128)S(1)} custom-call(s32[1]{0:T(128)} %bitcast.4.half_ref, bf16[8,336,128]{2,1,0:T(8,128)(2,1)} %bitcast.11.act_ref, bf16[16,128,768]{2,1,0:T(8,128)(2,1)S(1)} %get-tuple-element.37.w_ref), custom_call_target="tpu_custom_call" | custom-call | flops 528482304 | bytes 4866052 | tf_op jit(solution)/shard_map/pallas_call | solution.py:35
  117.7 0.6 collective-permute-done.1.act_ref
  118.3 2.8 %shard_map.115 = bf16[4,512,128]{2,1,0:T(8,128)(2,1)S(1)} custom-call(s32[1]{0:T(128)} %bitcast.3.half_ref, bf16[8,336,128]{2,1,0:T(8,128)(2,1)} %collective-permute-done.1.act_ref, bf16[16,128,768]{2,1,0:T(8,128)(2,1)S(1)} %get-tuple-element.37.w_ref, f32[336,768]{1,0:T(8,128)S(1)} %shard_map.114.sum_ref), custom_call_target="tpu_custom_call" | custom-call | flops 1056964608 | bytes 5390340 | tf_op jit(solution)/shard_map/pallas_call | solution.py:35
  121.1 0.0 copy-start.4
  121.1 0.8 copy-done.4
  121.9 0.0 copy-start.3
  121.9 5.0 %all-to-all-start.3 = ((bf16[4,512,128]{2,1,0:T(8,128)(2,1)}), bf16[4,512,128]{2,1,0:T(8,128)(2,1)S(1)}, u32[]{:S(2)}, u32[]{:S(2)}) async-start(bf16[4,512,128]{2,1,0:T(8,128)(2,1)} %copy-done.4), calls=%async_computation.3 | async-start | bytes 1048576 | tf_op jit(solution)/shard_map/all_to_all | solution.py:20
  127.0 2.3 %convolution_convert_fusion.1 = bf16[8,128,768]{2,1,0:T(8,128)(2,1)S(1)} fusion(bf16[8,336,128]{2,1,0:T(8,128)(2,1)} %bitcast.11.act_ref, bf16[336,768]{1,0:T(8,128)(2,1)} %copy-done.2), kind=kOutput, calls=%fused_computation.5 | convolution fusion | flops 529268736 | bytes 2777088 | tf_op jit(solution)/shard_map/dot_general | solution.py:16
  129.2 0.0 copy-done.3
  129.2 3.3 %convolution_convert_fusion = bf16[8,128,768]{2,1,0:T(8,128)(2,1)} fusion(bf16[8,336,128]{2,1,0:T(8,128)(2,1)} %collective-permute-done.1.act_ref, bf16[336,768]{1,0:T(8,128)(2,1)S(1)} %copy-done.3), kind=kOutput, calls=%fused_computation.4 | convolution fusion | flops 529268736 | bytes 2777088 | tf_op jit(solution)/shard_map/dot_general | solution.py:16
  132.5 3.1 %all-to-all-done.3 = bf16[4,512,128]{2,1,0:T(8,128)(2,1)S(1)} async-done(((bf16[4,512,128]{2,1,0:T(8,128)(2,1)}), bf16[4,512,128]{2,1,0:T(8,128)(2,1)S(1)}, u32[]{:S(2)}, u32[]{:S(2)}) %all-to-all-start.3) | async-done | bytes 524320 | tf_op jit(solution)/shard_map/all_to_all | solution.py:20
  135.6 0.8 reduce_sum.12
  136.3 5.7 %all-to-all-start.4 = ((bf16[16,32,128]{2,1,0:T(8,128)(2,1)}), bf16[16,32,128]{2,1,0:T(8,128)(2,1)S(1)}, u32[]{:S(2)}, u32[]{:S(2)}) async-start(bf16[16,32,128]{2,1,0:T(8,128)(2,1)} %bitcast.12), calls=%async_computation.4 | async-start | bytes 262144 | tf_op jit(solution)/shard_map/all_to_all | solution.py:20
  142.1 1.6 %broadcast_select_fusion.1 = (bf16[8,42,384]{2,1,0:T(8,128)(2,1)S(1)}, bf16[8,42,384]{2,1,0:T(8,128)(2,1)S(1)}, bf16[8,42,384]{2,1,0:T(8,128)(2,1)S(1)}, bf16[8,...) fusion(pred[]{:T(512)S(6)} %eq.2, ...), kind=kLoop, calls=%fused_computation.13 | loop fusion | flops 774144 | bytes 3096577 | tf_op jit(solution)/shard_map/jit(_where)/select_n | solution.py:357
  143.7 0.0 copy-start.5
  143.7 0.0 copy-start.6
  143.7 0.0 copy-start.7
  143.7 0.0 copy-start.8
  143.7 0.2 pad_maximum_fusion
  143.9 0.9 reshape.38
  144.8 0.9 reshape.39
  145.7 0.1 pad_maximum_fusion.2
  145.8 0.9 broadcast_in_dim_reshape.3
  146.8 9.4 %all-to-all-done.4 = bf16[16,32,128]{2,1,0:T(8,128)(2,1)S(1)} async-done(((bf16[16,32,128]{2,1,0:T(8,128)(2,1)}), bf16[16,32,128]{2,1,0:T(8,128)(2,1)S(1)}, u32[]{:S(2)}, u32[]{:S(2)}) %all-to-all-start.4) | async-done | bytes 131104 | tf_op jit(solution)/shard_map/all_to_all | solution.py:20
  156.2 0.0 copy-done.5
  156.2 0.0 copy-done.6
  156.2 0.0 copy-done.7
  156.2 0.0 copy-done.8
  156.2 1.2 shard_map.116
  (6 shorter events, 0.1 us)
Async XLA Ops:
  2.9 33.6 %all-to-all-start = ((bf16[16,32,128]{2,1,0:T(8,128)(2,1)}), bf16[16,32,128]{2,1,0:T(8,128)(2,1)S(1)}, u32[]{:S(2)}, u32[]{:S(2)}) async-start(bf16[16,32,128]{2,1,0:T(8,128)(2,1)} %bitcast.35), calls=%async_computation | async-start | bytes 262144 | tf_op jit(solution)/shard_map/all_to_all | solution.py:20
  37.3 11.6 %all-to-all-start.1 = ((bf16[4,512,128]{2,1,0:T(8,128)(2,1)}), bf16[4,512,128]{2,1,0:T(8,128)(2,1)}, u32[]{:S(2)}, u32[]{:S(2)}) async-start(bf16[4,512,128]{2,1,0:T(8,128)(2,1)} %broadcast_in_dim.36), calls=%async_computation.1 | async-start | bytes 1048576 | tf_op jit(solution)/shard_map/all_to_all | solution.py:20
  48.9 1.9 %copy-start = (bf16[16,128,768]{2,1,0:T(8,128)(2,1)S(1)}, bf16[16,128,768]{2,1,0:T(8,128)(2,1)}, u32[]{:S(2)}) copy-start(bf16[16,128,768]{2,1,0:T(8,128)(2,1)} %get-tuple-element.38.w_ref) | copy-start | bytes 9437188
  50.8 4.5 %copy-start.1 = (bf16[16,128,768]{2,1,0:T(8,128)(2,1)S(1)}, bf16[16,128,768]{2,1,0:T(8,128)(2,1)}, u32[]{:S(2)}) copy-start(bf16[16,128,768]{2,1,0:T(8,128)(2,1)} %get-tuple-element.38.w_ref) | copy-start | bytes 9437188
  53.4 4.3 %copy-start.2 = (bf16[336,768]{1,0:T(8,128)(2,1)}, bf16[336,768]{1,0:T(8,128)(2,1)S(1)}, u32[]{:S(2)}) copy-start(bf16[336,768]{1,0:T(8,128)(2,1)S(1)} %get-tuple-element.27.xg_ref) | copy-start | bytes 1548292
  53.4 4.0 %collective-permute-start = (bf16[8,336,128]{2,1,0:T(8,128)(2,1)S(1)}, bf16[8,336,128]{2,1,0:T(8,128)(2,1)S(1)}, u32[]{:S(2)}, u32[]{:S(2)}) collective-permute-start(bf16[8,336,128]{2,1,0:T(8,128)(2,1)S(1)} %get-tuple-element.28), channel_id=1, source_target_pairs={{0,1},{1,0},{2,3},{3,2},{4,5},{5,4},{6,7},{7,6},{8,9},{9,8},{10,11... | collective-permute-start | bytes 2064392 | tf_op jit(solution)/shard_map/ppermute | solution.py:323
  113.9 4.4 %collective-permute-start.1 = (bf16[8,336,128]{2,1,0:T(8,128)(2,1)}, bf16[8,336,128]{2,1,0:T(8,128)(2,1)}, u32[]{:S(2)}, u32[]{:S(2)}) collective-permute-start(bf16[8,336,128]{2,1,0:T(8,128)(2,1)} %bitcast.11.act_ref), channel_id=1, source_target_pairs={{0,1},{1,0},{2,3},{3,2},{4,5},{5,4},{6,7},{7,6},{8,9},{9,8},{10,11... | collective-permute-start | bytes 2064392 | tf_op jit(solution)/shard_map/ppermute | solution.py:334
  121.1 0.8 copy-start.4
  121.9 7.3 %copy-start.3 = (bf16[336,768]{1,0:T(8,128)(2,1)S(1)}, bf16[336,768]{1,0:T(8,128)(2,1)}, u32[]{:S(2)}) copy-start(bf16[336,768]{1,0:T(8,128)(2,1)} %copy-done.2) | copy-start | bytes 1548292
  121.9 13.6 %all-to-all-start.3 = ((bf16[4,512,128]{2,1,0:T(8,128)(2,1)}), bf16[4,512,128]{2,1,0:T(8,128)(2,1)S(1)}, u32[]{:S(2)}, u32[]{:S(2)}) async-start(bf16[4,512,128]{2,1,0:T(8,128)(2,1)} %copy-done.4), calls=%async_computation.3 | async-start | bytes 1048576 | tf_op jit(solution)/shard_map/all_to_all | solution.py:20
  136.3 19.9 %all-to-all-start.4 = ((bf16[16,32,128]{2,1,0:T(8,128)(2,1)}), bf16[16,32,128]{2,1,0:T(8,128)(2,1)S(1)}, u32[]{:S(2)}, u32[]{:S(2)}) async-start(bf16[16,32,128]{2,1,0:T(8,128)(2,1)} %bitcast.12), calls=%async_computation.4 | async-start | bytes 262144 | tf_op jit(solution)/shard_map/all_to_all | solution.py:20
  143.7 12.5 %copy-start.5 = (f32[512,64]{1,0:T(8,128)S(1)}, f32[512,64]{1,0:T(8,128)}, u32[]{:S(2)}) copy-start(f32[512,64]{1,0:T(8,128)} %get-tuple-element.18.weight_ref) | copy-start | bytes 393220
  143.7 12.5 %copy-start.6 = (bf16[512,64]{1,0:T(8,128)(2,1)S(1)}, bf16[512,64]{1,0:T(8,128)(2,1)}, u32[]{:S(2)}) copy-start(bf16[512,64]{1,0:T(8,128)(2,1)} %get-tuple-element.19.place_ref) | copy-start | bytes 196612
  143.7 12.5 %copy-start.7 = (bf16[512,64]{1,0:T(8,128)(2,1)S(1)}, bf16[512,64]{1,0:T(8,128)(2,1)}, u32[]{:S(2)}) copy-start(bf16[512,64]{1,0:T(8,128)(2,1)} %get-tuple-element.20.place_b_ref) | copy-start | bytes 196612
  143.7 12.5 %copy-start.8 = (bf16[512,64]{1,0:T(8,128)(2,1)S(1)}, bf16[512,64]{1,0:T(8,128)(2,1)}, u32[]{:S(2)}) copy-start(bf16[512,64]{1,0:T(8,128)(2,1)} %get-tuple-element.21.place_c_ref) | copy-start | bytes 196612

commit v4 on v3

--- a/solution.py
+++ b/solution.py
@@ -46,6 +46,7 @@
 CAP = 21
 PACK = 32
 FOLD = PACK - CAP
+HEAD = 240
 
 
 def dispatch_kernel(
@@ -141,8 +142,8 @@
 def partials(half_ref, xg, w_ref, part_ref):
     chunks = part_ref.shape[0]
     for j in range(0, chunks, 2):
-        at = half_ref[0] * chunks + j
-        w = jnp.concatenate([w_ref[at], w_ref[at + 1]], axis=0)
+        at = half_ref[0] + 2 * j
+        w = jnp.concatenate([w_ref[at], w_ref[at + 2]], axis=0)
         got = mm(xg, w, ((1,), (1,))).astype(bf16)
         part_ref[j] = got[:, :LANES]
         part_ref[j + 1] = got[:, LANES:]
@@ -188,32 +189,34 @@
     ).astype(bf16)
 
 
-def back_sum(half_ref, act_ref, w_ref):
-    chunks = act_ref.shape[0]
-    act = jnp.concatenate([act_ref[j] for j in range(chunks)], axis=1)
-    w = w_ref[pl.ds(half_ref[0] * chunks, chunks)]
-    return mm(act, w.reshape(chunks * LANES, w.shape[2]), ((1,), (0,)))
-
-
-def back_kernel(half_ref, act_ref, w_ref, sum_ref):
-    sum_ref[...] = back_sum(half_ref, act_ref, w_ref)
-
-
-def pack_kernel(piece, half_ref, act_ref, w_ref, sum_ref, pack_ref):
+def back_kernel(piece, head_ref, tail_ref, w_ref, pack_ref):
+    chunks, slots = head_ref.shape[0], head_ref.shape[1] + tail_ref.shape[1]
     n_etp, rows, _ = pack_ref.shape
-    slots, width = sum_ref.shape[0], sum_ref.shape[1] // 2
-    total = (sum_ref[...] + back_sum(half_ref, act_ref, w_ref)).astype(bf16).astype(f32)
+    width = w_ref.shape[2] // 2
+    act = jnp.concatenate(
+        [
+            jnp.concatenate([ref[j] for j in range(chunks)], axis=1)
+            for ref in (head_ref, tail_ref)
+        ],
+        axis=0,
+    )
+    total = mm(act, w_ref[...].reshape(chunks * LANES, 2 * width), ((1,), (0,)))
+    total = total.astype(bf16).astype(f32)
     sel_a, sel_b = selectors(slots, rows, True)
     low = is_low(slots, 64)
+    parts_a, parts_b = [], []
     for i in range(n_etp):
-        y = total[:, piece * i : piece * (i + 1)]
+        parts_a.append(total[:, piece * i : piece * (i + 1)])
         at = width + piece * i
-        a = jnp.concatenate([y, total[:, at : at + LANES - piece]], axis=1).astype(bf16)
+        parts_a.append(total[:, at : at + LANES - piece])
         tail = total[:, at + LANES - piece : at + piece]
-        b = jnp.concatenate(
-            [jnp.where(low, tail, 0.0), jnp.where(low, 0.0, tail)], axis=1
-        ).astype(bf16)
-        pack_ref[i] = (mm(sel_a, a, ((1,), (0,))) + mm(sel_b, b, ((1,), (0,)))).astype(bf16)
+        parts_b.append(jnp.where(low, tail, 0.0))
+        parts_b.append(jnp.where(low, 0.0, tail))
+    a = jnp.concatenate(parts_a, axis=1).astype(bf16)
+    b = jnp.concatenate(parts_b, axis=1).astype(bf16)
+    packed = (mm(sel_a, a, ((1,), (0,))) + mm(sel_b, b, ((1,), (0,)))).astype(bf16)
+    for i in range(n_etp):
+        pack_ref[i] = packed[:, LANES * i : LANES * (i + 1)]
 
 
 def combine_kernel(
@@ -286,22 +289,15 @@
     w_gate = gate_weight[0].T.reshape(n_dp, unit, width)
     w_up = up_weight[0].T.reshape(n_dp, unit, width)
     w_down = down_weight[0].reshape(n_dp, unit, width)
+    spare = LANES - 3 * unit
 
     def zeros(n):
         return jnp.zeros((n_dp, n, width), bf16)
 
-    spare = LANES - 3 * unit
     w_front = jnp.concatenate(
         [
             jnp.concatenate([w_gate, w_up, zeros(unit + spare)], axis=1),
             jnp.concatenate([zeros(2 * unit), w_down, zeros(spare)], axis=1),
-        ],
-        axis=2,
-    )
-    w_back = jnp.concatenate(
-        [
-            jnp.concatenate([w_down, zeros(2 * unit + spare)], axis=1),
-            jnp.concatenate([zeros(unit), w_gate, w_up, zeros(spare)], axis=1),
         ],
         axis=2,
     )
@@ -320,43 +316,47 @@
         packs,
         w_front,
     )
+    part_theirs, w_gate, w_up, w_down = lax.optimization_barrier(
+        (part_theirs, w_gate, w_up, w_down)
+    )
+    w_back = jnp.concatenate(
+        [
+            jnp.concatenate([w_down, zeros(2 * unit + spare)], axis=1),
+            jnp.concatenate([zeros(unit), w_gate, w_up, zeros(spare)], axis=1),
+        ],
+        axis=2,
+    )
     arrived = lax.ppermute(part_theirs, "dp", other_core)
     (part_mine,) = call(second_kernel, [part_shape], half_flops, 1, mine, xg, w_front)
     chip = (part_mine.astype(f32) + arrived.astype(f32)).astype(bf16)
+    sums, w_back = lax.optimization_barrier((swap(chip, "dp", same_core), w_back))
     (act,) = call(
         functools.partial(act_kernel, unit),
         [((slots, LANES), bf16)],
         10_000_000,
         0,
-        swap(chip, "dp", same_core),
-    )
-    act_mine = lax.all_gather(act, "dp", axis=0, axis_index_groups=same_core)
-    act_theirs = lax.ppermute(act_mine, "dp", other_core)
-    (total,) = call(
-        back_kernel, [((slots, 2 * width), f32)], half_flops, 1, mine, act_mine, w_back
-    )
+        sums,
+    )
+    tail = jnp.broadcast_to(act[HEAD:], (n_dp, slots - HEAD, LANES))
+    tail = swap(tail, "dp")
+    head = lax.all_gather(act[:HEAD], "dp", axis=0)
     (out,) = call(
-        functools.partial(pack_kernel, piece),
+        functools.partial(back_kernel, piece),
         [((n_etp, rows, LANES), bf16)],
-        2 * half_flops,
-        1,
-        theirs,
-        act_theirs,
+        4 * half_flops,
+        0,
+        head,
+        tail,
         w_back,
-        total,
     )
     out = jnp.sum(swap(out, "etp").astype(f32), axis=0).astype(bf16)
     back = swap(out.reshape(n_exp, PACK, LANES), "expert").reshape(rows, LANES)
 
-    grads = [mm(a, xg, ((1,), (0,))).astype(bf16) for a in (act_mine, act_theirs)]
+    full = jnp.concatenate([head, tail], axis=1)
+    grads = mm(full, xg, ((1,), (0,))).astype(bf16)
 
     def take(start, at):
-        own, other = (g[:, start : start + unit, at : at + width] for g in grads)
-        first = core == 0
-        ordered = jnp.concatenate(
-            [jnp.where(first, own, other), jnp.where(first, other, own)], axis=0
-        )
-        return ordered.reshape(hid, width)
+        return grads[:, start : start + unit, at : at + width].reshape(hid, width)
 
     down_grad = take(0, width)
     gate_grad = take(unit, 0).T

time: 158 us -> 155 us (0.981)
  blocking collectives: 56 us -> 38.9 us
  waiting for transfers between devices: 23.4 us -> 40.3 us
  matrix products: 5.53 us -> 1.83 us
  starting transfers between devices: 38.3 us -> 41.3 us
  Pallas kernels: 11.7 us -> 9.7 us
    all_to_all x4 -> x5, waiting for transfers between devices: 21.4 us -> 39 us  [swap(): lax.all_to_all(x, axis, split_axis=0, concat_axis=0, tiled=True, axis_ind...]
    all_to_all x1, blocking collectives: 28.2 us -> 12.7 us  [swap(): lax.all_to_all(x, axis, split_axis=0, concat_axis=0, tiled=True, axis_ind...]
    all_to_all x4 -> x5, starting transfers between devices: 34.5 us -> 39.4 us  [swap(): lax.all_to_all(x, axis, split_axis=0, concat_axis=0, tiled=True, axis_ind...]
    dot_general x2 -> x1, matrix products: 5.53 us -> 1.83 us  [mm(): lax.dot_general(left, right, (dims, ((), ())), preferred_element_type=f32)]
    pallas_call x7 -> x6, Pallas kernels: 11.7 us -> 9.7 us  [call(): pl.pallas_call(kernel, out_shape=outs, in_specs=[smem] * n_scalar + [held...]
    ppermute x1 -> x0, starting transfers between devices: 1.91 us -> none  [local(): act_theirs = lax.ppermute(act_mine, 'dp', other_core)]
    concatenate x2 -> x1, other arithmetic: 0.23 us -> 2.13 us  [local(): jnp.concatenate([jnp.concatenate([w_gate, w_up, zeros(unit + spare)], axi...]
    select_n x1 -> x0, other arithmetic: 1.6 us -> none  [take(): jnp.where(first, own, other)]
  transfers between devices with their start and end apart: 6 -> 6, of which waited for: 6 -> 5; matrix products, arithmetic and copies ran while one was open for 14% -> 11% of each run, Pallas kernels for 2% -> 0%
where the time goes in v4:
time: 155 us; the launch traced here: 154 us
  starting transfers between devices  41.3 us (27%)
  waiting for transfers between devices  40.3 us (26%)
  blocking collectives  38.9 us (25%)
  local copies, waits for them, and re-layouts  13.6 us (9%)
  Pallas kernels  9.7 us (6%)
  other arithmetic  7.61 us (5%)
  matrix products  1.83 us (1%)
    all_to_all x5, starting transfers between devices, swap(): lax.all_to_all(x, axis, split_axis=0, concat_axis=0, tiled=True, axis_ind...  39.4 us
    all_to_all x5, waiting for transfers between devices, swap(): lax.all_to_all(x, axis, split_axis=0, concat_axis=0, tiled=True, axis_ind...  39 us
    all_gather x1, blocking collectives, local(): head = lax.all_gather(act[:HEAD], 'dp', axis=0)  26.2 us
    all_to_all x1, blocking collectives, swap(): lax.all_to_all(x, axis, split_axis=0, concat_axis=0, tiled=True, axis_ind...  12.7 us
    pallas_call x6, Pallas kernels, call(): pl.pallas_call(kernel, out_shape=outs, in_specs=[smem] * n_scalar + [held...  9.7 us
    concatenate x1, other arithmetic, local(): jnp.concatenate([jnp.concatenate([w_down, zeros(2 * unit + spare)], axis=...  3.68 us
  transfers between devices with their start and end apart: 6, of which 5 were waited for; matrix products, arithmetic and copies ran while one was open for 11% of the time, Pallas kernels for 0%

profile of v4, /device:TPU:2, one launch (start us, length us, event | category | flops | bytes accessed | tf_op | source)
XLA Modules:
  0.0 154.2 jit_solution(13903290797483126592)
XLA Ops:
  0.6 2.2 %shard_map.110 = (bf16[512,128]{1,0:T(8,128)(2,1)}, bf16[512,64]{1,0:T(8,128)(2,1)}, bf16[512,64]{1,0:T(8,128)(2,1)}, bf16[512,64]{1,0:T(8,128)(2,1)}, f32[512,64]{1,0:T(8,128)}) custom-call(s32[1]{0:T(128)} %bitcast.col_ref, bf16[64,384]{1,0:T(8,128)(2,1)} %tok_hbm.1, bf16[64,384]{1,0:T(8,128)(2,1)} %cot_hbm.1, s32[4,64]{1,0:T(4,128)} %bitcast.34, ...), custom_call_target="tpu_custom_call" | custom-call | flops 60000000 | bytes 559108 | tf_op jit(solution)/shard_map/pallas_call | solution.py:35
  2.9 18.9 %all-to-all-start = ((bf16[16,32,128]{2,1,0:T(8,128)(2,1)}), bf16[16,32,128]{2,1,0:T(8,128)(2,1)S(1)}, u32[]{:S(2)}, u32[]{:S(2)}) async-start(bf16[16,32,128]{2,1,0:T(8,128)(2,1)} %bitcast.33), calls=%async_computation | async-start | bytes 262144 | tf_op jit(solution)/shard_map/all_to_all | solution.py:20
  21.8 2.0 %reshape_squeeze.3 = bf16[16,42,384]{2,1,0:T(8,128)(2,1)} reshape(bf16[1,672,384]{2,1,0:T(8,128)(2,1)} %param.12) | data formatting | bytes 1032192 | tf_op jit(solution)/shard_map/reshape;squeeze | solution.py:291
  23.8 2.0 %reshape.35 = bf16[16,42,384]{2,1,0:T(8,128)(2,1)} reshape(bf16[672,384]{1,0:T(8,128)(2,1)} %bitcast.29) | data formatting | bytes 1032192 | tf_op jit(solution)/shard_map/reshape | solution.py:290
  25.8 2.0 %reshape.34 = bf16[16,42,384]{2,1,0:T(8,128)(2,1)} reshape(bf16[672,384]{1,0:T(8,128)(2,1)} %bitcast.30) | data formatting | bytes 1032192 | tf_op jit(solution)/shard_map/reshape | solution.py:289
  27.8 0.7 pad.11.clone
  28.6 7.9 %all-to-all-done = bf16[16,32,128]{2,1,0:T(8,128)(2,1)S(1)} async-done(((bf16[16,32,128]{2,1,0:T(8,128)(2,1)}), bf16[16,32,128]{2,1,0:T(8,128)(2,1)S(1)}, u32[]{:S(2)}, u32[]{:S(2)}) %all-to-all-start) | async-done | bytes 131104 | tf_op jit(solution)/shard_map/all_to_all | solution.py:20
  36.5 0.9 broadcast_in_dim.39
  37.3 4.8 %all-to-all-start.1 = ((bf16[4,512,128]{2,1,0:T(8,128)(2,1)}), bf16[4,512,128]{2,1,0:T(8,128)(2,1)}, u32[]{:S(2)}, u32[]{:S(2)}) async-start(bf16[4,512,128]{2,1,0:T(8,128)(2,1)} %broadcast_in_dim.39), calls=%async_computation.1 | async-start | bytes 1048576 | tf_op jit(solution)/shard_map/all_to_all | solution.py:20
  42.2 2.1 %maximum_maximum_fusion.w_ref = bf16[16,128,768]{2,1,0:T(8,128)(2,1)S(1)} fusion(bf16[16,42,384]{2,1,0:T(8,128)(2,1)} %reshape_squeeze.3, bf16[16,42,384]{2,1,0:T(8,128)(2,1)} %reshape.35, bf16[16,42,384]{2,1,0:T(8,128)(2,1)} %reshape.34, bf16[128,768]{1,0:T(8,128)(2,1)S(1)} %pad.13.clone, bf16[128,768]{1,0:T(8,128)(2,1)} %pad.11.clone, ...), kind=kLoop, calls=%fused_computation.3 | loop fusion | flops 18874368 | bytes 5283840 | tf_op jit(solution)/shard_map/concatenate | solution.py:297
  44.3 4.6 %all-to-all-done.1.pack_ref = bf16[4,512,128]{2,1,0:T(8,128)(2,1)} async-done(((bf16[4,512,128]{2,1,0:T(8,128)(2,1)}), bf16[4,512,128]{2,1,0:T(8,128)(2,1)}, u32[]{:S(2)}, u32[]{:S(2)}) %all-to-all-start.1) | async-done | bytes 524320 | tf_op jit(solution)/shard_map/all_to_all | solution.py:20
  48.9 2.4 %shard_map.111 = (bf16[8,336,128]{2,1,0:T(8,128)(2,1)S(1)}, bf16[336,768]{1,0:T(8,128)(2,1)S(1)}) custom-call(s32[1]{0:T(128)} %bitcast.4.half_ref, bf16[4,512,128]{2,1,0:T(8,128)(2,1)} %all-to-all-done.1.pack_ref, bf16[16,128,768]{2,1,0:T(8,128)(2,1)S(1)} %maximum_maximum_fusion.w_ref), custom_call_target="tpu_custom_call" | custom-call | flops 1056964608 | bytes 4874244 | tf_op jit(solution)/shard_map/pallas_call | solution.py:35
  51.3 0.0 copy-start.1
  51.3 1.9 %collective-permute-start = (bf16[8,336,128]{2,1,0:T(8,128)(2,1)S(1)}, bf16[8,336,128]{2,1,0:T(8,128)(2,1)S(1)}, u32[]{:S(2)}, u32[]{:S(2)}) collective-permute-start(bf16[8,336,128]{2,1,0:T(8,128)(2,1)S(1)} %get-tuple-element.35), channel_id=1, source_target_pairs={{0,1},{1,0},{2,3},{3,2},{4,5},{5,4},{6,7},{7,6},{8,9},{9,8},{10,11... | collective-permute-start | bytes 2064392 | tf_op jit(solution)/shard_map/ppermute | solution.py:329
  53.2 0.7 shard_map.112
  54.0 0.0 copy-done.1
  54.0 0.0 copy-start.7
  54.0 0.0 copy-start.8
  54.0 0.0 copy-start.9
  54.0 1.3 collective-permute-done
  55.3 1.1 add_convert_fusion
  56.4 7.1 %all-to-all-start.2 = ((bf16[8,336,128]{2,1,0:T(8,128)(2,1)}), bf16[8,336,128]{2,1,0:T(8,128)(2,1)S(1)}, u32[]{:S(2)}, u32[]{:S(2)}) async-start(bf16[8,336,128]{2,1,0:T(8,128)(2,1)} %add_convert_fusion), calls=%async_computation.2 | async-start | bytes 1376256 | tf_op jit(solution)/shard_map/all_to_all | solution.py:20
  63.5 0.0 copy-done.7
  63.6 0.0 copy-done.8
  63.6 0.0 copy-done.9
  63.6 3.7 %fusion.1.w_ref = bf16[16,128,768]{2,1,0:T(8,128)(2,1)} fusion(bf16[16,42,384]{2,1,0:T(8,128)(2,1)S(1)} %copy-done.7, bf16[16,42,384]{2,1,0:T(8,128)(2,1)S(1)} %copy-done.8, bf16[16,42,384]{2,1,0:T(8,128)(2,1)S(1)} %copy-done.9, bf16[128,768]{1,0:T(8,128)(2,1)S(1)} %pad.4.clone, bf16[128,768]{1,0:T(8,128)(2,1)S(1)} %pad.13.clone), kind=kLoop, calls=%fused_computation.2 | loop fusion | flops 18874368 | bytes 5087232 | tf_op jit(solution)/shard_map/concatenate | solution.py:322
  67.3 17.6 %all-to-all-done.2.sum_ref = bf16[8,336,128]{2,1,0:T(8,128)(2,1)S(1)} async-done(((bf16[8,336,128]{2,1,0:T(8,128)(2,1)}), bf16[8,336,128]{2,1,0:T(8,128)(2,1)S(1)}, u32[]{:S(2)}, u32[]{:S(2)}) %all-to-all-start.2) | async-done | bytes 688160 | tf_op jit(solution)/shard_map/all_to_all | solution.py:20
  84.8 0.3 shard_map.113
  85.2 0.8 broadcast_in_dim.43
  86.0 3.6 %all-to-all-start.3 = ((bf16[16,96,128]{2,1,0:T(8,128)(2,1)}), bf16[16,96,128]{2,1,0:T(8,128)(2,1)S(1)}, u32[]{:S(2)}, u32[]{:S(2)}) async-start(bf16[16,96,128]{2,1,0:T(8,128)(2,1)} %broadcast_in_dim.43), calls=%async_computation.3 | async-start | bytes 786432 | tf_op jit(solution)/shard_map/all_to_all | solution.py:20
  89.5 26.2 %all-gather = bf16[3840,128]{1,0:T(8,128)(2,1)S(1)} all-gather(bf16[240,128]{1,0:T(8,128)(2,1)S(1)} %slice.20), channel_id=2, replica_groups=mesh['expert'=16,'etp'=4,'dp'=16] {'dp'}, dimensions={0}, use_global_device_ids=true | all-gather | bytes 1044480 | tf_op jit(solution)/shard_map/all_gather | solution.py:342
  115.7 0.0 all-to-all-done.3.tail_ref
  115.7 0.0 copy-start
  115.7 1.9 %copy-done = bf16[16,128,768]{2,1,0:T(8,128)(2,1)S(1)} copy-done((bf16[16,128,768]{2,1,0:T(8,128)(2,1)S(1)}, bf16[16,128,768]{2,1,0:T(8,128)(2,1)}, u32[]{:S(2)}) %copy-start) | copy-done | bytes 3145752
  117.6 0.0 copy-start.2
  117.6 2.8 %shard_map.114 = bf16[4,512,128]{2,1,0:T(8,128)(2,1)S(1)} custom-call(bf16[16,240,128]{2,1,0:T(8,128)(2,1)S(1)} %bitcast.25, bf16[16,96,128]{2,1,0:T(8,128)(2,1)S(1)} %all-to-all-done.3.tail_ref, bf16[16,128,768]{2,1,0:T(8,128)(2,1)S(1)} %copy-done), custom_call_target="tpu_custom_call" | custom-call | flops 2113929216 | bytes 5046272 | tf_op jit(solution)/shard_map/pallas_call | solution.py:35
  120.5 12.7 %all_to_all.30 = bf16[4,512,128]{2,1,0:T(8,128)(2,1)S(1)} all-to-all(bf16[4,512,128]{2,1,0:T(8,128)(2,1)S(1)} %shard_map.114), channel_id=1, replica_groups=mesh['expert'=16,'etp'=4,'dp'=16] {'etp'}, dimensions={0} | all-to-all | bytes 1048576 | tf_op jit(solution)/shard_map/all_to_all | solution.py:20
  133.1 0.7 reduce_sum.12
  133.9 5.1 %all-to-all-start.5 = ((bf16[16,32,128]{2,1,0:T(8,128)(2,1)}), bf16[16,32,128]{2,1,0:T(8,128)(2,1)S(1)}, u32[]{:S(2)}, u32[]{:S(2)}) async-start(bf16[16,32,128]{2,1,0:T(8,128)(2,1)} %bitcast.12), calls=%async_computation.5 | async-start | bytes 262144 | tf_op jit(solution)/shard_map/all_to_all | solution.py:20
  138.9 0.0 copy-done.2
  138.9 1.8 %convolution_convert_fusion = bf16[16,128,768]{2,1,0:T(8,128)(2,1)S(1)} fusion(bf16[16,96,128]{2,1,0:T(8,128)(2,1)S(1)} %all-to-all-done.3.tail_ref, bf16[16,240,128]{2,1,0:T(8,128)(2,1)S(1)} %bitcast.26, bf16[336,768]{1,0:T(8,128)(2,1)S(1)} %copy-done.2), kind=kOutput, calls=%fused_computation.4 | convolution fusion | flops 1061289984 | bytes 5038080 | tf_op jit(solution)/shard_map/dot_general | solution.py:16
  140.8 0.0 copy-start.3
  140.8 0.0 copy-start.4
  140.8 0.0 copy-start.5
  140.8 0.0 copy-start.6
  140.8 0.5 fusion.7
  141.3 0.9 reshape.38
  142.2 0.9 reshape.39
  143.2 0.9 broadcast_in_dim_reshape.3
  144.1 8.9 %all-to-all-done.5 = bf16[16,32,128]{2,1,0:T(8,128)(2,1)S(1)} async-done(((bf16[16,32,128]{2,1,0:T(8,128)(2,1)}), bf16[16,32,128]{2,1,0:T(8,128)(2,1)S(1)}, u32[]{:S(2)}, u32[]{:S(2)}) %all-to-all-start.5) | async-done | bytes 131104 | tf_op jit(solution)/shard_map/all_to_all | solution.py:20
  153.0 0.0 copy-done.3
  153.0 0.0 copy-done.4
  153.0 0.0 copy-done.5
  153.0 0.0 copy-done.6
  153.0 1.2 shard_map.115
  (9 shorter events, 0.1 us)
Async XLA Ops:
  2.9 33.6 %all-to-all-start = ((bf16[16,32,128]{2,1,0:T(8,128)(2,1)}), bf16[16,32,128]{2,1,0:T(8,128)(2,1)S(1)}, u32[]{:S(2)}, u32[]{:S(2)}) async-start(bf16[16,32,128]{2,1,0:T(8,128)(2,1)} %bitcast.33), calls=%async_computation | async-start | bytes 262144 | tf_op jit(solution)/shard_map/all_to_all | solution.py:20
  37.3 11.6 %all-to-all-start.1 = ((bf16[4,512,128]{2,1,0:T(8,128)(2,1)}), bf16[4,512,128]{2,1,0:T(8,128)(2,1)}, u32[]{:S(2)}, u32[]{:S(2)}) async-start(bf16[4,512,128]{2,1,0:T(8,128)(2,1)} %broadcast_in_dim.39), calls=%async_computation.1 | async-start | bytes 1048576 | tf_op jit(solution)/shard_map/all_to_all | solution.py:20
  51.3 2.7 %copy-start.1 = (bf16[336,768]{1,0:T(8,128)(2,1)}, bf16[336,768]{1,0:T(8,128)(2,1)S(1)}, u32[]{:S(2)}) copy-start(bf16[336,768]{1,0:T(8,128)(2,1)S(1)} %get-tuple-element.33.xg_ref) | copy-start | bytes 1548292
  51.3 4.0 %collective-permute-start = (bf16[8,336,128]{2,1,0:T(8,128)(2,1)S(1)}, bf16[8,336,128]{2,1,0:T(8,128)(2,1)S(1)}, u32[]{:S(2)}, u32[]{:S(2)}) collective-permute-start(bf16[8,336,128]{2,1,0:T(8,128)(2,1)S(1)} %get-tuple-element.35), channel_id=1, source_target_pairs={{0,1},{1,0},{2,3},{3,2},{4,5},{5,4},{6,7},{7,6},{8,9},{9,8},{10,11... | collective-permute-start | bytes 2064392 | tf_op jit(solution)/shard_map/ppermute | solution.py:329
  54.0 9.6 %copy-start.7 = (bf16[16,42,384]{2,1,0:T(8,128)(2,1)S(1)}, bf16[16,42,384]{2,1,0:T(8,128)(2,1)}, u32[]{:S(2)}) copy-start(bf16[16,42,384]{2,1,0:T(8,128)(2,1)} %reshape_squeeze.3) | copy-start | bytes 1548292
  54.0 9.6 %copy-start.8 = (bf16[16,42,384]{2,1,0:T(8,128)(2,1)S(1)}, bf16[16,42,384]{2,1,0:T(8,128)(2,1)}, u32[]{:S(2)}) copy-start(bf16[16,42,384]{2,1,0:T(8,128)(2,1)} %reshape.35) | copy-start | bytes 1548292
  54.0 9.6 %copy-start.9 = (bf16[16,42,384]{2,1,0:T(8,128)(2,1)S(1)}, bf16[16,42,384]{2,1,0:T(8,128)(2,1)}, u32[]{:S(2)}) copy-start(bf16[16,42,384]{2,1,0:T(8,128)(2,1)} %reshape.34) | copy-start | bytes 1548292
  56.4 28.4 %all-to-all-start.2 = ((bf16[8,336,128]{2,1,0:T(8,128)(2,1)}), bf16[8,336,128]{2,1,0:T(8,128)(2,1)S(1)}, u32[]{:S(2)}, u32[]{:S(2)}) async-start(bf16[8,336,128]{2,1,0:T(8,128)(2,1)} %add_convert_fusion), calls=%async_computation.2 | async-start | bytes 1376256 | tf_op jit(solution)/shard_map/all_to_all | solution.py:20
  86.0 29.8 %all-to-all-start.3 = ((bf16[16,96,128]{2,1,0:T(8,128)(2,1)}), bf16[16,96,128]{2,1,0:T(8,128)(2,1)S(1)}, u32[]{:S(2)}, u32[]{:S(2)}) async-start(bf16[16,96,128]{2,1,0:T(8,128)(2,1)} %broadcast_in_dim.43), calls=%async_computation.3 | async-start | bytes 786432 | tf_op jit(solution)/shard_map/all_to_all | solution.py:20
  115.7 1.9 %copy-start = (bf16[16,128,768]{2,1,0:T(8,128)(2,1)S(1)}, bf16[16,128,768]{2,1,0:T(8,128)(2,1)}, u32[]{:S(2)}) copy-start(bf16[16,128,768]{2,1,0:T(8,128)(2,1)} %fusion.1.w_ref) | copy-start | bytes 9437188
  117.6 21.3 %copy-start.2 = (bf16[336,768]{1,0:T(8,128)(2,1)S(1)}, bf16[336,768]{1,0:T(8,128)(2,1)}, u32[]{:S(2)}) copy-start(bf16[336,768]{1,0:T(8,128)(2,1)} %copy-done.1) | copy-start | bytes 1548292
  133.9 19.1 %all-to-all-start.5 = ((bf16[16,32,128]{2,1,0:T(8,128)(2,1)}), bf16[16,32,128]{2,1,0:T(8,128)(2,1)S(1)}, u32[]{:S(2)}, u32[]{:S(2)}) async-start(bf16[16,32,128]{2,1,0:T(8,128)(2,1)} %bitcast.12), calls=%async_computation.5 | async-start | bytes 262144 | tf_op jit(solution)/shard_map/all_to_all | solution.py:20
  140.8 12.2 %copy-start.3 = (f32[512,64]{1,0:T(8,128)S(1)}, f32[512,64]{1,0:T(8,128)}, u32[]{:S(2)}) copy-start(f32[512,64]{1,0:T(8,128)} %get-tuple-element.24.weight_ref) | copy-start | bytes 393220
  140.8 12.2 %copy-start.4 = (bf16[512,64]{1,0:T(8,128)(2,1)S(1)}, bf16[512,64]{1,0:T(8,128)(2,1)}, u32[]{:S(2)}) copy-start(bf16[512,64]{1,0:T(8,128)(2,1)} %get-tuple-element.25.place_ref) | copy-start | bytes 196612
  140.8 12.2 %copy-start.5 = (bf16[512,64]{1,0:T(8,128)(2,1)S(1)}, bf16[512,64]{1,0:T(8,128)(2,1)}, u32[]{:S(2)}) copy-start(bf16[512,64]{1,0:T(8,128)(2,1)} %get-tuple-element.26.place_b_ref) | copy-start | bytes 196612
  140.8 12.2 %copy-start.6 = (bf16[512,64]{1,0:T(8,128)(2,1)S(1)}, bf16[512,64]{1,0:T(8,128)(2,1)}, u32[]{:S(2)}) copy-start(bf16[512,64]{1,0:T(8,128)(2,1)} %get-tuple-element.27.place_c_ref) | copy-start | bytes 196612

commit v5 on v4

--- a/solution.py
+++ b/solution.py
@@ -172,7 +172,7 @@
     partials(half_ref, xg_ref[...], w_ref, part_ref)
 
 
-def act_kernel(unit, sum_ref, act_ref):
+def act_kernel(unit, sum_ref, head_ref, tail_ref):
     total = sum_ref[0].astype(f32)
     for j in range(1, sum_ref.shape[0]):
         total = total + sum_ref[j].astype(f32)
@@ -184,9 +184,12 @@
     hidden = gate * sig * up
     d_gate = d_hidden * up * sig * (1.0 + gate * (1.0 - sig))
     d_up = d_hidden * gate * sig
-    act_ref[...] = (
-        hidden + pltpu.roll(d_gate, unit, 1) + pltpu.roll(d_up, 2 * unit, 1)
-    ).astype(bf16)
+    act = d_gate + pltpu.roll(d_up, unit, 1) + pltpu.roll(hidden, 2 * unit, 1)
+    act = act.astype(bf16)
+    n_head = head_ref.shape[0]
+    head_ref[...] = act[:n_head]
+    for j in range(tail_ref.shape[0]):
+        tail_ref[j] = act[n_head:]
 
 
 def back_kernel(piece, head_ref, tail_ref, w_ref, pack_ref):
@@ -206,8 +209,8 @@
     low = is_low(slots, 64)
     parts_a, parts_b = [], []
     for i in range(n_etp):
-        parts_a.append(total[:, piece * i : piece * (i + 1)])
-        at = width + piece * i
+        at = piece * i
+        parts_a.append(total[:, width + at : width + at + piece])
         parts_a.append(total[:, at : at + LANES - piece])
         tail = total[:, at + LANES - piece : at + piece]
         parts_b.append(jnp.where(low, tail, 0.0))
@@ -303,6 +306,7 @@
     )
 
     got = swap(send.reshape(n_exp, PACK, LANES), "expert").reshape(1, rows, LANES)
+    got, w_front = lax.optimization_barrier((got, w_front))
     packs = swap(jnp.broadcast_to(got, (n_etp, rows, LANES)), "etp")
 
     half_flops = 2 * slots * 2 * width * n_y * LANES
@@ -316,30 +320,18 @@
         packs,
         w_front,
     )
-    part_theirs, w_gate, w_up, w_down = lax.optimization_barrier(
-        (part_theirs, w_gate, w_up, w_down)
-    )
-    w_back = jnp.concatenate(
-        [
-            jnp.concatenate([w_down, zeros(2 * unit + spare)], axis=1),
-            jnp.concatenate([zeros(unit), w_gate, w_up, zeros(spare)], axis=1),
-        ],
-        axis=2,
-    )
     arrived = lax.ppermute(part_theirs, "dp", other_core)
     (part_mine,) = call(second_kernel, [part_shape], half_flops, 1, mine, xg, w_front)
     chip = (part_mine.astype(f32) + arrived.astype(f32)).astype(bf16)
-    sums, w_back = lax.optimization_barrier((swap(chip, "dp", same_core), w_back))
-    (act,) = call(
+    head, tail = call(
         functools.partial(act_kernel, unit),
-        [((slots, LANES), bf16)],
+        [((HEAD, LANES), bf16), ((n_dp, slots - HEAD, LANES), bf16)],
         10_000_000,
         0,
-        sums,
-    )
-    tail = jnp.broadcast_to(act[HEAD:], (n_dp, slots - HEAD, LANES))
+        swap(chip, "dp", same_core),
+    )
     tail = swap(tail, "dp")
-    head = lax.all_gather(act[:HEAD], "dp", axis=0)
+    head = lax.all_gather(head, "dp", axis=0)
     (out,) = call(
         functools.partial(back_kernel, piece),
         [((n_etp, rows, LANES), bf16)],
@@ -347,7 +339,7 @@
         0,
         head,
         tail,
-        w_back,
+        w_front,
     )
     out = jnp.sum(swap(out, "etp").astype(f32), axis=0).astype(bf16)
     back = swap(out.reshape(n_exp, PACK, LANES), "expert").reshape(rows, LANES)
@@ -358,9 +350,9 @@
     def take(start, at):
         return grads[:, start : start + unit, at : at + width].reshape(hid, width)
 
-    down_grad = take(0, width)
-    gate_grad = take(unit, 0).T
-    up_grad = take(2 * unit, 0).T
+    gate_grad = take(0, 0).T
+    up_grad = take(unit, 0).T
+    down_grad = take(2 * unit, width)
     layer_output, tokens_grad = call(
         functools.partial(combine_kernel, piece),
         [((block_len, piece), bf16), ((block_len, piece), bf16)],

time: 155 us -> 156 us (level)
  blocking collectives: 38.9 us -> 68.5 us
  waiting for transfers between devices: 40.3 us -> 22.1 us
  starting transfers between devices: 41.3 us -> 35.7 us
  other arithmetic: 7.61 us -> 3.03 us
    all_to_all x1 -> x2, blocking collectives: 12.7 us -> 40.9 us  [swap(): lax.all_to_all(x, axis, split_axis=0, concat_axis=0, tiled=True, axis_ind...]
    all_to_all x5 -> x4, waiting for transfers between devices: 39 us -> 20.8 us  [swap(): lax.all_to_all(x, axis, split_axis=0, concat_axis=0, tiled=True, axis_ind...]
    all_to_all x5 -> x4, starting transfers between devices: 39.4 us -> 33.7 us  [swap(): lax.all_to_all(x, axis, split_axis=0, concat_axis=0, tiled=True, axis_ind...]
    concatenate x1 -> x0, other arithmetic: 3.68 us -> none  [local(): jnp.concatenate([jnp.concatenate([w_down, zeros(2 * unit + spare)], axis=...]
  transfers between devices with their start and end apart: 6 -> 5, of which waited for: 5 -> 4; matrix products, arithmetic and copies ran while one was open for 11% -> 9% of each run, Pallas kernels for 0% -> 0%
where the time goes in v5:
time: 156 us; the launch traced here: 155 us
  blocking collectives  68.5 us (44%)
  starting transfers between devices  35.7 us (23%)
  waiting for transfers between devices  22.1 us (14%)
  local copies, waits for them, and re-layouts  12.8 us (8%)
  Pallas kernels  9.29 us (6%)
  matrix products  3.17 us (2%)
  other arithmetic  3.03 us (2%)
    all_to_all x2, blocking collectives, swap(): lax.all_to_all(x, axis, split_axis=0, concat_axis=0, tiled=True, axis_ind...  40.9 us
    all_to_all x4, starting transfers between devices, swap(): lax.all_to_all(x, axis, split_axis=0, concat_axis=0, tiled=True, axis_ind...  33.7 us
    all_gather x1, blocking collectives, local(): head = lax.all_gather(head, 'dp', axis=0)  27.6 us
    all_to_all x4, waiting for transfers between devices, swap(): lax.all_to_all(x, axis, split_axis=0, concat_axis=0, tiled=True, axis_ind...  20.8 us
    pallas_call x6, Pallas kernels, call(): pl.pallas_call(kernel, out_shape=outs, in_specs=[smem] * n_scalar + [held...  9.29 us
    dot_general x1, matrix products, mm(): lax.dot_general(left, right, (dims, ((), ())), preferred_element_type=f32)  3.17 us
  transfers between devices with their start and end apart: 5, of which 4 were waited for; matrix products, arithmetic and copies ran while one was open for 9% of the time, Pallas kernels for 0%

profile of v5, /device:TPU:2, one launch (start us, length us, event | category | flops | bytes accessed | tf_op | source)
XLA Modules:
  0.0 155.5 jit_solution(12566057159725330730)
XLA Ops:
  0.6 2.2 %shard_map.110 = (bf16[512,128]{1,0:T(8,128)(2,1)}, bf16[512,64]{1,0:T(8,128)(2,1)}, bf16[512,64]{1,0:T(8,128)(2,1)}, bf16[512,64]{1,0:T(8,128)(2,1)}, f32[512,64]{1,0:T(8,128)}) custom-call(s32[1]{0:T(128)} %bitcast.col_ref, bf16[64,384]{1,0:T(8,128)(2,1)} %tok_hbm.1, bf16[64,384]{1,0:T(8,128)(2,1)} %cot_hbm.1, s32[4,64]{1,0:T(4,128)} %bitcast.35, ...), custom_call_target="tpu_custom_call" | custom-call | flops 60000000 | bytes 559108 | tf_op jit(solution)/shard_map/pallas_call | solution.py:35
  2.9 18.9 %all-to-all-start = ((bf16[16,32,128]{2,1,0:T(8,128)(2,1)}), bf16[16,32,128]{2,1,0:T(8,128)(2,1)S(1)}, u32[]{:S(2)}, u32[]{:S(2)}) async-start(bf16[16,32,128]{2,1,0:T(8,128)(2,1)} %bitcast.34), calls=%async_computation | async-start | bytes 262144 | tf_op jit(solution)/shard_map/all_to_all | solution.py:20
  21.8 2.0 %reshape_squeeze.3 = bf16[16,42,384]{2,1,0:T(8,128)(2,1)} reshape(bf16[1,672,384]{2,1,0:T(8,128)(2,1)} %param.12) | data formatting | bytes 1032192 | tf_op jit(solution)/shard_map/reshape;squeeze | solution.py:294
  23.8 2.0 %reshape.37 = bf16[16,42,384]{2,1,0:T(8,128)(2,1)} reshape(bf16[672,384]{1,0:T(8,128)(2,1)} %bitcast.30) | data formatting | bytes 1032192 | tf_op jit(solution)/shard_map/reshape | solution.py:293
  25.8 2.0 %reshape.36 = bf16[16,42,384]{2,1,0:T(8,128)(2,1)} reshape(bf16[672,384]{1,0:T(8,128)(2,1)} %bitcast.31) | data formatting | bytes 1032192 | tf_op jit(solution)/shard_map/reshape | solution.py:292
  27.9 2.1 %maximum_maximum_fusion.w_ref = bf16[16,128,768]{2,1,0:T(8,128)(2,1)S(1)} fusion(bf16[16,42,384]{2,1,0:T(8,128)(2,1)} %reshape_squeeze.3, bf16[16,42,384]{2,1,0:T(8,128)(2,1)} %reshape.37, bf16[16,42,384]{2,1,0:T(8,128)(2,1)} %reshape.36, bf16[128,768]{1,0:T(8,128)(2,1)S(1)} %pad.7.clone, bf16[128,768]{1,0:T(8,128)(2,1)S(1)} %pad.5.clone, ...), kind=kLoop, calls=%fused_computation | loop fusion | flops 18874368 | bytes 5283840 | tf_op jit(solution)/shard_map/concatenate | solution.py:300
  30.0 6.5 %all-to-all-done = bf16[16,32,128]{2,1,0:T(8,128)(2,1)S(1)} async-done(((bf16[16,32,128]{2,1,0:T(8,128)(2,1)}), bf16[16,32,128]{2,1,0:T(8,128)(2,1)S(1)}, u32[]{:S(2)}, u32[]{:S(2)}) %all-to-all-start) | async-done | bytes 131104 | tf_op jit(solution)/shard_map/all_to_all | solution.py:20
  36.5 0.9 broadcast_in_dim.38
  37.3 4.8 %all-to-all-start.1 = ((bf16[4,512,128]{2,1,0:T(8,128)(2,1)}), bf16[4,512,128]{2,1,0:T(8,128)(2,1)}, u32[]{:S(2)}, u32[]{:S(2)}) async-start(bf16[4,512,128]{2,1,0:T(8,128)(2,1)} %broadcast_in_dim.38), calls=%async_computation.1 | async-start | bytes 1048576 | tf_op jit(solution)/shard_map/all_to_all | solution.py:20
  42.2 6.7 %all-to-all-done.1.pack_ref = bf16[4,512,128]{2,1,0:T(8,128)(2,1)} async-done(((bf16[4,512,128]{2,1,0:T(8,128)(2,1)}), bf16[4,512,128]{2,1,0:T(8,128)(2,1)}, u32[]{:S(2)}, u32[]{:S(2)}) %all-to-all-start.1) | async-done | bytes 524320 | tf_op jit(solution)/shard_map/all_to_all | solution.py:20
  48.9 2.4 %shard_map.111 = (bf16[8,336,128]{2,1,0:T(8,128)(2,1)S(1)}, bf16[336,768]{1,0:T(8,128)(2,1)S(1)}) custom-call(s32[1]{0:T(128)} %bitcast.4.half_ref, bf16[4,512,128]{2,1,0:T(8,128)(2,1)} %all-to-all-done.1.pack_ref, bf16[16,128,768]{2,1,0:T(8,128)(2,1)S(1)} %maximum_maximum_fusion.w_ref), custom_call_target="tpu_custom_call" | custom-call | flops 1056964608 | bytes 4874244 | tf_op jit(solution)/shard_map/pallas_call | solution.py:35
  51.3 0.0 copy-start.1
  51.3 1.9 %collective-permute-start = (bf16[8,336,128]{2,1,0:T(8,128)(2,1)S(1)}, bf16[8,336,128]{2,1,0:T(8,128)(2,1)S(1)}, u32[]{:S(2)}, u32[]{:S(2)}) collective-permute-start(bf16[8,336,128]{2,1,0:T(8,128)(2,1)S(1)} %get-tuple-element.34), channel_id=1, source_target_pairs={{0,1},{1,0},{2,3},{3,2},{4,5},{5,4},{6,7},{7,6},{8,9},{9,8},{10,11... | collective-permute-start | bytes 2064392 | tf_op jit(solution)/shard_map/ppermute | solution.py:323
  53.2 0.7 shard_map.112
  54.0 1.4 collective-permute-done
  55.3 0.2 add_convert_fusion
  55.6 0.0 copy-done.1
  55.6 28.2 %all_to_all.30.sum_ref = bf16[8,336,128]{2,1,0:T(8,128)(2,1)S(1)} all-to-all(bf16[8,336,128]{2,1,0:T(8,128)(2,1)S(1)} %add_convert_fusion), channel_id=1, replica_groups={{0,2,4,6,8,10,12,14},{1,3,5,7,9,11,13,15},{16,18,20,22,24,26,28,30},{17..., dimensions={0} | all-to-all | bytes 1376256 | tf_op jit(solution)/shard_map/all_to_all | solution.py:20
  83.8 0.3 shard_map.113
  84.1 0.0 copy-start.2
  84.1 0.7 copy-done.2
  84.9 0.0 copy-start.7
  84.9 0.6 copy-done.7
  85.5 3.6 %all-to-all-start.3 = ((bf16[16,96,128]{2,1,0:T(8,128)(2,1)}), bf16[16,96,128]{2,1,0:T(8,128)(2,1)S(1)}, u32[]{:S(2)}, u32[]{:S(2)}) async-start(bf16[16,96,128]{2,1,0:T(8,128)(2,1)} %copy-done.2), calls=%async_computation.3 | async-start | bytes 786432 | tf_op jit(solution)/shard_map/all_to_all | solution.py:20
  89.1 27.6 %all-gather = bf16[3840,128]{1,0:T(8,128)(2,1)} all-gather(bf16[240,128]{1,0:T(8,128)(2,1)} %copy-done.7), channel_id=2, replica_groups=mesh['expert'=16,'etp'=4,'dp'=16] {'dp'}, dimensions={0}, use_global_device_ids=true | all-gather | bytes 1044480 | tf_op jit(solution)/shard_map/all_gather | solution.py:334
  116.7 0.0 all-to-all-done.3.tail_ref
  116.7 0.0 copy-start
  116.7 1.2 copy-done
  117.9 2.4 %shard_map.114 = bf16[4,512,128]{2,1,0:T(8,128)(2,1)S(1)} custom-call(bf16[16,240,128]{2,1,0:T(8,128)(2,1)S(1)} %bitcast.27, bf16[16,96,128]{2,1,0:T(8,128)(2,1)S(1)} %all-to-all-done.3.tail_ref, bf16[16,128,768]{2,1,0:T(8,128)(2,1)S(1)} %maximum_maximum_fusion.w_ref), custom_call_target="tpu_custom_call" | custom-call | flops 2113929216 | bytes 5046272 | tf_op jit(solution)/shard_map/pallas_call | solution.py:35
  120.3 12.7 %all_to_all.31 = bf16[4,512,128]{2,1,0:T(8,128)(2,1)S(1)} all-to-all(bf16[4,512,128]{2,1,0:T(8,128)(2,1)S(1)} %shard_map.114), channel_id=1, replica_groups=mesh['expert'=16,'etp'=4,'dp'=16] {'etp'}, dimensions={0} | all-to-all | bytes 1048576 | tf_op jit(solution)/shard_map/all_to_all | solution.py:20
  132.9 0.7 reduce_sum.12
  133.7 6.5 %all-to-all-start.5 = ((bf16[16,32,128]{2,1,0:T(8,128)(2,1)}), bf16[16,32,128]{2,1,0:T(8,128)(2,1)S(1)}, u32[]{:S(2)}, u32[]{:S(2)}) async-start(bf16[16,32,128]{2,1,0:T(8,128)(2,1)} %bitcast.13), calls=%async_computation.5 | async-start | bytes 262144 | tf_op jit(solution)/shard_map/all_to_all | solution.py:20
  140.2 3.2 %convolution_convert_fusion = bf16[16,128,768]{2,1,0:T(8,128)(2,1)S(1)} fusion(bf16[16,96,128]{2,1,0:T(8,128)(2,1)S(1)} %all-to-all-done.3.tail_ref, bf16[16,240,128]{2,1,0:T(8,128)(2,1)} %bitcast.26, bf16[336,768]{1,0:T(8,128)(2,1)} %copy-done.1), kind=kOutput, calls=%fused_computation.1 | convolution fusion | flops 1061289984 | bytes 5038080 | tf_op jit(solution)/shard_map/dot_general | solution.py:16
  143.3 0.0 copy-start.3
  143.4 0.0 copy-start.4
  143.4 0.0 copy-start.5
  143.4 0.0 copy-start.6
  143.4 0.5 fusion.5
  143.9 0.9 reshape.40
  144.8 0.9 reshape.41
  145.7 0.9 broadcast_in_dim_reshape.3
  146.7 7.6 %all-to-all-done.5 = bf16[16,32,128]{2,1,0:T(8,128)(2,1)S(1)} async-done(((bf16[16,32,128]{2,1,0:T(8,128)(2,1)}), bf16[16,32,128]{2,1,0:T(8,128)(2,1)S(1)}, u32[]{:S(2)}, u32[]{:S(2)}) %all-to-all-start.5) | async-done | bytes 131104 | tf_op jit(solution)/shard_map/all_to_all | solution.py:20
  154.2 0.0 copy-done.3
  154.3 0.0 copy-done.4
  154.3 0.0 copy-done.5
  154.3 0.0 copy-done.6
  154.3 1.2 shard_map.115
  (6 shorter events, 0.1 us)
Async XLA Ops:
  2.9 33.6 %all-to-all-start = ((bf16[16,32,128]{2,1,0:T(8,128)(2,1)}), bf16[16,32,128]{2,1,0:T(8,128)(2,1)S(1)}, u32[]{:S(2)}, u32[]{:S(2)}) async-start(bf16[16,32,128]{2,1,0:T(8,128)(2,1)} %bitcast.34), calls=%async_computation | async-start | bytes 262144 | tf_op jit(solution)/shard_map/all_to_all | solution.py:20
  37.3 11.6 %all-to-all-start.1 = ((bf16[4,512,128]{2,1,0:T(8,128)(2,1)}), bf16[4,512,128]{2,1,0:T(8,128)(2,1)}, u32[]{:S(2)}, u32[]{:S(2)}) async-start(bf16[4,512,128]{2,1,0:T(8,128)(2,1)} %broadcast_in_dim.38), calls=%async_computation.1 | async-start | bytes 1048576 | tf_op jit(solution)/shard_map/all_to_all | solution.py:20
  51.3 4.3 %copy-start.1 = (bf16[336,768]{1,0:T(8,128)(2,1)}, bf16[336,768]{1,0:T(8,128)(2,1)S(1)}, u32[]{:S(2)}) copy-start(bf16[336,768]{1,0:T(8,128)(2,1)S(1)} %get-tuple-element.33.xg_ref) | copy-start | bytes 1548292
  51.3 4.0 %collective-permute-start = (bf16[8,336,128]{2,1,0:T(8,128)(2,1)S(1)}, bf16[8,336,128]{2,1,0:T(8,128)(2,1)S(1)}, u32[]{:S(2)}, u32[]{:S(2)}) collective-permute-start(bf16[8,336,128]{2,1,0:T(8,128)(2,1)S(1)} %get-tuple-element.34), channel_id=1, source_target_pairs={{0,1},{1,0},{2,3},{3,2},{4,5},{5,4},{6,7},{7,6},{8,9},{9,8},{10,11... | collective-permute-start | bytes 2064392 | tf_op jit(solution)/shard_map/ppermute | solution.py:323
  84.1 0.7 copy-start.2
  84.9 0.6 copy-start.7
  85.5 31.2 %all-to-all-start.3 = ((bf16[16,96,128]{2,1,0:T(8,128)(2,1)}), bf16[16,96,128]{2,1,0:T(8,128)(2,1)S(1)}, u32[]{:S(2)}, u32[]{:S(2)}) async-start(bf16[16,96,128]{2,1,0:T(8,128)(2,1)} %copy-done.2), calls=%async_computation.3 | async-start | bytes 786432 | tf_op jit(solution)/shard_map/all_to_all | solution.py:20
  116.7 1.2 copy-start
  133.7 20.6 %all-to-all-start.5 = ((bf16[16,32,128]{2,1,0:T(8,128)(2,1)}), bf16[16,32,128]{2,1,0:T(8,128)(2,1)S(1)}, u32[]{:S(2)}, u32[]{:S(2)}) async-start(bf16[16,32,128]{2,1,0:T(8,128)(2,1)} %bitcast.13), calls=%async_computation.5 | async-start | bytes 262144 | tf_op jit(solution)/shard_map/all_to_all | solution.py:20
  143.3 10.9 %copy-start.3 = (f32[512,64]{1,0:T(8,128)S(1)}, f32[512,64]{1,0:T(8,128)}, u32[]{:S(2)}) copy-start(f32[512,64]{1,0:T(8,128)} %get-tuple-element.22.weight_ref) | copy-start | bytes 393220
  143.4 10.9 %copy-start.4 = (bf16[512,64]{1,0:T(8,128)(2,1)S(1)}, bf16[512,64]{1,0:T(8,128)(2,1)}, u32[]{:S(2)}) copy-start(bf16[512,64]{1,0:T(8,128)(2,1)} %get-tuple-element.23.place_ref) | copy-start | bytes 196612
  143.4 10.9 %copy-start.5 = (bf16[512,64]{1,0:T(8,128)(2,1)S(1)}, bf16[512,64]{1,0:T(8,128)(2,1)}, u32[]{:S(2)}) copy-start(bf16[512,64]{1,0:T(8,128)(2,1)} %get-tuple-element.24.place_b_ref) | copy-start | bytes 196612
  143.4 10.9 %copy-start.6 = (bf16[512,64]{1,0:T(8,128)(2,1)S(1)}, bf16[512,64]{1,0:T(8,128)(2,1)}, u32[]{:S(2)}) copy-start(bf16[512,64]{1,0:T(8,128)(2,1)} %get-tuple-element.25.place_c_ref) | copy-start | bytes 196612

commit v6 on v5

--- a/solution.py
+++ b/solution.py
@@ -139,17 +139,21 @@
     return rank < FOLD
 
 
-def partials(half_ref, xg, w_ref, part_ref):
+def partials(split, half_ref, xg, w_ref, part_ref):
     chunks = part_ref.shape[0]
+    width = w_ref.shape[2]
+    from_x = (iota((xg.shape[0], 2 * LANES), 1) & (LANES - 1)) < split
     for j in range(0, chunks, 2):
         at = half_ref[0] + 2 * j
         w = jnp.concatenate([w_ref[at], w_ref[at + 2]], axis=0)
-        got = mm(xg, w, ((1,), (1,))).astype(bf16)
+        by_x = mm(xg[:, :width], w, ((1,), (1,)))
+        by_g = mm(xg[:, width:], w, ((1,), (1,)))
+        got = jnp.where(from_x, by_x, by_g).astype(bf16)
         part_ref[j] = got[:, :LANES]
         part_ref[j + 1] = got[:, LANES:]
 
 
-def first_kernel(piece, half_ref, pack_ref, w_ref, part_ref, xg_ref):
+def first_kernel(piece, split, half_ref, pack_ref, w_ref, part_ref, xg_ref):
     n_etp, rows, _ = pack_ref.shape
     slots = part_ref.shape[1]
     sel_a, sel_b = selectors(slots, rows, False)
@@ -165,11 +169,11 @@
         parts_g.append(jnp.where(low, b[:, at : at + 64], b[:, at + 64 : at + LANES]))
     xg = jnp.concatenate(parts_x + parts_g, axis=1).astype(bf16)
     xg_ref[...] = xg
-    partials(half_ref, xg, w_ref, part_ref)
-
-
-def second_kernel(half_ref, xg_ref, w_ref, part_ref):
-    partials(half_ref, xg_ref[...], w_ref, part_ref)
+    partials(split, half_ref, xg, w_ref, part_ref)
+
+
+def second_kernel(split, half_ref, xg_ref, w_ref, part_ref):
+    partials(split, half_ref, xg_ref[...], w_ref, part_ref)
 
 
 def act_kernel(unit, sum_ref, head_ref, tail_ref):
@@ -192,27 +196,34 @@
         tail_ref[j] = act[n_head:]
 
 
-def back_kernel(piece, head_ref, tail_ref, w_ref, pack_ref):
+def back_kernel(piece, split, head_ref, tail_ref, w_ref, pack_ref):
     chunks, slots = head_ref.shape[0], head_ref.shape[1] + tail_ref.shape[1]
     n_etp, rows, _ = pack_ref.shape
-    width = w_ref.shape[2] // 2
-    act = jnp.concatenate(
-        [
-            jnp.concatenate([ref[j] for j in range(chunks)], axis=1)
-            for ref in (head_ref, tail_ref)
-        ],
-        axis=0,
-    )
-    total = mm(act, w_ref[...].reshape(chunks * LANES, 2 * width), ((1,), (0,)))
-    total = total.astype(bf16).astype(f32)
+    width = w_ref.shape[2]
+    w = w_ref[...].reshape(chunks * LANES, width)
+    first = iota((1, LANES), 1) < split
+
+    def product(keep):
+        keep = jnp.where(keep, 1.0, 0.0).astype(bf16)
+        act = jnp.concatenate(
+            [
+                jnp.concatenate([ref[j] * keep for j in range(chunks)], axis=1)
+                for ref in (head_ref, tail_ref)
+            ],
+            axis=0,
+        )
+        return mm(act, w, ((1,), (0,))).astype(bf16).astype(f32)
+
+    dx = product(first)
+    y = product(jnp.logical_not(first))
     sel_a, sel_b = selectors(slots, rows, True)
     low = is_low(slots, 64)
     parts_a, parts_b = [], []
     for i in range(n_etp):
         at = piece * i
-        parts_a.append(total[:, width + at : width + at + piece])
-        parts_a.append(total[:, at : at + LANES - piece])
-        tail = total[:, at + LANES - piece : at + piece]
+        parts_a.append(y[:, at : at + piece])
+        parts_a.append(dx[:, at : at + LANES - piece])
+        tail = dx[:, at + LANES - piece : at + piece]
         parts_b.append(jnp.where(low, tail, 0.0))
         parts_b.append(jnp.where(low, 0.0, tail))
     a = jnp.concatenate(parts_a, axis=1).astype(bf16)
@@ -294,15 +305,8 @@
     w_down = down_weight[0].reshape(n_dp, unit, width)
     spare = LANES - 3 * unit
 
-    def zeros(n):
-        return jnp.zeros((n_dp, n, width), bf16)
-
     w_front = jnp.concatenate(
-        [
-            jnp.concatenate([w_gate, w_up, zeros(unit + spare)], axis=1),
-            jnp.concatenate([zeros(2 * unit), w_down, zeros(spare)], axis=1),
-        ],
-        axis=2,
+        [w_gate, w_up, w_down, jnp.zeros((n_dp, spare, width), bf16)], axis=1
     )
 
     got = swap(send.reshape(n_exp, PACK, LANES), "expert").reshape(1, rows, LANES)
@@ -312,7 +316,7 @@
     half_flops = 2 * slots * 2 * width * n_y * LANES
     part_shape = ((n_y, slots, LANES), bf16)
     part_theirs, xg = call(
-        functools.partial(first_kernel, piece),
+        functools.partial(first_kernel, piece, 2 * unit),
         [part_shape, ((slots, 2 * width), bf16)],
         2 * half_flops,
         1,
@@ -321,7 +325,8 @@
         w_front,
     )
     arrived = lax.ppermute(part_theirs, "dp", other_core)
-    (part_mine,) = call(second_kernel, [part_shape], half_flops, 1, mine, xg, w_front)
+    (part_mine,) = call(
+        functools.partial(second_kernel, 2 * unit), [part_shape], half_flops, 1, mine, xg, w_front)
     chip = (part_mine.astype(f32) + arrived.astype(f32)).astype(bf16)
     head, tail = call(
         functools.partial(act_kernel, unit),
@@ -333,7 +338,7 @@
     tail = swap(tail, "dp")
     head = lax.all_gather(head, "dp", axis=0)
     (out,) = call(
-        functools.partial(back_kernel, piece),
+        functools.partial(back_kernel, piece, 2 * unit),
         [((n_etp, rows, LANES), bf16)],
         4 * half_flops,
         0,

time: 156 us -> 150 us (0.962)
  local copies, waits for them, and re-layouts: 12.8 us -> 6.75 us
  waiting for transfers between devices: 22.1 us -> 28 us
  starting transfers between devices: 35.7 us -> 33.8 us
    all_to_all x4, waiting for transfers between devices: 20.8 us -> 26.8 us  [swap(): lax.all_to_all(x, axis, split_axis=0, concat_axis=0, tiled=True, axis_ind...]
    unnamed x16 -> x10, local copies, waits for them, and re-layouts: 2.59 us -> 0.02 us
    all_to_all x4, starting transfers between devices: 33.7 us -> 31.9 us  [swap(): lax.all_to_all(x, axis, split_axis=0, concat_axis=0, tiled=True, axis_ind...]
    another operation x1, local copies, waits for them, and re-layouts: 2 us -> 0.14 us  [local(): w_down = down_weight[0].reshape(n_dp, unit, width)]
  transfers between devices with their start and end apart: 5 -> 5, of which waited for: 4 -> 4; matrix products, arithmetic and copies ran while one was open for 9% -> 6% of each run, Pallas kernels for 0% -> 1%
where the time goes in v6:
time: 150 us; the launch traced here: 149 us
  blocking collectives  67.1 us (45%)
  starting transfers between devices  33.8 us (23%)
  waiting for transfers between devices  28 us (19%)
  Pallas kernels  9.25 us (6%)
  local copies, waits for them, and re-layouts  6.75 us (4%)
  matrix products  1.84 us (1%)
  other arithmetic  1.78 us (1%)
    all_to_all x2, blocking collectives, swap(): lax.all_to_all(x, axis, split_axis=0, concat_axis=0, tiled=True, axis_ind...  40.9 us
    all_to_all x4, starting transfers between devices, swap(): lax.all_to_all(x, axis, split_axis=0, concat_axis=0, tiled=True, axis_ind...  31.9 us
    all_to_all x4, waiting for transfers between devices, swap(): lax.all_to_all(x, axis, split_axis=0, concat_axis=0, tiled=True, axis_ind...  26.8 us
    all_gather x1, blocking collectives, local(): head = lax.all_gather(head, 'dp', axis=0)  26.2 us
    pallas_call x6, Pallas kernels, call(): pl.pallas_call(kernel, out_shape=outs, in_specs=[smem] * n_scalar + [held...  9.25 us
  transfers between devices with their start and end apart: 5, of which 4 were waited for; matrix products, arithmetic and copies ran while one was open for 6% of the time, Pallas kernels for 1%

profile of v6, /device:TPU:2, one launch (start us, length us, event | category | flops | bytes accessed | tf_op | source)
XLA Modules:
  0.0 149.3 jit_solution(6915055483719827259)
XLA Ops:
  0.6 0.0 copy-start.4
  0.6 2.3 %shard_map.110 = (bf16[512,128]{1,0:T(8,128)(2,1)}, bf16[512,64]{1,0:T(8,128)(2,1)}, bf16[512,64]{1,0:T(8,128)(2,1)}, bf16[512,64]{1,0:T(8,128)(2,1)}, f32[512,64]{1,0:T(8,128)}) custom-call(s32[1]{0:T(128)} %bitcast.col_ref, bf16[64,384]{1,0:T(8,128)(2,1)} %tok_hbm.1, bf16[64,384]{1,0:T(8,128)(2,1)} %cot_hbm.1, s32[4,64]{1,0:T(4,128)} %bitcast.35, ...), custom_call_target="tpu_custom_call" | custom-call | flops 60000000 | bytes 559108 | tf_op jit(solution)/shard_map/pallas_call | solution.py:35
  3.0 18.9 %all-to-all-start = ((bf16[16,32,128]{2,1,0:T(8,128)(2,1)}), bf16[16,32,128]{2,1,0:T(8,128)(2,1)S(1)}, u32[]{:S(2)}, u32[]{:S(2)}) async-start(bf16[16,32,128]{2,1,0:T(8,128)(2,1)} %bitcast.34), calls=%async_computation | async-start | bytes 262144 | tf_op jit(solution)/shard_map/all_to_all | solution.py:20
  21.8 1.2 reshape.36
  23.0 1.2 reshape.37
  24.2 0.0 copy-done.4
  24.2 0.1 reshape_squeeze.3
  24.4 0.1 pad.5.clone
  24.5 0.9 maximum_maximum_fusion.w_ref
  25.3 11.2 %all-to-all-done = bf16[16,32,128]{2,1,0:T(8,128)(2,1)S(1)} async-done(((bf16[16,32,128]{2,1,0:T(8,128)(2,1)}), bf16[16,32,128]{2,1,0:T(8,128)(2,1)S(1)}, u32[]{:S(2)}, u32[]{:S(2)}) %all-to-all-start) | async-done | bytes 131104 | tf_op jit(solution)/shard_map/all_to_all | solution.py:20
  36.5 0.9 broadcast_in_dim.30
  37.4 4.8 %all-to-all-start.1 = ((bf16[4,512,128]{2,1,0:T(8,128)(2,1)}), bf16[4,512,128]{2,1,0:T(8,128)(2,1)S(1)}, u32[]{:S(2)}, u32[]{:S(2)}) async-start(bf16[4,512,128]{2,1,0:T(8,128)(2,1)} %broadcast_in_dim.30), calls=%async_computation.1 | async-start | bytes 1048576 | tf_op jit(solution)/shard_map/all_to_all | solution.py:20
  42.2 6.6 %all-to-all-done.1.pack_ref = bf16[4,512,128]{2,1,0:T(8,128)(2,1)S(1)} async-done(((bf16[4,512,128]{2,1,0:T(8,128)(2,1)}), bf16[4,512,128]{2,1,0:T(8,128)(2,1)S(1)}, u32[]{:S(2)}, u32[]{:S(2)}) %all-to-all-start.1) | async-done | bytes 524320 | tf_op jit(solution)/shard_map/all_to_all | solution.py:20
  48.9 1.6 %shard_map.111 = (bf16[8,336,128]{2,1,0:T(8,128)(2,1)S(1)}, bf16[336,768]{1,0:T(8,128)(2,1)S(1)}) custom-call(s32[1]{0:T(128)} %bitcast.4.half_ref, bf16[4,512,128]{2,1,0:T(8,128)(2,1)S(1)} %all-to-all-done.1.pack_ref, bf16[16,128,384]{2,1,0:T(8,128)(2,1)S(1)} %maximum_maximum_fusion.w_ref), custom_call_target="tpu_custom_call" | custom-call | flops 1056964608 | bytes 3301380 | tf_op jit(solution)/shard_map/pallas_call | solution.py:35
  50.4 1.9 %collective-permute-start = (bf16[8,336,128]{2,1,0:T(8,128)(2,1)S(1)}, bf16[8,336,128]{2,1,0:T(8,128)(2,1)S(1)}, u32[]{:S(2)}, u32[]{:S(2)}) collective-permute-start(bf16[8,336,128]{2,1,0:T(8,128)(2,1)S(1)} %get-tuple-element.34), channel_id=1, source_target_pairs={{0,1},{1,0},{2,3},{3,2},{4,5},{5,4},{6,7},{7,6},{8,9},{9,8},{10,11... | collective-permute-start | bytes 2064392 | tf_op jit(solution)/shard_map/ppermute | solution.py:327
  52.3 0.9 shard_map.112
  53.3 1.2 collective-permute-done
  54.5 0.2 add_convert_fusion
  54.6 28.2 %all_to_all.30.sum_ref = bf16[8,336,128]{2,1,0:T(8,128)(2,1)S(1)} all-to-all(bf16[8,336,128]{2,1,0:T(8,128)(2,1)S(1)} %add_convert_fusion), channel_id=1, replica_groups={{0,2,4,6,8,10,12,14},{1,3,5,7,9,11,13,15},{16,18,20,22,24,26,28,30},{17..., dimensions={0} | all-to-all | bytes 1376256 | tf_op jit(solution)/shard_map/all_to_all | solution.py:20
  82.8 1.1 shard_map.113
  83.9 3.6 %all-to-all-start.3 = ((bf16[16,96,128]{2,1,0:T(8,128)(2,1)}), bf16[16,96,128]{2,1,0:T(8,128)(2,1)S(1)}, u32[]{:S(2)}, u32[]{:S(2)}) async-start(bf16[16,96,128]{2,1,0:T(8,128)(2,1)} %get-tuple-element.36), calls=%async_computation.3 | async-start | bytes 786432 | tf_op jit(solution)/shard_map/all_to_all | solution.py:20
  87.5 26.2 %all-gather = bf16[3840,128]{1,0:T(8,128)(2,1)S(1)} all-gather(bf16[240,128]{1,0:T(8,128)(2,1)S(1)} %get-tuple-element.35), channel_id=2, replica_groups=mesh['expert'=16,'etp'=4,'dp'=16] {'dp'}, dimensions={0}, use_global_device_ids=true | all-gather | bytes 1044480 | tf_op jit(solution)/shard_map/all_gather | solution.py:339
  113.7 0.0 all-to-all-done.3.tail_ref
  113.7 2.2 %shard_map.114 = bf16[4,512,128]{2,1,0:T(8,128)(2,1)S(1)} custom-call(bf16[16,240,128]{2,1,0:T(8,128)(2,1)S(1)} %bitcast.26, bf16[16,96,128]{2,1,0:T(8,128)(2,1)S(1)} %all-to-all-done.3.tail_ref, bf16[16,128,384]{2,1,0:T(8,128)(2,1)S(1)} %maximum_maximum_fusion.w_ref), custom_call_target="tpu_custom_call" | custom-call | flops 2113929216 | bytes 3473408 | tf_op jit(solution)/shard_map/pallas_call | solution.py:35
  115.9 12.7 %all_to_all.31 = bf16[4,512,128]{2,1,0:T(8,128)(2,1)S(1)} all-to-all(bf16[4,512,128]{2,1,0:T(8,128)(2,1)S(1)} %shard_map.114), channel_id=1, replica_groups=mesh['expert'=16,'etp'=4,'dp'=16] {'etp'}, dimensions={0} | all-to-all | bytes 1048576 | tf_op jit(solution)/shard_map/all_to_all | solution.py:20
  128.6 0.7 reduce_sum.12
  129.3 4.6 %all-to-all-start.5 = ((bf16[16,32,128]{2,1,0:T(8,128)(2,1)}), bf16[16,32,128]{2,1,0:T(8,128)(2,1)S(1)}, u32[]{:S(2)}, u32[]{:S(2)}) async-start(bf16[16,32,128]{2,1,0:T(8,128)(2,1)} %bitcast.13), calls=%async_computation.5 | async-start | bytes 262144 | tf_op jit(solution)/shard_map/all_to_all | solution.py:20
  134.0 1.8 %convolution_convert_fusion = bf16[16,128,768]{2,1,0:T(8,128)(2,1)S(1)} fusion(bf16[16,96,128]{2,1,0:T(8,128)(2,1)S(1)} %all-to-all-done.3.tail_ref, bf16[16,240,128]{2,1,0:T(8,128)(2,1)S(1)} %bitcast.27, bf16[336,768]{1,0:T(8,128)(2,1)S(1)} %get-tuple-element.33.xg_ref), kind=kOutput, calls=%fused_computation | convolution fusion | flops 1061289984 | bytes 5038080 | tf_op jit(solution)/shard_map/dot_general | solution.py:16
  135.8 0.0 copy-start
  135.8 0.0 copy-start.1
  135.8 0.0 copy-start.2
  135.8 0.0 copy-start.3
  135.9 0.5 fusion.5
  136.4 0.9 broadcast_in_dim_reshape.3
  137.3 0.9 reshape.41
  138.2 0.9 reshape.40
  139.1 8.9 %all-to-all-done.5 = bf16[16,32,128]{2,1,0:T(8,128)(2,1)S(1)} async-done(((bf16[16,32,128]{2,1,0:T(8,128)(2,1)}), bf16[16,32,128]{2,1,0:T(8,128)(2,1)S(1)}, u32[]{:S(2)}, u32[]{:S(2)}) %all-to-all-start.5) | async-done | bytes 131104 | tf_op jit(solution)/shard_map/all_to_all | solution.py:20
  148.1 0.0 copy-done
  148.1 0.0 copy-done.1
  148.1 0.0 copy-done.2
  148.1 0.0 copy-done.3
  148.1 1.2 shard_map.115
  (1 shorter events, 0.0 us)
Async XLA Ops:
  0.6 23.6 %copy-start.4 = (bf16[1,672,384]{2,1,0:T(8,128)(2,1)S(1)}, bf16[1,672,384]{2,1,0:T(8,128)(2,1)}, u32[]{:S(2)}) copy-start(bf16[1,672,384]{2,1,0:T(8,128)(2,1)} %param.12) | copy-start | bytes 1548292
  3.0 33.6 %all-to-all-start = ((bf16[16,32,128]{2,1,0:T(8,128)(2,1)}), bf16[16,32,128]{2,1,0:T(8,128)(2,1)S(1)}, u32[]{:S(2)}, u32[]{:S(2)}) async-start(bf16[16,32,128]{2,1,0:T(8,128)(2,1)} %bitcast.34), calls=%async_computation | async-start | bytes 262144 | tf_op jit(solution)/shard_map/all_to_all | solution.py:20
  37.4 11.5 %all-to-all-start.1 = ((bf16[4,512,128]{2,1,0:T(8,128)(2,1)}), bf16[4,512,128]{2,1,0:T(8,128)(2,1)S(1)}, u32[]{:S(2)}, u32[]{:S(2)}) async-start(bf16[4,512,128]{2,1,0:T(8,128)(2,1)} %broadcast_in_dim.30), calls=%async_computation.1 | async-start | bytes 1048576 | tf_op jit(solution)/shard_map/all_to_all | solution.py:20
  50.4 4.0 %collective-permute-start = (bf16[8,336,128]{2,1,0:T(8,128)(2,1)S(1)}, bf16[8,336,128]{2,1,0:T(8,128)(2,1)S(1)}, u32[]{:S(2)}, u32[]{:S(2)}) collective-permute-start(bf16[8,336,128]{2,1,0:T(8,128)(2,1)S(1)} %get-tuple-element.34), channel_id=1, source_target_pairs={{0,1},{1,0},{2,3},{3,2},{4,5},{5,4},{6,7},{7,6},{8,9},{9,8},{10,11... | collective-permute-start | bytes 2064392 | tf_op jit(solution)/shard_map/ppermute | solution.py:327
  83.9 29.8 %all-to-all-start.3 = ((bf16[16,96,128]{2,1,0:T(8,128)(2,1)}), bf16[16,96,128]{2,1,0:T(8,128)(2,1)S(1)}, u32[]{:S(2)}, u32[]{:S(2)}) async-start(bf16[16,96,128]{2,1,0:T(8,128)(2,1)} %get-tuple-element.36), calls=%async_computation.3 | async-start | bytes 786432 | tf_op jit(solution)/shard_map/all_to_all | solution.py:20
  129.3 18.7 %all-to-all-start.5 = ((bf16[16,32,128]{2,1,0:T(8,128)(2,1)}), bf16[16,32,128]{2,1,0:T(8,128)(2,1)S(1)}, u32[]{:S(2)}, u32[]{:S(2)}) async-start(bf16[16,32,128]{2,1,0:T(8,128)(2,1)} %bitcast.13), calls=%async_computation.5 | async-start | bytes 262144 | tf_op jit(solution)/shard_map/all_to_all | solution.py:20
  135.8 12.2 %copy-start = (f32[512,64]{1,0:T(8,128)S(1)}, f32[512,64]{1,0:T(8,128)}, u32[]{:S(2)}) copy-start(f32[512,64]{1,0:T(8,128)} %get-tuple-element.22.weight_ref) | copy-start | bytes 393220
  135.8 12.2 %copy-start.1 = (bf16[512,64]{1,0:T(8,128)(2,1)S(1)}, bf16[512,64]{1,0:T(8,128)(2,1)}, u32[]{:S(2)}) copy-start(bf16[512,64]{1,0:T(8,128)(2,1)} %get-tuple-element.23.place_ref) | copy-start | bytes 196612
  135.8 12.2 %copy-start.2 = (bf16[512,64]{1,0:T(8,128)(2,1)S(1)}, bf16[512,64]{1,0:T(8,128)(2,1)}, u32[]{:S(2)}) copy-start(bf16[512,64]{1,0:T(8,128)(2,1)} %get-tuple-element.24.place_b_ref) | copy-start | bytes 196612
  135.8 12.2 %copy-start.3 = (bf16[512,64]{1,0:T(8,128)(2,1)S(1)}, bf16[512,64]{1,0:T(8,128)(2,1)}, u32[]{:S(2)}) copy-start(bf16[512,64]{1,0:T(8,128)(2,1)} %get-tuple-element.25.place_c_ref) | copy-start | bytes 196612

commit v7 on v6

--- a/solution.py
+++ b/solution.py
@@ -144,8 +144,9 @@
     width = w_ref.shape[2]
     from_x = (iota((xg.shape[0], 2 * LANES), 1) & (LANES - 1)) < split
     for j in range(0, chunks, 2):
-        at = half_ref[0] + 2 * j
-        w = jnp.concatenate([w_ref[at], w_ref[at + 2]], axis=0)
+        parity = half_ref[1] if j >= chunks // 2 else 1 - half_ref[1]
+        at = half_ref[0] + 2 * parity + 4 * (j % (chunks // 2))
+        w = jnp.concatenate([w_ref[at], w_ref[at + 4]], axis=0)
         by_x = mm(xg[:, :width], w, ((1,), (1,)))
         by_g = mm(xg[:, width:], w, ((1,), (1,)))
         got = jnp.where(from_x, by_x, by_g).astype(bf16)
@@ -265,10 +266,11 @@
     unit = hid // n_dp
     slots = n_exp * CAP
     rows = n_exp * PACK
-    same_core = [[2 * y + c for y in range(n_y)] for c in range(2)]
+    same_parity = [[4 * k + i for k in range(n_y // 2)] for i in range(4)]
     other_core = [(i, i ^ 1) for i in range(n_dp)]
     core = lax.bitwise_and(lax.axis_index("dp"), 1)
-    mine, theirs = core[None], (1 - core)[None]
+    parity = lax.bitwise_and(lax.shift_right_logical(lax.axis_index("dp"), 1), 1)
+    mine, theirs = jnp.stack([core, parity]), jnp.stack([1 - core, parity])
     col = lax.axis_index("etp") * piece
 
     send, place, place_b, place_c, weight = call(
@@ -327,13 +329,17 @@
     arrived = lax.ppermute(part_theirs, "dp", other_core)
     (part_mine,) = call(
         functools.partial(second_kernel, 2 * unit), [part_shape], half_flops, 1, mine, xg, w_front)
-    chip = (part_mine.astype(f32) + arrived.astype(f32)).astype(bf16)
+    cut = n_y // 2
+    away = (part_mine[:cut].astype(f32) + arrived[:cut].astype(f32)).astype(bf16)
+    away = lax.ppermute(away, "dp", [(i, i ^ 2) for i in range(n_dp)])
+    kept = part_mine[cut:].astype(f32) + arrived[cut:].astype(f32)
+    kept = (kept + away.astype(f32)).astype(bf16)
     head, tail = call(
         functools.partial(act_kernel, unit),
         [((HEAD, LANES), bf16), ((n_dp, slots - HEAD, LANES), bf16)],
         10_000_000,
         0,
-        swap(chip, "dp", same_core),
+        swap(kept, "dp", same_parity),
     )
     tail = swap(tail, "dp")
     head = lax.all_gather(head, "dp", axis=0)

time: 150 us -> 153 us (1.020)
  blocking collectives: 67.1 us -> 57.9 us
  waiting for transfers between devices: 28 us -> 35.8 us
  starting transfers between devices: 33.8 us -> 37.3 us
    all_to_all x2, blocking collectives: 40.9 us -> 31.7 us  [swap(): lax.all_to_all(x, axis, split_axis=0, concat_axis=0, tiled=True, axis_ind...]
    ppermute x0 -> x1, waiting for transfers between devices: none -> 8.51 us  [local(): away = lax.ppermute(away, 'dp', [(i, i ^ 2) for i in range(n_dp)])]
    ppermute x0 -> x1, starting transfers between devices: none -> 3.48 us  [local(): away = lax.ppermute(away, 'dp', [(i, i ^ 2) for i in range(n_dp)])]
  transfers between devices with their start and end apart: 5 -> 6, of which waited for: 4 -> 5; matrix products, arithmetic and copies ran while one was open for 6% -> 6% of each run, Pallas kernels for 1% -> 1%
where the time goes in v7:
time: 153 us
  blocking collectives  57.9 us (38%)
  starting transfers between devices  37.3 us (24%)
  waiting for transfers between devices  35.8 us (23%)
  Pallas kernels  10.3 us (7%)
  local copies, waits for them, and re-layouts  6.74 us (4%)
  other arithmetic  1.98 us (1%)
  matrix products  1.84 us (1%)
    all_to_all x4, starting transfers between devices, swap(): lax.all_to_all(x, axis, split_axis=0, concat_axis=0, tiled=True, axis_ind...  31.9 us
    all_to_all x2, blocking collectives, swap(): lax.all_to_all(x, axis, split_axis=0, concat_axis=0, tiled=True, axis_ind...  31.7 us
    all_to_all x4, waiting for transfers between devices, swap(): lax.all_to_all(x, axis, split_axis=0, concat_axis=0, tiled=True, axis_ind...  26.7 us
    all_gather x1, blocking collectives, local(): head = lax.all_gather(head, 'dp', axis=0)  26.2 us
    pallas_call x6, Pallas kernels, call(): pl.pallas_call(kernel, out_shape=outs, in_specs=[smem] * n_scalar + [held...  10.3 us
    ppermute x1, waiting for transfers between devices, local(): away = lax.ppermute(away, 'dp', [(i, i ^ 2) for i in range(n_dp)])  8.51 us
    ppermute x1, starting transfers between devices, local(): away = lax.ppermute(away, 'dp', [(i, i ^ 2) for i in range(n_dp)])  3.48 us
  transfers between devices with their start and end apart: 6, of which 5 were waited for; matrix products, arithmetic and copies ran while one was open for 6% of the time, Pallas kernels for 1%

profile of v7, /device:TPU:2, one launch (start us, length us, event | category | flops | bytes accessed | tf_op | source)
XLA Modules:
  0.0 152.6 jit_solution(14947051236442126050)
XLA Ops:
  0.6 0.0 copy-start.4
  0.6 2.3 %shard_map.110 = (bf16[512,128]{1,0:T(8,128)(2,1)}, bf16[512,64]{1,0:T(8,128)(2,1)}, bf16[512,64]{1,0:T(8,128)(2,1)}, bf16[512,64]{1,0:T(8,128)(2,1)}, f32[512,64]{1,0:T(8,128)}) custom-call(s32[1]{0:T(128)} %bitcast.col_ref, bf16[64,384]{1,0:T(8,128)(2,1)} %tok_hbm.1, bf16[64,384]{1,0:T(8,128)(2,1)} %cot_hbm.1, s32[4,64]{1,0:T(4,128)} %bitcast.36, ...), custom_call_target="tpu_custom_call" | custom-call | flops 60000000 | bytes 559108 | tf_op jit(solution)/shard_map/pallas_call | solution.py:35
  3.0 18.9 %all-to-all-start = ((bf16[16,32,128]{2,1,0:T(8,128)(2,1)}), bf16[16,32,128]{2,1,0:T(8,128)(2,1)S(1)}, u32[]{:S(2)}, u32[]{:S(2)}) async-start(bf16[16,32,128]{2,1,0:T(8,128)(2,1)} %bitcast.35), calls=%async_computation | async-start | bytes 262144 | tf_op jit(solution)/shard_map/all_to_all | solution.py:20
  21.8 1.2 reshape.36
  23.0 1.2 reshape.37
  24.2 0.0 copy-done.4
  24.2 0.1 reshape_squeeze.3
  24.4 0.1 pad.5.clone
  24.5 0.9 maximum_maximum_fusion.w_ref
  25.3 11.2 %all-to-all-done = bf16[16,32,128]{2,1,0:T(8,128)(2,1)S(1)} async-done(((bf16[16,32,128]{2,1,0:T(8,128)(2,1)}), bf16[16,32,128]{2,1,0:T(8,128)(2,1)S(1)}, u32[]{:S(2)}, u32[]{:S(2)}) %all-to-all-start) | async-done | bytes 131104 | tf_op jit(solution)/shard_map/all_to_all | solution.py:20
  36.5 0.9 broadcast_in_dim.22
  37.4 4.8 %all-to-all-start.1 = ((bf16[4,512,128]{2,1,0:T(8,128)(2,1)}), bf16[4,512,128]{2,1,0:T(8,128)(2,1)S(1)}, u32[]{:S(2)}, u32[]{:S(2)}) async-start(bf16[4,512,128]{2,1,0:T(8,128)(2,1)} %broadcast_in_dim.22), calls=%async_computation.1 | async-start | bytes 1048576 | tf_op jit(solution)/shard_map/all_to_all | solution.py:20
  42.2 0.1 pad_add_fusion.1.half_ref
  42.3 6.5 %all-to-all-done.1.pack_ref = bf16[4,512,128]{2,1,0:T(8,128)(2,1)S(1)} async-done(((bf16[4,512,128]{2,1,0:T(8,128)(2,1)}), bf16[4,512,128]{2,1,0:T(8,128)(2,1)S(1)}, u32[]{:S(2)}, u32[]{:S(2)}) %all-to-all-start.1) | async-done | bytes 524320 | tf_op jit(solution)/shard_map/all_to_all | solution.py:20
  48.8 2.1 %shard_map.111 = (bf16[8,336,128]{2,1,0:T(8,128)(2,1)S(1)}, bf16[336,768]{1,0:T(8,128)(2,1)S(1)}) custom-call(s32[2]{0:T(128)S(1)} %pad_add_fusion.1.half_ref, bf16[4,512,128]{2,1,0:T(8,128)(2,1)S(1)} %all-to-all-done.1.pack_ref, bf16[16,128,384]{2,1,0:T(8,128)(2,1)S(1)} %maximum_maximum_fusion.w_ref), custom_call_target="tpu_custom_call" | custom-call | flops 1056964608 | bytes 3301384 | tf_op jit(solution)/shard_map/pallas_call | solution.py:35
  51.0 1.9 %collective-permute-start = (bf16[8,336,128]{2,1,0:T(8,128)(2,1)S(1)}, bf16[8,336,128]{2,1,0:T(8,128)(2,1)S(1)}, u32[]{:S(2)}, u32[]{:S(2)}) collective-permute-start(bf16[8,336,128]{2,1,0:T(8,128)(2,1)S(1)} %get-tuple-element.34), channel_id=1, source_target_pairs={{0,1},{1,0},{2,3},{3,2},{4,5},{5,4},{6,7},{7,6},{8,9},{9,8},{10,11... | collective-permute-start | bytes 2064392 | tf_op jit(solution)/shard_map/ppermute | solution.py:329
  52.9 0.1 pad_add_fusion.half_ref
  53.0 1.5 shard_map.112
  54.4 0.6 collective-permute-done
  55.0 0.1 add_convert_fusion.1
  55.1 3.5 %collective-permute-start.1 = (bf16[4,336,128]{2,1,0:T(8,128)(2,1)S(1)}, bf16[4,336,128]{2,1,0:T(8,128)(2,1)S(1)}, u32[]{:S(2)}, u32[]{:S(2)}) collective-permute-start(bf16[4,336,128]{2,1,0:T(8,128)(2,1)S(1)} %add_convert_fusion.1), channel_id=1, source_target_pairs={{0,2},{1,3},{2,0},{3,1},{4,6},{5,7},{6,4},{7,5},{8,10},{9,11},{10,... | collective-permute-start | bytes 1032200 | tf_op jit(solution)/shard_map/ppermute | solution.py:334
  58.6 8.5 %collective-permute-done.1 = bf16[4,336,128]{2,1,0:T(8,128)(2,1)S(1)} collective-permute-done((bf16[4,336,128]{2,1,0:T(8,128)(2,1)S(1)}, bf16[4,336,128]{2,1,0:T(8,128)(2,1)S(1)}, u32[]{:S(2)}, u32[]{:S(2)}) %collective-permute-start.1) | collective-permute-done | bytes 344096 | tf_op jit(solution)/shard_map/ppermute | solution.py:334
  67.1 0.1 add_convert_fusion
  67.2 19.0 %all_to_all.30.sum_ref = bf16[4,336,128]{2,1,0:T(8,128)(2,1)S(1)} all-to-all(bf16[4,336,128]{2,1,0:T(8,128)(2,1)S(1)} %add_convert_fusion), channel_id=1, replica_groups={{0,4,8,12},{1,5,9,13},{2,6,10,14},{3,7,11,15},{16,20,24,28},{17,21,25,2..., dimensions={0} | all-to-all | bytes 688128 | tf_op jit(solution)/shard_map/all_to_all | solution.py:20
  86.2 1.0 shard_map.113
  87.2 3.6 %all-to-all-start.3 = ((bf16[16,96,128]{2,1,0:T(8,128)(2,1)}), bf16[16,96,128]{2,1,0:T(8,128)(2,1)S(1)}, u32[]{:S(2)}, u32[]{:S(2)}) async-start(bf16[16,96,128]{2,1,0:T(8,128)(2,1)} %get-tuple-element.36), calls=%async_computation.3 | async-start | bytes 786432 | tf_op jit(solution)/shard_map/all_to_all | solution.py:20
  90.8 26.2 %all-gather = bf16[3840,128]{1,0:T(8,128)(2,1)S(1)} all-gather(bf16[240,128]{1,0:T(8,128)(2,1)S(1)} %get-tuple-element.35), channel_id=2, replica_groups=mesh['expert'=16,'etp'=4,'dp'=16] {'dp'}, dimensions={0}, use_global_device_ids=true | all-gather | bytes 1044480 | tf_op jit(solution)/shard_map/all_gather | solution.py:345
  117.0 0.0 all-to-all-done.3.tail_ref
  117.0 2.2 %shard_map.114 = bf16[4,512,128]{2,1,0:T(8,128)(2,1)S(1)} custom-call(bf16[16,240,128]{2,1,0:T(8,128)(2,1)S(1)} %bitcast.27, bf16[16,96,128]{2,1,0:T(8,128)(2,1)S(1)} %all-to-all-done.3.tail_ref, bf16[16,128,384]{2,1,0:T(8,128)(2,1)S(1)} %maximum_maximum_fusion.w_ref), custom_call_target="tpu_custom_call" | custom-call | flops 2113929216 | bytes 3473408 | tf_op jit(solution)/shard_map/pallas_call | solution.py:35
  119.3 12.7 %all_to_all.31 = bf16[4,512,128]{2,1,0:T(8,128)(2,1)S(1)} all-to-all(bf16[4,512,128]{2,1,0:T(8,128)(2,1)S(1)} %shard_map.114), channel_id=1, replica_groups=mesh['expert'=16,'etp'=4,'dp'=16] {'etp'}, dimensions={0} | all-to-all | bytes 1048576 | tf_op jit(solution)/shard_map/all_to_all | solution.py:20
  131.9 0.7 reduce_sum.12
  132.7 4.6 %all-to-all-start.5 = ((bf16[16,32,128]{2,1,0:T(8,128)(2,1)}), bf16[16,32,128]{2,1,0:T(8,128)(2,1)S(1)}, u32[]{:S(2)}, u32[]{:S(2)}) async-start(bf16[16,32,128]{2,1,0:T(8,128)(2,1)} %bitcast.14), calls=%async_computation.5 | async-start | bytes 262144 | tf_op jit(solution)/shard_map/all_to_all | solution.py:20
  137.3 1.8 %convolution_convert_fusion = bf16[16,128,768]{2,1,0:T(8,128)(2,1)S(1)} fusion(bf16[16,96,128]{2,1,0:T(8,128)(2,1)S(1)} %all-to-all-done.3.tail_ref, bf16[16,240,128]{2,1,0:T(8,128)(2,1)S(1)} %bitcast.28, bf16[336,768]{1,0:T(8,128)(2,1)S(1)} %get-tuple-element.33.xg_ref), kind=kOutput, calls=%fused_computation | convolution fusion | flops 1061289984 | bytes 5038080 | tf_op jit(solution)/shard_map/dot_general | solution.py:16
  139.2 0.0 copy-start
  139.2 0.0 copy-start.1
  139.2 0.0 copy-start.2
  139.2 0.0 copy-start.3
  139.2 0.5 fusion.5
  139.7 0.9 broadcast_in_dim_reshape.3
  140.6 0.9 reshape.41
  141.6 0.9 reshape.40
  142.5 8.9 %all-to-all-done.5 = bf16[16,32,128]{2,1,0:T(8,128)(2,1)S(1)} async-done(((bf16[16,32,128]{2,1,0:T(8,128)(2,1)}), bf16[16,32,128]{2,1,0:T(8,128)(2,1)S(1)}, u32[]{:S(2)}, u32[]{:S(2)}) %all-to-all-start.5) | async-done | bytes 131104 | tf_op jit(solution)/shard_map/all_to_all | solution.py:20
  151.4 0.0 copy-done
  151.4 0.0 copy-done.1
  151.4 0.0 copy-done.2
  151.4 0.0 copy-done.3
  151.4 1.2 shard_map.115
  (1 shorter events, 0.0 us)
Async XLA Ops:
  0.6 23.6 %copy-start.4 = (bf16[1,672,384]{2,1,0:T(8,128)(2,1)S(1)}, bf16[1,672,384]{2,1,0:T(8,128)(2,1)}, u32[]{:S(2)}) copy-start(bf16[1,672,384]{2,1,0:T(8,128)(2,1)} %param.12) | copy-start | bytes 1548292
  3.0 33.6 %all-to-all-start = ((bf16[16,32,128]{2,1,0:T(8,128)(2,1)}), bf16[16,32,128]{2,1,0:T(8,128)(2,1)S(1)}, u32[]{:S(2)}, u32[]{:S(2)}) async-start(bf16[16,32,128]{2,1,0:T(8,128)(2,1)} %bitcast.35), calls=%async_computation | async-start | bytes 262144 | tf_op jit(solution)/shard_map/all_to_all | solution.py:20
  37.4 11.5 %all-to-all-start.1 = ((bf16[4,512,128]{2,1,0:T(8,128)(2,1)}), bf16[4,512,128]{2,1,0:T(8,128)(2,1)S(1)}, u32[]{:S(2)}, u32[]{:S(2)}) async-start(bf16[4,512,128]{2,1,0:T(8,128)(2,1)} %broadcast_in_dim.22), calls=%async_computation.1 | async-start | bytes 1048576 | tf_op jit(solution)/shard_map/all_to_all | solution.py:20
  51.0 4.0 %collective-permute-start = (bf16[8,336,128]{2,1,0:T(8,128)(2,1)S(1)}, bf16[8,336,128]{2,1,0:T(8,128)(2,1)S(1)}, u32[]{:S(2)}, u32[]{:S(2)}) collective-permute-start(bf16[8,336,128]{2,1,0:T(8,128)(2,1)S(1)} %get-tuple-element.34), channel_id=1, source_target_pairs={{0,1},{1,0},{2,3},{3,2},{4,5},{5,4},{6,7},{7,6},{8,9},{9,8},{10,11... | collective-permute-start | bytes 2064392 | tf_op jit(solution)/shard_map/ppermute | solution.py:329
  55.1 12.0 %collective-permute-start.1 = (bf16[4,336,128]{2,1,0:T(8,128)(2,1)S(1)}, bf16[4,336,128]{2,1,0:T(8,128)(2,1)S(1)}, u32[]{:S(2)}, u32[]{:S(2)}) collective-permute-start(bf16[4,336,128]{2,1,0:T(8,128)(2,1)S(1)} %add_convert_fusion.1), channel_id=1, source_target_pairs={{0,2},{1,3},{2,0},{3,1},{4,6},{5,7},{6,4},{7,5},{8,10},{9,11},{10,... | collective-permute-start | bytes 1032200 | tf_op jit(solution)/shard_map/ppermute | solution.py:334
  87.2 29.8 %all-to-all-start.3 = ((bf16[16,96,128]{2,1,0:T(8,128)(2,1)}), bf16[16,96,128]{2,1,0:T(8,128)(2,1)S(1)}, u32[]{:S(2)}, u32[]{:S(2)}) async-start(bf16[16,96,128]{2,1,0:T(8,128)(2,1)} %get-tuple-element.36), calls=%async_computation.3 | async-start | bytes 786432 | tf_op jit(solution)/shard_map/all_to_all | solution.py:20
  132.7 18.7 %all-to-all-start.5 = ((bf16[16,32,128]{2,1,0:T(8,128)(2,1)}), bf16[16,32,128]{2,1,0:T(8,128)(2,1)S(1)}, u32[]{:S(2)}, u32[]{:S(2)}) async-start(bf16[16,32,128]{2,1,0:T(8,128)(2,1)} %bitcast.14), calls=%async_computation.5 | async-start | bytes 262144 | tf_op jit(solution)/shard_map/all_to_all | solution.py:20
  139.2 12.2 %copy-start = (f32[512,64]{1,0:T(8,128)S(1)}, f32[512,64]{1,0:T(8,128)}, u32[]{:S(2)}) copy-start(f32[512,64]{1,0:T(8,128)} %get-tuple-element.22.weight_ref) | copy-start | bytes 393220
  139.2 12.2 %copy-start.1 = (bf16[512,64]{1,0:T(8,128)(2,1)S(1)}, bf16[512,64]{1,0:T(8,128)(2,1)}, u32[]{:S(2)}) copy-start(bf16[512,64]{1,0:T(8,128)(2,1)} %get-tuple-element.23.place_ref) | copy-start | bytes 196612
  139.2 12.2 %copy-start.2 = (bf16[512,64]{1,0:T(8,128)(2,1)S(1)}, bf16[512,64]{1,0:T(8,128)(2,1)}, u32[]{:S(2)}) copy-start(bf16[512,64]{1,0:T(8,128)(2,1)} %get-tuple-element.24.place_b_ref) | copy-start | bytes 196612
  139.2 12.2 %copy-start.3 = (bf16[512,64]{1,0:T(8,128)(2,1)S(1)}, bf16[512,64]{1,0:T(8,128)(2,1)}, u32[]{:S(2)}) copy-start(bf16[512,64]{1,0:T(8,128)(2,1)} %get-tuple-element.25.place_c_ref) | copy-start | bytes 196612

commit v8 on v6

--- a/solution.py
+++ b/solution.py
@@ -20,6 +20,10 @@
     return lax.all_to_all(
         x, axis, split_axis=0, concat_axis=0, tiled=True, axis_index_groups=groups
     )
+
+
+def far_order(count):
+    return [(k >> 1) + (count // 2) * (k & 1) for k in range(count)]
 
 
 def iota(shape, axis):
@@ -77,7 +81,8 @@
     top_count, block_len = route_ref.shape
     rows = send_ref.shape[0]
     row = iota((rows, block_len), 0)
-    owner = lax.shift_right_logical(row, 5)
+    place_in_ring = lax.shift_right_logical(row, 5)
+    owner = lax.shift_right_logical(place_in_ring, 1) + (place_in_ring & 1) * (rows // PACK // 2)
     inner = row & (PACK - 1)
     hit = jnp.zeros((rows, block_len), f32)
     weight = jnp.zeros((rows, block_len), f32)
@@ -144,8 +149,9 @@
     width = w_ref.shape[2]
     from_x = (iota((xg.shape[0], 2 * LANES), 1) & (LANES - 1)) < split
     for j in range(0, chunks, 2):
-        at = half_ref[0] + 2 * j
-        w = jnp.concatenate([w_ref[at], w_ref[at + 2]], axis=0)
+        order = far_order(chunks)
+        at, after = half_ref[0] + 2 * order[j], half_ref[0] + 2 * order[j + 1]
+        w = jnp.concatenate([w_ref[at], w_ref[after]], axis=0)
         by_x = mm(xg[:, :width], w, ((1,), (1,)))
         by_g = mm(xg[:, width:], w, ((1,), (1,)))
         got = jnp.where(from_x, by_x, by_g).astype(bf16)
@@ -265,8 +271,9 @@
     unit = hid // n_dp
     slots = n_exp * CAP
     rows = n_exp * PACK
-    same_core = [[2 * y + c for y in range(n_y)] for c in range(2)]
+    same_core = [[2 * y + c for y in far_order(n_y)] for c in range(2)]
     other_core = [(i, i ^ 1) for i in range(n_dp)]
+    experts = [far_order(n_exp)]
     core = lax.bitwise_and(lax.axis_index("dp"), 1)
     mine, theirs = core[None], (1 - core)[None]
     col = lax.axis_index("etp") * piece
@@ -309,7 +316,7 @@
         [w_gate, w_up, w_down, jnp.zeros((n_dp, spare, width), bf16)], axis=1
     )
 
-    got = swap(send.reshape(n_exp, PACK, LANES), "expert").reshape(1, rows, LANES)
+    got = swap(send.reshape(n_exp, PACK, LANES), "expert", experts).reshape(1, rows, LANES)
     got, w_front = lax.optimization_barrier((got, w_front))
     packs = swap(jnp.broadcast_to(got, (n_etp, rows, LANES)), "etp")
 
@@ -347,7 +354,7 @@
         w_front,
     )
     out = jnp.sum(swap(out, "etp").astype(f32), axis=0).astype(bf16)
-    back = swap(out.reshape(n_exp, PACK, LANES), "expert").reshape(rows, LANES)
+    back = swap(out.reshape(n_exp, PACK, LANES), "expert", experts).reshape(rows, LANES)
 
     full = jnp.concatenate([head, tail], axis=1)
     grads = mm(full, xg, ((1,), (0,))).astype(bf16)

time: 150 us -> 150 us (level)
  the two profiles are of different devices: /device:TPU:2 before, /device:TPU:64 now
where the time goes in v8:
time: 150 us; the launch traced here: 149 us
  blocking collectives  65.6 us (44%)
  starting transfers between devices  32.5 us (22%)
  waiting for transfers between devices  30.5 us (20%)
  Pallas kernels  9.26 us (6%)
  local copies, waits for them, and re-layouts  6.74 us (4%)
  matrix products  1.84 us (1%)
  other arithmetic  1.78 us (1%)
    all_to_all x2, blocking collectives, swap(): lax.all_to_all(x, axis, split_axis=0, concat_axis=0, tiled=True, axis_ind...  39.4 us
    all_to_all x4, starting transfers between devices, swap(): lax.all_to_all(x, axis, split_axis=0, concat_axis=0, tiled=True, axis_ind...  30.6 us
    all_to_all x4, waiting for transfers between devices, swap(): lax.all_to_all(x, axis, split_axis=0, concat_axis=0, tiled=True, axis_ind...  29.3 us
    all_gather x1, blocking collectives, local(): head = lax.all_gather(head, 'dp', axis=0)  26.2 us
    pallas_call x6, Pallas kernels, call(): pl.pallas_call(kernel, out_shape=outs, in_specs=[smem] * n_scalar + [held...  9.26 us
  transfers between devices with their start and end apart: 5, of which 4 were waited for; matrix products, arithmetic and copies ran while one was open for 6% of the time, Pallas kernels for 1%

profile of v8, /device:TPU:64, one launch (start us, length us, event | category | flops | bytes accessed | tf_op | source)
XLA Modules:
  0.0 149.0 jit_solution(16089047713412906742)
XLA Ops:
  0.6 0.0 copy-start.4
  0.6 2.3 %shard_map.110 = (bf16[512,128]{1,0:T(8,128)(2,1)}, bf16[512,64]{1,0:T(8,128)(2,1)}, bf16[512,64]{1,0:T(8,128)(2,1)}, bf16[512,64]{1,0:T(8,128)(2,1)}, f32[512,64]{1,0:T(8,128)}) custom-call(s32[1]{0:T(128)} %bitcast.col_ref, bf16[64,384]{1,0:T(8,128)(2,1)} %tok_hbm.1, bf16[64,384]{1,0:T(8,128)(2,1)} %cot_hbm.1, s32[4,64]{1,0:T(4,128)} %bitcast.35, ...), custom_call_target="tpu_custom_call" | custom-call | flops 60000000 | bytes 559108 | tf_op jit(solution)/shard_map/pallas_call | solution.py:39
  3.0 18.4 %all-to-all-start = ((bf16[16,32,128]{2,1,0:T(8,128)(2,1)}), bf16[16,32,128]{2,1,0:T(8,128)(2,1)S(1)}, u32[]{:S(2)}, u32[]{:S(2)}) async-start(bf16[16,32,128]{2,1,0:T(8,128)(2,1)} %bitcast.34), calls=%async_computation | async-start | bytes 262144 | tf_op jit(solution)/shard_map/all_to_all | solution.py:20
  21.4 1.2 reshape.36
  22.6 1.2 reshape.37
  23.8 0.0 copy-done.4
  23.8 0.1 reshape_squeeze.3
  23.9 0.1 pad.5.clone
  24.0 0.9 maximum_maximum_fusion.w_ref
  24.9 11.8 %all-to-all-done = bf16[16,32,128]{2,1,0:T(8,128)(2,1)S(1)} async-done(((bf16[16,32,128]{2,1,0:T(8,128)(2,1)}), bf16[16,32,128]{2,1,0:T(8,128)(2,1)S(1)}, u32[]{:S(2)}, u32[]{:S(2)}) %all-to-all-start) | async-done | bytes 131104 | tf_op jit(solution)/shard_map/all_to_all | solution.py:20
  36.6 0.9 broadcast_in_dim.30
  37.5 4.3 %all-to-all-start.1 = ((bf16[4,512,128]{2,1,0:T(8,128)(2,1)}), bf16[4,512,128]{2,1,0:T(8,128)(2,1)S(1)}, u32[]{:S(2)}, u32[]{:S(2)}) async-start(bf16[4,512,128]{2,1,0:T(8,128)(2,1)} %broadcast_in_dim.30), calls=%async_computation.1 | async-start | bytes 1048576 | tf_op jit(solution)/shard_map/all_to_all | solution.py:20
  41.8 8.1 %all-to-all-done.1.pack_ref = bf16[4,512,128]{2,1,0:T(8,128)(2,1)S(1)} async-done(((bf16[4,512,128]{2,1,0:T(8,128)(2,1)}), bf16[4,512,128]{2,1,0:T(8,128)(2,1)S(1)}, u32[]{:S(2)}, u32[]{:S(2)}) %all-to-all-start.1) | async-done | bytes 524320 | tf_op jit(solution)/shard_map/all_to_all | solution.py:20
  49.9 1.6 %shard_map.111 = (bf16[8,336,128]{2,1,0:T(8,128)(2,1)S(1)}, bf16[336,768]{1,0:T(8,128)(2,1)S(1)}) custom-call(s32[1]{0:T(128)} %bitcast.4.half_ref, bf16[4,512,128]{2,1,0:T(8,128)(2,1)S(1)} %all-to-all-done.1.pack_ref, bf16[16,128,384]{2,1,0:T(8,128)(2,1)S(1)} %maximum_maximum_fusion.w_ref), custom_call_target="tpu_custom_call" | custom-call | flops 1056964608 | bytes 3301380 | tf_op jit(solution)/shard_map/pallas_call | solution.py:39
  51.4 1.9 %collective-permute-start = (bf16[8,336,128]{2,1,0:T(8,128)(2,1)S(1)}, bf16[8,336,128]{2,1,0:T(8,128)(2,1)S(1)}, u32[]{:S(2)}, u32[]{:S(2)}) collective-permute-start(bf16[8,336,128]{2,1,0:T(8,128)(2,1)S(1)} %get-tuple-element.34), channel_id=1, source_target_pairs={{0,1},{1,0},{2,3},{3,2},{4,5},{5,4},{6,7},{7,6},{8,9},{9,8},{10,11... | collective-permute-start | bytes 2064392 | tf_op jit(solution)/shard_map/ppermute | solution.py:334
  53.4 0.9 shard_map.112
  54.3 1.2 collective-permute-done
  55.5 0.2 add_convert_fusion
  55.7 26.7 %all_to_all.30.sum_ref = bf16[8,336,128]{2,1,0:T(8,128)(2,1)S(1)} all-to-all(bf16[8,336,128]{2,1,0:T(8,128)(2,1)S(1)} %add_convert_fusion), channel_id=1, replica_groups={{0,8,2,10,4,12,6,14},{1,9,3,11,5,13,7,15},{16,24,18,26,20,28,22,30},{17..., dimensions={0} | all-to-all | bytes 1376256 | tf_op jit(solution)/shard_map/all_to_all | solution.py:20
  82.4 1.1 shard_map.113
  83.4 3.6 %all-to-all-start.3 = ((bf16[16,96,128]{2,1,0:T(8,128)(2,1)}), bf16[16,96,128]{2,1,0:T(8,128)(2,1)S(1)}, u32[]{:S(2)}, u32[]{:S(2)}) async-start(bf16[16,96,128]{2,1,0:T(8,128)(2,1)} %get-tuple-element.36), calls=%async_computation.3 | async-start | bytes 786432 | tf_op jit(solution)/shard_map/all_to_all | solution.py:20
  87.0 26.2 %all-gather = bf16[3840,128]{1,0:T(8,128)(2,1)S(1)} all-gather(bf16[240,128]{1,0:T(8,128)(2,1)S(1)} %get-tuple-element.35), channel_id=2, replica_groups=mesh['expert'=16,'etp'=4,'dp'=16] {'dp'}, dimensions={0}, use_global_device_ids=true | all-gather | bytes 1044480 | tf_op jit(solution)/shard_map/all_gather | solution.py:346
  113.2 0.0 all-to-all-done.3.tail_ref
  113.2 2.2 %shard_map.114 = bf16[4,512,128]{2,1,0:T(8,128)(2,1)S(1)} custom-call(bf16[16,240,128]{2,1,0:T(8,128)(2,1)S(1)} %bitcast.26, bf16[16,96,128]{2,1,0:T(8,128)(2,1)S(1)} %all-to-all-done.3.tail_ref, bf16[16,128,384]{2,1,0:T(8,128)(2,1)S(1)} %maximum_maximum_fusion.w_ref), custom_call_target="tpu_custom_call" | custom-call | flops 2113929216 | bytes 3473408 | tf_op jit(solution)/shard_map/pallas_call | solution.py:39
  115.4 12.7 %all_to_all.31 = bf16[4,512,128]{2,1,0:T(8,128)(2,1)S(1)} all-to-all(bf16[4,512,128]{2,1,0:T(8,128)(2,1)S(1)} %shard_map.114), channel_id=1, replica_groups=mesh['expert'=16,'etp'=4,'dp'=16] {'etp'}, dimensions={0} | all-to-all | bytes 1048576 | tf_op jit(solution)/shard_map/all_to_all | solution.py:20
  128.1 0.7 reduce_sum.12
  128.9 4.3 %all-to-all-start.5 = ((bf16[16,32,128]{2,1,0:T(8,128)(2,1)}), bf16[16,32,128]{2,1,0:T(8,128)(2,1)S(1)}, u32[]{:S(2)}, u32[]{:S(2)}) async-start(bf16[16,32,128]{2,1,0:T(8,128)(2,1)} %bitcast.13), calls=%async_computation.5 | async-start | bytes 262144 | tf_op jit(solution)/shard_map/all_to_all | solution.py:20
  133.2 1.8 %convolution_convert_fusion = bf16[16,128,768]{2,1,0:T(8,128)(2,1)S(1)} fusion(bf16[16,96,128]{2,1,0:T(8,128)(2,1)S(1)} %all-to-all-done.3.tail_ref, bf16[16,240,128]{2,1,0:T(8,128)(2,1)S(1)} %bitcast.27, bf16[336,768]{1,0:T(8,128)(2,1)S(1)} %get-tuple-element.33.xg_ref), kind=kOutput, calls=%fused_computation | convolution fusion | flops 1061289984 | bytes 5038080 | tf_op jit(solution)/shard_map/dot_general | solution.py:16
  135.0 0.0 copy-start
  135.0 0.0 copy-start.1
  135.0 0.0 copy-start.2
  135.0 0.0 copy-start.3
  135.0 0.5 fusion.5
  135.5 0.9 broadcast_in_dim_reshape.3
  136.5 0.9 reshape.41
  137.4 0.9 reshape.40
  138.3 9.5 %all-to-all-done.5 = bf16[16,32,128]{2,1,0:T(8,128)(2,1)S(1)} async-done(((bf16[16,32,128]{2,1,0:T(8,128)(2,1)}), bf16[16,32,128]{2,1,0:T(8,128)(2,1)S(1)}, u32[]{:S(2)}, u32[]{:S(2)}) %all-to-all-start.5) | async-done | bytes 131104 | tf_op jit(solution)/shard_map/all_to_all | solution.py:20
  147.8 0.0 copy-done
  147.8 0.0 copy-done.1
  147.8 0.0 copy-done.2
  147.8 0.0 copy-done.3
  147.8 1.2 shard_map.115
  (1 shorter events, 0.0 us)
Async XLA Ops:
  0.6 23.1 %copy-start.4 = (bf16[1,672,384]{2,1,0:T(8,128)(2,1)S(1)}, bf16[1,672,384]{2,1,0:T(8,128)(2,1)}, u32[]{:S(2)}) copy-start(bf16[1,672,384]{2,1,0:T(8,128)(2,1)} %param.12) | copy-start | bytes 1548292
  3.0 33.7 %all-to-all-start = ((bf16[16,32,128]{2,1,0:T(8,128)(2,1)}), bf16[16,32,128]{2,1,0:T(8,128)(2,1)S(1)}, u32[]{:S(2)}, u32[]{:S(2)}) async-start(bf16[16,32,128]{2,1,0:T(8,128)(2,1)} %bitcast.34), calls=%async_computation | async-start | bytes 262144 | tf_op jit(solution)/shard_map/all_to_all | solution.py:20
  37.5 12.4 %all-to-all-start.1 = ((bf16[4,512,128]{2,1,0:T(8,128)(2,1)}), bf16[4,512,128]{2,1,0:T(8,128)(2,1)S(1)}, u32[]{:S(2)}, u32[]{:S(2)}) async-start(bf16[4,512,128]{2,1,0:T(8,128)(2,1)} %broadcast_in_dim.30), calls=%async_computation.1 | async-start | bytes 1048576 | tf_op jit(solution)/shard_map/all_to_all | solution.py:20
  51.4 4.0 %collective-permute-start = (bf16[8,336,128]{2,1,0:T(8,128)(2,1)S(1)}, bf16[8,336,128]{2,1,0:T(8,128)(2,1)S(1)}, u32[]{:S(2)}, u32[]{:S(2)}) collective-permute-start(bf16[8,336,128]{2,1,0:T(8,128)(2,1)S(1)} %get-tuple-element.34), channel_id=1, source_target_pairs={{0,1},{1,0},{2,3},{3,2},{4,5},{5,4},{6,7},{7,6},{8,9},{9,8},{10,11... | collective-permute-start | bytes 2064392 | tf_op jit(solution)/shard_map/ppermute | solution.py:334
  83.4 29.8 %all-to-all-start.3 = ((bf16[16,96,128]{2,1,0:T(8,128)(2,1)}), bf16[16,96,128]{2,1,0:T(8,128)(2,1)S(1)}, u32[]{:S(2)}, u32[]{:S(2)}) async-start(bf16[16,96,128]{2,1,0:T(8,128)(2,1)} %get-tuple-element.36), calls=%async_computation.3 | async-start | bytes 786432 | tf_op jit(solution)/shard_map/all_to_all | solution.py:20
  128.9 19.0 %all-to-all-start.5 = ((bf16[16,32,128]{2,1,0:T(8,128)(2,1)}), bf16[16,32,128]{2,1,0:T(8,128)(2,1)S(1)}, u32[]{:S(2)}, u32[]{:S(2)}) async-start(bf16[16,32,128]{2,1,0:T(8,128)(2,1)} %bitcast.13), calls=%async_computation.5 | async-start | bytes 262144 | tf_op jit(solution)/shard_map/all_to_all | solution.py:20
  135.0 12.8 %copy-start = (f32[512,64]{1,0:T(8,128)S(1)}, f32[512,64]{1,0:T(8,128)}, u32[]{:S(2)}) copy-start(f32[512,64]{1,0:T(8,128)} %get-tuple-element.22.weight_ref) | copy-start | bytes 393220
  135.0 12.8 %copy-start.1 = (bf16[512,64]{1,0:T(8,128)(2,1)S(1)}, bf16[512,64]{1,0:T(8,128)(2,1)}, u32[]{:S(2)}) copy-start(bf16[512,64]{1,0:T(8,128)(2,1)} %get-tuple-element.23.place_ref) | copy-start | bytes 196612
  135.0 12.8 %copy-start.2 = (bf16[512,64]{1,0:T(8,128)(2,1)S(1)}, bf16[512,64]{1,0:T(8,128)(2,1)}, u32[]{:S(2)}) copy-start(bf16[512,64]{1,0:T(8,128)(2,1)} %get-tuple-element.24.place_b_ref) | copy-start | bytes 196612
  135.0 12.8 %copy-start.3 = (bf16[512,64]{1,0:T(8,128)(2,1)S(1)}, bf16[512,64]{1,0:T(8,128)(2,1)}, u32[]{:S(2)}) copy-start(bf16[512,64]{1,0:T(8,128)(2,1)} %get-tuple-element.25.place_c_ref) | copy-start | bytes 196612

commit v9 on v8

--- a/solution.py
+++ b/solution.py
@@ -208,13 +208,14 @@
     width = w_ref.shape[2]
     w = w_ref[...].reshape(chunks * LANES, width)
     first = iota((1, LANES), 1) < split
+    arrival = far_order(chunks)
 
     def product(keep):
         keep = jnp.where(keep, 1.0, 0.0).astype(bf16)
         act = jnp.concatenate(
             [
-                jnp.concatenate([ref[j] * keep for j in range(chunks)], axis=1)
-                for ref in (head_ref, tail_ref)
+                jnp.concatenate([ref[at(j)] * keep for j in range(chunks)], axis=1)
+                for ref, at in ((head_ref, int), (tail_ref, arrival.index))
             ],
             axis=0,
         )
@@ -342,7 +343,7 @@
         0,
         swap(chip, "dp", same_core),
     )
-    tail = swap(tail, "dp")
+    tail = swap(tail, "dp", [far_order(n_dp)])
     head = lax.all_gather(head, "dp", axis=0)
     (out,) = call(
         functools.partial(back_kernel, piece, 2 * unit),
@@ -356,7 +357,8 @@
     out = jnp.sum(swap(out, "etp").astype(f32), axis=0).astype(bf16)
     back = swap(out.reshape(n_exp, PACK, LANES), "expert", experts).reshape(rows, LANES)
 
-    full = jnp.concatenate([head, tail], axis=1)
+    in_place = jnp.stack([tail[far_order(n_dp).index(j)] for j in range(n_dp)])
+    full = jnp.concatenate([head, in_place], axis=1)
     grads = mm(full, xg, ((1,), (0,))).astype(bf16)
 
     def take(start, at):

time: 150 us -> 152 us (1.013)
  blocking collectives: 65.6 us -> 52.8 us
  waiting for transfers between devices: 30.5 us -> 38.9 us
  starting transfers between devices: 32.5 us -> 36 us
  local copies, waits for them, and re-layouts: 6.74 us -> 8.51 us
    all_to_all x2 -> x1, blocking collectives: 39.4 us -> 26.7 us  [swap(): lax.all_to_all(x, axis, split_axis=0, concat_axis=0, tiled=True, axis_ind...]
    all_to_all x4 -> x5, waiting for transfers between devices: 29.3 us -> 37.7 us  [swap(): lax.all_to_all(x, axis, split_axis=0, concat_axis=0, tiled=True, axis_ind...]
    all_to_all x4 -> x5, starting transfers between devices: 30.6 us -> 34.1 us  [swap(): lax.all_to_all(x, axis, split_axis=0, concat_axis=0, tiled=True, axis_ind...]
  transfers between devices with their start and end apart: 5 -> 6, of which waited for: 4 -> 5; matrix products, arithmetic and copies ran while one was open for 6% -> 7% of each run, Pallas kernels for 1% -> 1%
where the time goes in v9:
time: 152 us; the launch traced here: 151 us
  blocking collectives  52.8 us (35%)
  waiting for transfers between devices  38.9 us (26%)
  starting transfers between devices  36 us (24%)
  Pallas kernels  9.26 us (6%)
  local copies, waits for them, and re-layouts  8.51 us (6%)
  other arithmetic  2.85 us (2%)
  matrix products  1.84 us (1%)
    all_to_all x5, waiting for transfers between devices, swap(): lax.all_to_all(x, axis, split_axis=0, concat_axis=0, tiled=True, axis_ind...  37.7 us
    all_to_all x5, starting transfers between devices, swap(): lax.all_to_all(x, axis, split_axis=0, concat_axis=0, tiled=True, axis_ind...  34.1 us
    all_to_all x1, blocking collectives, swap(): lax.all_to_all(x, axis, split_axis=0, concat_axis=0, tiled=True, axis_ind...  26.7 us
    all_gather x1, blocking collectives, local(): head = lax.all_gather(head, 'dp', axis=0)  26.1 us
    pallas_call x6, Pallas kernels, call(): pl.pallas_call(kernel, out_shape=outs, in_specs=[smem] * n_scalar + [held...  9.26 us
  transfers between devices with their start and end apart: 6, of which 5 were waited for; matrix products, arithmetic and copies ran while one was open for 7% of the time, Pallas kernels for 1%

profile of v9, /device:TPU:64, one launch (start us, length us, event | category | flops | bytes accessed | tf_op | source)
XLA Modules:
  0.0 151.0 jit_solution(12761366580164010972)
XLA Ops:
  0.6 0.0 copy-start.5
  0.6 2.3 %shard_map.110 = (bf16[512,128]{1,0:T(8,128)(2,1)}, bf16[512,64]{1,0:T(8,128)(2,1)}, bf16[512,64]{1,0:T(8,128)(2,1)}, bf16[512,64]{1,0:T(8,128)(2,1)}, f32[512,64]{1,0:T(8,128)}) custom-call(s32[1]{0:T(128)} %bitcast.col_ref, bf16[64,384]{1,0:T(8,128)(2,1)} %tok_hbm.1, bf16[64,384]{1,0:T(8,128)(2,1)} %cot_hbm.1, s32[4,64]{1,0:T(4,128)} %bitcast.35, ...), custom_call_target="tpu_custom_call" | custom-call | flops 60000000 | bytes 559108 | tf_op jit(solution)/shard_map/pallas_call | solution.py:39
  3.0 18.4 %all-to-all-start = ((bf16[16,32,128]{2,1,0:T(8,128)(2,1)}), bf16[16,32,128]{2,1,0:T(8,128)(2,1)S(1)}, u32[]{:S(2)}, u32[]{:S(2)}) async-start(bf16[16,32,128]{2,1,0:T(8,128)(2,1)} %bitcast.34), calls=%async_computation | async-start | bytes 262144 | tf_op jit(solution)/shard_map/all_to_all | solution.py:20
  21.4 1.2 reshape.36
  22.6 1.2 reshape.37
  23.8 0.0 copy-done.5
  23.8 1.0 reshape_squeeze.3
  24.8 0.1 pad.5.clone
  24.8 1.9 %maximum_maximum_fusion.w_ref = bf16[16,128,384]{2,1,0:T(8,128)(2,1)S(1)} fusion(bf16[16,42,384]{2,1,0:T(8,128)(2,1)} %reshape_squeeze.3, bf16[16,42,384]{2,1,0:T(8,128)(2,1)S(1)} %reshape.37, bf16[16,42,384]{2,1,0:T(8,128)(2,1)S(1)} %reshape.36, bf16[128]{0:T(256)(128)(2,1)S(1)} %pad.5.clone), kind=kLoop, calls=%fused_computation.1 | loop fusion | flops 6291456 | bytes 3121408 | tf_op jit(solution)/shard_map/concatenate | solution.py:316
  26.8 9.9 %all-to-all-done = bf16[16,32,128]{2,1,0:T(8,128)(2,1)S(1)} async-done(((bf16[16,32,128]{2,1,0:T(8,128)(2,1)}), bf16[16,32,128]{2,1,0:T(8,128)(2,1)S(1)}, u32[]{:S(2)}, u32[]{:S(2)}) %all-to-all-start) | async-done | bytes 131104 | tf_op jit(solution)/shard_map/all_to_all | solution.py:20
  36.6 0.9 broadcast_in_dim.30
  37.5 4.3 %all-to-all-start.1 = ((bf16[4,512,128]{2,1,0:T(8,128)(2,1)}), bf16[4,512,128]{2,1,0:T(8,128)(2,1)S(1)}, u32[]{:S(2)}, u32[]{:S(2)}) async-start(bf16[4,512,128]{2,1,0:T(8,128)(2,1)} %broadcast_in_dim.30), calls=%async_computation.1 | async-start | bytes 1048576 | tf_op jit(solution)/shard_map/all_to_all | solution.py:20
  41.8 8.1 %all-to-all-done.1.pack_ref = bf16[4,512,128]{2,1,0:T(8,128)(2,1)S(1)} async-done(((bf16[4,512,128]{2,1,0:T(8,128)(2,1)}), bf16[4,512,128]{2,1,0:T(8,128)(2,1)S(1)}, u32[]{:S(2)}, u32[]{:S(2)}) %all-to-all-start.1) | async-done | bytes 524320 | tf_op jit(solution)/shard_map/all_to_all | solution.py:20
  49.9 1.6 %shard_map.111 = (bf16[8,336,128]{2,1,0:T(8,128)(2,1)S(1)}, bf16[336,768]{1,0:T(8,128)(2,1)S(1)}) custom-call(s32[1]{0:T(128)} %bitcast.4.half_ref, bf16[4,512,128]{2,1,0:T(8,128)(2,1)S(1)} %all-to-all-done.1.pack_ref, bf16[16,128,384]{2,1,0:T(8,128)(2,1)S(1)} %maximum_maximum_fusion.w_ref), custom_call_target="tpu_custom_call" | custom-call | flops 1056964608 | bytes 3301380 | tf_op jit(solution)/shard_map/pallas_call | solution.py:39
  51.5 1.9 %collective-permute-start = (bf16[8,336,128]{2,1,0:T(8,128)(2,1)S(1)}, bf16[8,336,128]{2,1,0:T(8,128)(2,1)S(1)}, u32[]{:S(2)}, u32[]{:S(2)}) collective-permute-start(bf16[8,336,128]{2,1,0:T(8,128)(2,1)S(1)} %get-tuple-element.34), channel_id=1, source_target_pairs={{0,1},{1,0},{2,3},{3,2},{4,5},{5,4},{6,7},{7,6},{8,9},{9,8},{10,11... | collective-permute-start | bytes 2064392 | tf_op jit(solution)/shard_map/ppermute | solution.py:335
  53.4 0.9 shard_map.112
  54.3 1.2 collective-permute-done
  55.5 0.2 add_convert_fusion
  55.7 26.7 %all_to_all.30.sum_ref = bf16[8,336,128]{2,1,0:T(8,128)(2,1)S(1)} all-to-all(bf16[8,336,128]{2,1,0:T(8,128)(2,1)S(1)} %add_convert_fusion), channel_id=1, replica_groups={{0,8,2,10,4,12,6,14},{1,9,3,11,5,13,7,15},{16,24,18,26,20,28,22,30},{17..., dimensions={0} | all-to-all | bytes 1376256 | tf_op jit(solution)/shard_map/all_to_all | solution.py:20
  82.4 1.1 shard_map.113
  83.4 3.6 %all-to-all-start.3 = ((bf16[16,96,128]{2,1,0:T(8,128)(2,1)}), bf16[16,96,128]{2,1,0:T(8,128)(2,1)S(1)}, u32[]{:S(2)}, u32[]{:S(2)}) async-start(bf16[16,96,128]{2,1,0:T(8,128)(2,1)} %get-tuple-element.36), calls=%async_computation.3 | async-start | bytes 786432 | tf_op jit(solution)/shard_map/all_to_all | solution.py:20
  87.0 26.1 %all-gather = bf16[3840,128]{1,0:T(8,128)(2,1)S(1)} all-gather(bf16[240,128]{1,0:T(8,128)(2,1)S(1)} %get-tuple-element.35), channel_id=2, replica_groups=mesh['expert'=16,'etp'=4,'dp'=16] {'dp'}, dimensions={0}, use_global_device_ids=true | all-gather | bytes 1044480 | tf_op jit(solution)/shard_map/all_gather | solution.py:347
  113.1 0.0 all-to-all-done.3.tail_ref
  113.1 2.2 %shard_map.114 = bf16[4,512,128]{2,1,0:T(8,128)(2,1)S(1)} custom-call(bf16[16,240,128]{2,1,0:T(8,128)(2,1)S(1)} %bitcast.26, bf16[16,96,128]{2,1,0:T(8,128)(2,1)S(1)} %all-to-all-done.3.tail_ref, bf16[16,128,384]{2,1,0:T(8,128)(2,1)S(1)} %maximum_maximum_fusion.w_ref), custom_call_target="tpu_custom_call" | custom-call | flops 2113929216 | bytes 3473408 | tf_op jit(solution)/shard_map/pallas_call | solution.py:39
  115.3 0.0 copy-start
  115.3 0.8 copy-done
  116.1 3.5 %all-to-all-start.4 = ((bf16[4,512,128]{2,1,0:T(8,128)(2,1)}), bf16[4,512,128]{2,1,0:T(8,128)(2,1)S(1)}, u32[]{:S(2)}, u32[]{:S(2)}) async-start(bf16[4,512,128]{2,1,0:T(8,128)(2,1)} %copy-done), calls=%async_computation.4 | async-start | bytes 1048576 | tf_op jit(solution)/shard_map/all_to_all | solution.py:20
  119.8 10.0 %all-to-all-done.4 = bf16[4,512,128]{2,1,0:T(8,128)(2,1)S(1)} async-done(((bf16[4,512,128]{2,1,0:T(8,128)(2,1)}), bf16[4,512,128]{2,1,0:T(8,128)(2,1)S(1)}, u32[]{:S(2)}, u32[]{:S(2)}) %all-to-all-start.4) | async-done | bytes 524320 | tf_op jit(solution)/shard_map/all_to_all | solution.py:20
  129.8 0.7 reduce_sum.12
  130.6 4.3 %all-to-all-start.5 = ((bf16[16,32,128]{2,1,0:T(8,128)(2,1)}), bf16[16,32,128]{2,1,0:T(8,128)(2,1)S(1)}, u32[]{:S(2)}, u32[]{:S(2)}) async-start(bf16[16,32,128]{2,1,0:T(8,128)(2,1)} %bitcast.13), calls=%async_computation.5 | async-start | bytes 262144 | tf_op jit(solution)/shard_map/all_to_all | solution.py:20
  134.9 1.8 %convolution_convert_fusion = bf16[16,128,768]{2,1,0:T(8,128)(2,1)S(1)} fusion(bf16[16,96,128]{2,1,0:T(8,128)(2,1)S(1)} %constant_dynamic-update-slice_fusion, bf16[16,240,128]{2,1,0:T(8,128)(2,1)S(1)} %bitcast.27, bf16[336,768]{1,0:T(8,128)(2,1)S(1)} %get-tuple-element.33.xg_ref), kind=kOutput, calls=%fused_computation | convolution fusion | flops 1061289984 | bytes 5038080 | tf_op jit(solution)/shard_map/dot_general | solution.py:16
  136.7 0.0 copy-start.1
  136.7 0.0 copy-start.2
  136.8 0.0 copy-start.3
  136.8 0.0 copy-start.4
  136.8 0.5 fusion.5
  137.3 0.9 broadcast_in_dim_reshape.3
  138.2 0.9 reshape.41
  139.1 0.9 reshape.40
  140.1 9.8 %all-to-all-done.5 = bf16[16,32,128]{2,1,0:T(8,128)(2,1)S(1)} async-done(((bf16[16,32,128]{2,1,0:T(8,128)(2,1)}), bf16[16,32,128]{2,1,0:T(8,128)(2,1)S(1)}, u32[]{:S(2)}, u32[]{:S(2)}) %all-to-all-start.5) | async-done | bytes 131104 | tf_op jit(solution)/shard_map/all_to_all | solution.py:20
  149.8 0.0 copy-done.1
  149.8 0.0 copy-done.2
  149.8 0.0 copy-done.3
  149.8 0.0 copy-done.4
  149.9 1.2 shard_map.115
  (17 shorter events, 0.2 us)
Async XLA Ops:
  0.6 23.1 %copy-start.5 = (bf16[1,672,384]{2,1,0:T(8,128)(2,1)S(1)}, bf16[1,672,384]{2,1,0:T(8,128)(2,1)}, u32[]{:S(2)}) copy-start(bf16[1,672,384]{2,1,0:T(8,128)(2,1)} %param.12) | copy-start | bytes 1548292
  3.0 33.7 %all-to-all-start = ((bf16[16,32,128]{2,1,0:T(8,128)(2,1)}), bf16[16,32,128]{2,1,0:T(8,128)(2,1)S(1)}, u32[]{:S(2)}, u32[]{:S(2)}) async-start(bf16[16,32,128]{2,1,0:T(8,128)(2,1)} %bitcast.34), calls=%async_computation | async-start | bytes 262144 | tf_op jit(solution)/shard_map/all_to_all | solution.py:20
  37.5 12.4 %all-to-all-start.1 = ((bf16[4,512,128]{2,1,0:T(8,128)(2,1)}), bf16[4,512,128]{2,1,0:T(8,128)(2,1)S(1)}, u32[]{:S(2)}, u32[]{:S(2)}) async-start(bf16[4,512,128]{2,1,0:T(8,128)(2,1)} %broadcast_in_dim.30), calls=%async_computation.1 | async-start | bytes 1048576 | tf_op jit(solution)/shard_map/all_to_all | solution.py:20
  51.5 4.0 %collective-permute-start = (bf16[8,336,128]{2,1,0:T(8,128)(2,1)S(1)}, bf16[8,336,128]{2,1,0:T(8,128)(2,1)S(1)}, u32[]{:S(2)}, u32[]{:S(2)}) collective-permute-start(bf16[8,336,128]{2,1,0:T(8,128)(2,1)S(1)} %get-tuple-element.34), channel_id=1, source_target_pairs={{0,1},{1,0},{2,3},{3,2},{4,5},{5,4},{6,7},{7,6},{8,9},{9,8},{10,11... | collective-permute-start | bytes 2064392 | tf_op jit(solution)/shard_map/ppermute | solution.py:335
  83.4 29.7 %all-to-all-start.3 = ((bf16[16,96,128]{2,1,0:T(8,128)(2,1)}), bf16[16,96,128]{2,1,0:T(8,128)(2,1)S(1)}, u32[]{:S(2)}, u32[]{:S(2)}) async-start(bf16[16,96,128]{2,1,0:T(8,128)(2,1)} %get-tuple-element.36), calls=%async_computation.3 | async-start | bytes 786432 | tf_op jit(solution)/shard_map/all_to_all | solution.py:20
  115.3 0.8 copy-start
  116.1 13.7 %all-to-all-start.4 = ((bf16[4,512,128]{2,1,0:T(8,128)(2,1)}), bf16[4,512,128]{2,1,0:T(8,128)(2,1)S(1)}, u32[]{:S(2)}, u32[]{:S(2)}) async-start(bf16[4,512,128]{2,1,0:T(8,128)(2,1)} %copy-done), calls=%async_computation.4 | async-start | bytes 1048576 | tf_op jit(solution)/shard_map/all_to_all | solution.py:20
  130.6 19.2 %all-to-all-start.5 = ((bf16[16,32,128]{2,1,0:T(8,128)(2,1)}), bf16[16,32,128]{2,1,0:T(8,128)(2,1)S(1)}, u32[]{:S(2)}, u32[]{:S(2)}) async-start(bf16[16,32,128]{2,1,0:T(8,128)(2,1)} %bitcast.13), calls=%async_computation.5 | async-start | bytes 262144 | tf_op jit(solution)/shard_map/all_to_all | solution.py:20
  136.7 13.1 %copy-start.1 = (f32[512,64]{1,0:T(8,128)S(1)}, f32[512,64]{1,0:T(8,128)}, u32[]{:S(2)}) copy-start(f32[512,64]{1,0:T(8,128)} %get-tuple-element.22.weight_ref) | copy-start | bytes 393220
  136.7 13.1 %copy-start.2 = (bf16[512,64]{1,0:T(8,128)(2,1)S(1)}, bf16[512,64]{1,0:T(8,128)(2,1)}, u32[]{:S(2)}) copy-start(bf16[512,64]{1,0:T(8,128)(2,1)} %get-tuple-element.23.place_ref) | copy-start | bytes 196612
  136.8 13.1 %copy-start.3 = (bf16[512,64]{1,0:T(8,128)(2,1)S(1)}, bf16[512,64]{1,0:T(8,128)(2,1)}, u32[]{:S(2)}) copy-start(bf16[512,64]{1,0:T(8,128)(2,1)} %get-tuple-element.24.place_b_ref) | copy-start | bytes 196612
  136.8 13.1 %copy-start.4 = (bf16[512,64]{1,0:T(8,128)(2,1)S(1)}, bf16[512,64]{1,0:T(8,128)(2,1)}, u32[]{:S(2)}) copy-start(bf16[512,64]{1,0:T(8,128)(2,1)} %get-tuple-element.25.place_c_ref) | copy-start | bytes 196612
